TPU v7x, 32 devices: a whole 2x2x4 slice. The times are simulated.
32 devices in a mesh: dp: 8 (over z, x), mp: 4 (over y, core).
Axes of the slice: x: 2, y: 2, z: 4, core: 2. Of those that a mesh axis runs over, the one named last changes fastest.
Arguments:
- tokens: bfloat16 [16384, 768], P('dp'), may hold values from -6 to 6
- cotangent: bfloat16 [16384, 768], P('dp'), may hold values from -6 to 6
- lengths: int32 [16], P('dp'), may hold values from 128 to 1024, as said below
- tile_order: int32 [192], replicated, may hold values from 0 to 191, as said below
- master: float32 [4, 192, 96, 96], P('mp', 'dp')
- first_moment: float32 [4, 192, 96, 96], P('mp', 'dp')
- second_moment: float32 [4, 192, 96, 96], P('mp', 'dp')
- basis_left: float32 [4, 192, 96, 96], P('mp', 'dp'), may hold values from -0.625 to 0.625
- basis_right: float32 [4, 192, 96, 96], P('mp', 'dp'), may hold values from -0.625 to 0.625
- local_vec: float32 [4, 1152], P('mp'), may hold values from -1.2 to 1.2
- local_first: float32 [4, 1152], P('mp')
- local_second: float32 [4, 1152], P('mp')
- shared_vec: float32 [6, 768], replicated
- shared_first: float32 [6, 768], replicated
- shared_second: float32 [6, 768], replicated
Outputs:
- output: bfloat16 [16384, 768], P(('dp', 'mp'))
- input_grad: float32 [16384, 768], P(('dp', 'mp'))
- tile_grad: float32 [4, 192, 96, 96], P('mp', 'dp')
- tile_first: float32 [4, 192, 96, 96], P('mp', 'dp')
- tile_second: float32 [4, 192, 96, 96], P('mp', 'dp')
- tile_weight: float32 [4, 192, 96, 96], P('mp', 'dp')
- local_grad: float32 [4, 1152], P('mp')
- local_first_new: float32 [4, 1152], P('mp')
- local_second_new: float32 [4, 1152], P('mp')
- local_new: float32 [4, 1152], P('mp')
- shared_grad: float32 [6, 768], replicated
- shared_first_new: float32 [6, 768], replicated
- shared_second_new: float32 [6, 768], replicated
- shared_new: float32 [6, 768], replicated
Inputs may be any that keep to these rules, and one draw needn't show every extreme that they name: `lengths`: the first len slots of each sequence hold its tokens, the rest padding; some sequence has 1024 tokens and some has 128. `tile_order`: a permutation of the 192 tiles; owner i along dp holds slots i * 24 to (i + 1) * 24 - 1.
All inputs are finite; a program needn't handle non-finite values.
Results may differ from a plain program's by a relative error of at most 0.019.
Values may be sent and summed in bfloat16 or wider, within the bound.
A program may use at most 192 MiB of HBM per device.

v0:
```python
import jax
import jax.numpy as jnp
from jax import lax
from jax.sharding import PartitionSpec as P

HD = 64
GRAIN = 64
STEP = 5


NORM_EPS = 1e-05
BETA_ONE = 0.5
BETA_TWO = 0.5
ADAM_EPS = 1e-08
RATE_TILES = 0.04
RATE_VECTORS = 0.2
DECAY = 0.01
NEG_BIG = -1e30
HIGH = lax.Precision.HIGHEST
ROOT_HALF = 0.7071067811865476


def gelu(values):
    return 0.5 * values * (1.0 + lax.erf(values * ROOT_HALF))


def normalize(values, gain, shift):
    centre = values - jnp.mean(values, -1, keepdims=True)
    inv_scale = lax.rsqrt(jnp.mean(centre * centre, -1, keepdims=True) + NORM_EPS)
    normed = centre * inv_scale
    return (normed * gain + shift, normed, inv_scale)


def normalize_back(grad_in, normed, inv_scale, gain):
    grad_normed = grad_in * gain
    return inv_scale * (
        grad_normed
        - jnp.mean(grad_normed, -1, keepdims=True)
        - normed * jnp.mean(grad_normed * normed, -1, keepdims=True)
    )


def permitted(length, head_kind, seq_len):
    positions = jnp.arange(seq_len, dtype=jnp.int32)
    boundary = GRAIN * ((length + 2 * GRAIN - 1) // (2 * GRAIN))
    upper_half = positions >= boundary
    same_block = upper_half[:, None] == upper_half[None, :]
    within = (head_kind == 0)[:, None, None]
    return (positions < length)[None, None, :] & (same_block[None] == within)


def to_tiles(matrix, tile_edge):
    row_count, col_count = matrix.shape
    return (
        matrix.reshape(row_count // tile_edge, tile_edge, col_count // tile_edge, tile_edge)
        .transpose(0, 2, 1, 3)
        .reshape(-1, tile_edge, tile_edge)
    )


def from_tiles(tile_set, row_count, col_count):
    tile_edge = tile_set.shape[-1]
    return (
        tile_set.reshape(row_count // tile_edge, col_count // tile_edge, tile_edge, tile_edge)
        .transpose(0, 2, 1, 3)
        .reshape(row_count, col_count)
    )


def adam(grad, first, second):
    first_new = BETA_ONE * first + (1.0 - BETA_ONE) * grad
    second_new = BETA_TWO * second + (1.0 - BETA_TWO) * grad * grad
    step_dir = (
        first_new
        / (1.0 - BETA_ONE**STEP)
        / (jnp.sqrt(second_new / (1.0 - BETA_TWO**STEP)) + ADAM_EPS)
    )
    return (first_new, second_new, step_dir)


def shards(
    tokens,
    cotangent,
    lengths,
    tile_order,
    master,
    first_moment,
    second_moment,
    basis_left,
    basis_right,
    local_vec,
    local_first,
    local_second,
    shared_vec,
    shared_first,
    shared_second,
):
    f32 = jnp.float32
    bf16 = jnp.bfloat16
    group_count = lax.axis_size("mp")
    group_index = lax.axis_index("mp")
    row_total, model_width = tokens.shape
    seq_count = lengths.shape[0]
    seq_len = row_total // seq_count
    share_rows = row_total // group_count
    row_start = group_index * share_rows
    attn_width = model_width // group_count
    heads_here = attn_width // HD
    hidden_width = local_vec.shape[1] - 2 * attn_width
    tile_edge = master.shape[-1]
    scale_qk = HD ** (-0.5)

    def own_rows(values):
        return lax.dynamic_slice_in_dim(values, row_start, share_rows, 0)

    def tally(values):
        return jnp.sum(own_rows(values), 0)

    gathered = lax.all_gather(master[0].astype(bf16), "dp", axis=0, tiled=True)
    tile_count = gathered.shape[0]
    inverse = (
        jnp.zeros((tile_count,), jnp.int32)
        .at[tile_order]
        .set(jnp.arange(tile_count, dtype=jnp.int32))
    )
    natural = gathered[inverse]
    cut_one = model_width // tile_edge * (3 * attn_width // tile_edge)
    cut_two = cut_one + attn_width // tile_edge * (model_width // tile_edge)
    cut_three = cut_two + model_width // tile_edge * (hidden_width // tile_edge)
    w_qkv = from_tiles(natural[:cut_one], model_width, 3 * attn_width)
    w_out = from_tiles(natural[cut_one:cut_two], attn_width, model_width)
    w_up = from_tiles(natural[cut_two:cut_three], model_width, hidden_width)
    w_down = from_tiles(natural[cut_three:], hidden_width, model_width)
    vector = local_vec[0]
    bias_qkv = jnp.concatenate(
        [vector[:attn_width], jnp.zeros((attn_width,), f32), vector[attn_width : 2 * attn_width]]
    )
    bias_up = vector[2 * attn_width :]
    positions = jnp.arange(seq_len, dtype=jnp.int32)
    valid = (positions[None, :] < lengths[:, None]).astype(f32).reshape(row_total)
    head_kind = (group_index * heads_here + jnp.arange(heads_here, dtype=jnp.int32)) % 2
    inputs = tokens.astype(f32)
    qkv_all = (jnp.dot(tokens, w_qkv, preferred_element_type=f32) + bias_qkv).astype(bf16)
    qkv_seq = qkv_all.reshape(seq_count, seq_len, 3, heads_here, HD)

    def attend(seq_item):
        block, length = seq_item
        allowed = permitted(length, head_kind, seq_len)
        scores = (
            jnp.einsum("qhd,khd->hqk", block[:, 0], block[:, 1], preferred_element_type=f32)
            * scale_qk
        )
        scores = jnp.where(allowed, scores, NEG_BIG)
        row_top = jnp.max(scores, -1, keepdims=True)
        exponent = jnp.exp(scores - row_top)
        row_total_exp = jnp.sum(exponent, -1, keepdims=True)
        attn_probs = (exponent / row_total_exp).astype(bf16)
        mixed_heads = jnp.einsum(
            "hqk,khd->qhd", attn_probs, block[:, 2], preferred_element_type=f32
        )
        return (
            mixed_heads.astype(bf16).reshape(seq_len, heads_here * HD),
            (row_top + jnp.log(row_total_exp))[..., 0],
        )

    attended, log_sums = lax.map(attend, (qkv_seq, lengths))
    attended = attended.reshape(row_total, attn_width)
    part_attn = jnp.dot(attended, w_out, preferred_element_type=f32)
    z_one = (
        inputs + lax.psum(part_attn.astype(jnp.bfloat16), "mp").astype(jnp.float32) + shared_vec[0]
    )
    hidden, normed_one, scale_one = normalize(z_one, shared_vec[2], shared_vec[3])
    hidden_low = hidden.astype(bf16)
    pre_act = jnp.dot(hidden_low, w_up, preferred_element_type=f32) + bias_up
    activation = gelu(pre_act).astype(bf16)
    part_ffn = jnp.dot(activation, w_down, preferred_element_type=f32)
    ffn_out = lax.psum(part_ffn.astype(jnp.bfloat16), "mp").astype(jnp.float32)
    z_two = hidden + ffn_out + shared_vec[1]
    normal_two, normed_two, scale_two = normalize(z_two, shared_vec[4], shared_vec[5])
    result = normal_two * valid[:, None]
    output = own_rows(result).astype(bf16)
    grad_out = cotangent.astype(f32) * valid[:, None]
    grad_two = normalize_back(grad_out, normed_two, scale_two, shared_vec[4])
    d_gain_two = tally(grad_out * normed_two)
    d_shift_two = tally(grad_out)
    d_bias_down = tally(grad_two)
    grad_two_low = grad_two.astype(bf16)
    d_down = jnp.einsum("tf,td->fd", activation, grad_two_low, preferred_element_type=f32)
    grad_act = jnp.einsum("td,fd->tf", grad_two_low, w_down, preferred_element_type=f32)
    gelu_value, gelu_pull = jax.vjp(gelu, pre_act)
    grad_pre = gelu_pull(grad_act)[0].astype(bf16)
    d_bias_up = jnp.sum(grad_pre, 0, dtype=f32)
    d_up = jnp.einsum("td,tf->df", hidden_low, grad_pre, preferred_element_type=f32)
    part_hidden = jnp.einsum("tf,df->td", grad_pre, w_up, preferred_element_type=f32)
    grad_hidden = grad_two + lax.psum(part_hidden.astype(jnp.bfloat16), "mp").astype(jnp.float32)
    grad_one = normalize_back(grad_hidden, normed_one, scale_one, shared_vec[2])
    d_gain_one = tally(grad_hidden * normed_one)
    d_shift_one = tally(grad_hidden)
    d_bias_out = tally(grad_one)
    grad_one_low = grad_one.astype(bf16)
    d_out = jnp.einsum("tm,td->md", attended, grad_one_low, preferred_element_type=f32)
    grad_mixed = jnp.einsum("td,md->tm", grad_one_low, w_out, preferred_element_type=f32).astype(
        bf16
    )
    grad_mixed = grad_mixed.reshape(seq_count, seq_len, heads_here, HD)

    def attend_back(seq_item):
        block, length, top_sums, grad_block = seq_item
        allowed = permitted(length, head_kind, seq_len)
        scores = (
            jnp.einsum("qhd,khd->hqk", block[:, 0], block[:, 1], preferred_element_type=f32)
            * scale_qk
        )
        scores = jnp.where(allowed, scores, NEG_BIG)
        attn_probs = jnp.exp(scores - top_sums[..., None])
        grad_probs = jnp.einsum("qhd,khd->hqk", grad_block, block[:, 2], preferred_element_type=f32)
        inner = jnp.sum(attn_probs * grad_probs, -1, keepdims=True)
        grad_scores = (attn_probs * (grad_probs - inner)).astype(bf16)
        grad_query = (
            jnp.einsum("hqk,khd->qhd", grad_scores, block[:, 1], preferred_element_type=f32)
            * scale_qk
        )
        grad_key = (
            jnp.einsum("hqk,qhd->khd", grad_scores, block[:, 0], preferred_element_type=f32)
            * scale_qk
        )
        grad_value = jnp.einsum(
            "hqk,qhd->khd", attn_probs.astype(bf16), grad_block, preferred_element_type=f32
        )
        return jnp.stack([grad_query, grad_key, grad_value], 1).astype(bf16)

    grad_qkv = lax.map(attend_back, (qkv_seq, lengths, log_sums, grad_mixed)).reshape(
        row_total, 3 * attn_width
    )
    d_qkv = jnp.einsum("td,tc->dc", tokens, grad_qkv, preferred_element_type=f32)
    bias_sums = jnp.sum(grad_qkv, 0, dtype=f32)
    part_input = jnp.einsum("tc,dc->td", grad_qkv, w_qkv, preferred_element_type=f32)
    input_grad = own_rows(
        grad_one + lax.psum(part_input.astype(jnp.bfloat16), "mp").astype(jnp.float32)
    )
    natural_grads = jnp.concatenate(
        [
            to_tiles(d_qkv, tile_edge),
            to_tiles(d_out, tile_edge),
            to_tiles(d_up, tile_edge),
            to_tiles(d_down, tile_edge),
        ],
        0,
    )
    owned = lax.psum_scatter(natural_grads[tile_order], "dp", scatter_dimension=0, tiled=True)
    local_terms = jnp.concatenate([bias_sums[:attn_width], bias_sums[2 * attn_width :], d_bias_up])
    spread = jnp.where(jnp.arange(group_count)[:, None] == group_index, local_terms[None, :], 0.0)
    shared_terms = jnp.stack(
        [d_bias_out, d_bias_down, d_gain_one, d_shift_one, d_gain_two, d_shift_two]
    )
    spread_sum, shared_grad = lax.psum((spread, shared_terms), ("dp", "mp"))
    local_grad = lax.dynamic_slice_in_dim(spread_sum, group_index, 1, 0)
    left_basis = basis_left[0]
    right_basis = basis_right[0]
    rotated = jnp.einsum("ski,skl->sil", left_basis, owned, precision=HIGH)
    rotated = jnp.einsum("sil,slj->sij", rotated, right_basis, precision=HIGH)
    tile_first, tile_second, direction = adam(rotated, first_moment[0], second_moment[0])
    turned = jnp.einsum("sik,skl->sil", left_basis, direction, precision=HIGH)
    turned = jnp.einsum("sil,sjl->sij", turned, right_basis, precision=HIGH)
    tile_weight = master[0] - RATE_TILES * (turned + DECAY * master[0])
    local_first_new, local_second_new, local_dir = adam(local_grad, local_first, local_second)
    shared_first_new, shared_second_new, shared_dir = adam(shared_grad, shared_first, shared_second)
    return (
        output,
        input_grad,
        owned[None],
        tile_first[None],
        tile_second[None],
        tile_weight[None],
        local_grad,
        local_first_new,
        local_second_new,
        local_vec - RATE_VECTORS * local_dir,
        shared_grad,
        shared_first_new,
        shared_second_new,
        shared_vec - RATE_VECTORS * shared_dir,
    )


def solution(mesh):
    placed = (
        P("dp", None),
        P("dp", None),
        P("dp"),
        P(),
        P("mp", "dp", None, None),
        P("mp", "dp", None, None),
        P("mp", "dp", None, None),
        P("mp", "dp", None, None),
        P("mp", "dp", None, None),
        P("mp", None),
        P("mp", None),
        P("mp", None),
        P(),
        P(),
        P(),
    )
    return jax.shard_map(
        shards,
        mesh=mesh,
        in_specs=placed,
        out_specs=(
            P(("dp", "mp"), None),
            P(("dp", "mp"), None),
            P("mp", "dp", None, None),
            P("mp", "dp", None, None),
            P("mp", "dp", None, None),
            P("mp", "dp", None, None),
            P("mp", None),
            P("mp", None),
            P("mp", None),
            P("mp", None),
            P(),
            P(),
            P(),
            P(),
        ),
        check_vma=False,
    )
```

profile of v0, /device:TPU:16, one launch (start us, length us, event | category | flops | bytes accessed | tf_op | source)
XLA Modules:
  0.0 764.8 jit_solution(5379120619863724201)
XLA Ops:
  12.4 78.4 %all-gather.2.cloned.1.call-done = bf16[192,96,96]{2,1,0:T(8,128)(2,1)} async-done(((bf16[24,96,96]{2,1,0:T(8,128)(2,1)}), bf16[192,96,96]{2,1,0:T(8,128)(2,1)}) %all-gather.2.cloned.1.call-update) | async-done | bytes 3538960 | tf_op jit(solution)/shard_map/all_gather | solution.py:119
  90.8 5.8 gather_fusion
  112.8 36.7 %while.34 = (s32[]{:T(128)}, bf16[2,1024,192]{1,2,0:T(8,128)(2,1)}, f32[2,3,1024]{2,1,0:T(4,128)}, bf16[2,1024,3,3,64]{1,4,3,2,0:T(8,128)(2,1)S(1)}, s32[2]{0:T(...) while((s32[]{:T(128)}, bf16[2,1024,192]{1,2,0:T(8,128)(2,1)}, ...), condition=%wide.region_4.5_spmd.clone, body=%wide.region_1.4_spmd.clone.sunk | while | flops 863173696 | bytes 53276100 | solution.py:166
  169.7 53.9 %all-reduce.6.cloned.1.call-done = bf16[2048,768]{1,0:T(8,128)(2,1)} async-done(((bf16[2048,768]{1,0:T(8,128)(2,1)}), bf16[2048,768]{1,0:T(8,128)(2,1)}) %all-reduce.6.cloned.1.call-update) | async-done | bytes 3145744 | tf_op jit(solution)/shard_map/psum | solution.py:170
  242.2 68.5 %all-reduce.8.cloned.1.call-done = bf16[2048,768]{1,0:T(8,128)(2,1)} async-done(((bf16[2048,768]{1,0:T(8,128)(2,1)}), bf16[2048,768]{1,0:T(8,128)(2,1)}) %all-reduce.8.cloned.1.call-update) | async-done | bytes 3145744 | tf_op jit(solution)/shard_map/psum | solution.py:177
  318.9 5.3 multiply_reduce_fusion.6
  326.9 8.9 %convert_reduce_fusion = (f32[768]{0:T(1024)}, bf16[2048,768]{1,0:T(8,128)(2,1)S(1)}) fusion(bf16[768,768]{1,0:T(8,128)(2,1)S(1)} %copy-done.29, f32[2048,768]{1,0:T(8,128)S(1)} %subtract_multiply_fusion.1, f32[2048,768]{1,0:T(8,128)} %get-tuple-element.466, f32[768]{0:T(1024)S(1)} %get-tuple-element.469), kind=kOutput, calls=%fused_computation.64 | convolution fusion | flops 2442657024 | bytes 16914432 | tf_op jit(solution)/shard_map/td,fd->tf/dot_general | solution.py:189
  342.8 7.8 %fusion.61 = f32[768,768]{1,0:T(8,128)} fusion(bf16[2048,768]{1,0:T(8,128)(2,1)} %copy-done.22, f32[2048,768]{1,0:T(8,128)} %copy-done.1, f32[768]{0:T(1024)S(1)} %get-tuple-element.406, f32[768]{0:T(1024)S(1)} %get-tuple-element.407), kind=kOutput, calls=%fused_computation.132 | convolution fusion | flops 2420637696 | bytes 11802624 | tf_op jit(solution)/shard_map/td,tf->df/dot_general | solution.py:193
  350.6 59.6 %all-reduce.10.cloned.1.call-done = bf16[2048,768]{1,0:T(8,128)(2,1)} async-done(((bf16[2048,768]{1,0:T(8,128)(2,1)}), bf16[2048,768]{1,0:T(8,128)(2,1)}) %all-reduce.10.cloned.1.call-update) | async-done | bytes 3145744 | tf_op jit(solution)/shard_map/psum | solution.py:195
  410.2 7.0 multiply_reduce_fusion.5
  417.3 7.0 convert_bitcast_fusion
  434.6 64.3 %while.35 = (s32[]{:T(128)}, bf16[2,1024,3,3,64]{1,4,3,2,0:T(8,128)(2,1)}, bf16[2,1024,3,3,64]{1,4,3,2,0:T(8,128)(2,1)S(1)}, s32[2]{0:T(128)S(1)}, f32[2,3,1024]...) while((s32[]{:T(128)}, ...), condition=%wide.region_18.19_spmd.clone, body=%wide.region_16.18_spmd.clone.sunk | while | flops 2053438464 | bytes 127210408 | solution.py:232
  440.3 8.5 %multiply_reduce_fusion.9 = (f32[3,1024]{1,0:T(4,128)S(1)}, f32[3,1024,1024]{1,2,0:T(8,128)}) fusion(f32[3,1024,1024]{1,2,0:T(8,128)S(1)} %fusion.132, f32[3,1024]{1,0:T(4,128)S(1)} %dynamic-slice_bitcast_fusion.8, bf16[1024,3,3,64]{0,3,2,1:T(8,128)(2,1)S(1)} %dynamic-slice_bitcast_fusion.7, pred[3]{0:T(512)(128)(4,1)S(1)} %fusion.133, ...), kind=kOutput, calls=%fused_computation.30.clone.1 | convolution fusion | flops 424670208 | bytes 27031040 | tf_op jit(solution)/shard_map/while/body/eval_jaxpr/qhd,khd->hqk/dot_general | solution.py:211
  448.8 6.6 multiply_convert_fusion.4
  455.4 6.6 fusion.134
  472.2 8.5 %multiply_reduce_fusion.9 = (f32[3,1024]{1,0:T(4,128)S(1)}, f32[3,1024,1024]{1,2,0:T(8,128)}) fusion(f32[3,1024,1024]{1,2,0:T(8,128)S(1)} %fusion.132, f32[3,1024]{1,0:T(4,128)S(1)} %dynamic-slice_bitcast_fusion.8, bf16[1024,3,3,64]{0,3,2,1:T(8,128)(2,1)S(1)} %dynamic-slice_bitcast_fusion.7, pred[3]{0:T(512)(128)(4,1)S(1)} %fusion.133, ...), kind=kOutput, calls=%fused_computation.30.clone.1 | convolution fusion | flops 424670208 | bytes 27031040 | tf_op jit(solution)/shard_map/while/body/eval_jaxpr/qhd,khd->hqk/dot_general | solution.py:211
  480.7 6.6 multiply_convert_fusion.4
  487.3 6.6 fusion.134
  509.2 6.4 fusion.39
  548.4 5.8 pad_maximum_fusion
  554.2 8.7 %gather_fusion.1 = f32[192,96,96]{2,1,0:T(8,128)} fusion(f32[192,96,96]{2,1,0:T(8,128)} %pad_maximum_fusion, s32[1024]{0:T(1024)} %pad_clamp_fusion), kind=kCustom, calls=%fused_computation.1 | custom fusion | bytes 14156544 | tf_op jit(solution)/shard_map/gather | solution.py:250
  571.5 6.3 all-reduce.12.cloned.1.call-done
  580.8 43.9 %all-reduce = (f32[4,1152]{1,0:T(4,128)S(1)}, f32[6,768]{1,0:T(8,128)S(1)}) all-reduce(f32[4,1152]{1,0:T(4,128)S(1)} %broadcast_select_fusion, f32[6,768]{1,0:T(8,128)S(1)} %stack.39), channel_id=1, replica_groups=mesh['dp'=8,'mp'=4] {'dp','mp'}, use_global_device_ids=true, to_apply=%region_23.24 | all-reduce | flops 9216 | bytes 73728 | tf_op jit(solution)/shard_map/psum | solution.py:256
  626.0 119.5 %reduce-scatter.2.cloned.1.call-done = f32[24,96,96]{2,1,0:T(8,128)} async-done(((f32[192,96,96]{2,1,0:T(8,128)}), f32[24,96,96]{2,1,0:T(8,128)}) %reduce-scatter.2.cloned.1.call-update) | async-done | bytes 884752 | tf_op jit(solution)/shard_map/reduce_scatter | solution.py:250
  (275 shorter events, 209.2 us)
Async XLA Ops:
  7.2 738.4 %copy-start = (f32[1,24,96,96]{3,2,1,0:T(8,128)S(1)}, f32[1,24,96,96]{3,2,1,0:T(8,128)}, u32[]{:S(2)}) copy-start(f32[1,24,96,96]{3,2,1,0:T(8,128)} %param.26) | copy-start | bytes 2654212
  7.2 83.6 %all-gather.2.cloned.1.call-start = ((), (), s32[]{:S(2)}) async-start(), calls=%async_computation.1 | async-start | bytes 5308416 | tf_op jit(solution)/shard_map/all_gather | solution.py:119
  9.5 214.1 %all-reduce.6.cloned.1.call-start = ((), (), s32[]{:S(2)}) async-start(), calls=%async_computation.2 | async-start | bytes 6291456 | tf_op jit(solution)/shard_map/psum | solution.py:170
  155.9 154.9 %all-reduce.8.cloned.1.call-start = ((), (), s32[]{:S(2)}) async-start(), calls=%async_computation.3 | async-start | bytes 6291456 | tf_op jit(solution)/shard_map/psum | solution.py:177
  157.3 166.9 %copy-start.40 = (f32[768]{0:T(1024)}, f32[768]{0:T(1024)S(1)}, u32[]{:S(2)}) copy-start(f32[768]{0:T(1024)S(1)} %get-tuple-element.404) | copy-start | bytes 9220
  169.7 61.7 %copy-start.30 = (bf16[768,768]{1,0:T(8,128)(2,1)}, bf16[768,768]{1,0:T(8,128)(2,1)S(1)}, u32[]{:S(2)}) copy-start(bf16[768,768]{1,0:T(8,128)(2,1)S(1)} %reshape.372) | copy-start | bytes 3538948
  231.3 6.7 copy-start.28
  242.1 73.9 %slice-start = ((s8[6291456]{0:T(1024)(128)(4,1)}), s8[2097152]{0:T(1024)(128)(4,1)S(1)}, s32[]{:S(2)}) async-start(s8[6291456]{0:T(1024)(128)(4,1)} %bitcast.237), calls=%async_computation.7 | async-start | bytes 4194304
  242.1 168.1 %all-reduce.10.cloned.1.call-start = ((), (), s32[]{:S(2)}) async-start(), calls=%async_computation.4 | async-start | bytes 6291456 | tf_op jit(solution)/shard_map/psum | solution.py:195
  242.2 82.0 %copy-start.37 = (f32[1,8,2,128]{3,1,2,0:T(8,128)}, f32[1,8,2,128]{3,1,2,0:T(8,128)S(1)}, u32[]{:S(2)}) copy-start(f32[1,8,2,128]{3,1,2,0:T(8,128)S(1)} %copy.94) | copy-start | bytes 24580
  326.9 8.9 %copy-start.4 = (f32[2048,768]{1,0:T(8,128)}, f32[2048,768]{1,0:T(8,128)S(1)}, u32[]{:S(2)}) copy-start(f32[2048,768]{1,0:T(8,128)S(1)} %subtract_multiply_fusion.1) | copy-start | bytes 18874372
  326.9 10.6 %copy-start.31 = (bf16[768,768]{1,0:T(8,128)(2,1)S(1)}, bf16[768,768]{1,0:T(8,128)(2,1)}, u32[]{:S(2)}) copy-start(bf16[768,768]{1,0:T(8,128)(2,1)} %copy-done.30) | copy-start | bytes 3538948
  341.6 236.3 %all-reduce.12.cloned.1.call-start = ((), (), s32[]{:S(2)}) async-start(), calls=%async_computation.5 | async-start | bytes 6291456 | tf_op jit(solution)/shard_map/psum | solution.py:239
  417.3 7.1 copy-start.7
  417.3 9.6 %copy-start.23 = (bf16[192,768]{1,0:T(8,128)(2,1)S(1)}, bf16[192,768]{1,0:T(8,128)(2,1)}, u32[]{:S(2)}) copy-start(bf16[192,768]{1,0:T(8,128)(2,1)} %reshape.370) | copy-start | bytes 884740
  509.2 236.4 %reduce-scatter.2.cloned.1.call-start = ((), (), s32[]{:S(2)}) async-start(), calls=%async_computation.6 | async-start | bytes 10616832 | tf_op jit(solution)/shard_map/reduce_scatter | solution.py:250
  570.7 53.9 %copy-start.39 = (f32[6,768]{1,0:T(8,128)S(1)}, f32[6,768]{1,0:T(8,128)}, u32[]{:S(2)}) copy-start(f32[6,768]{1,0:T(8,128)} %param.31) | copy-start | bytes 55300
  570.8 53.9 %copy-start.42 = (f32[6,768]{1,0:T(8,128)S(1)}, f32[6,768]{1,0:T(8,128)}, u32[]{:S(2)}) copy-start(f32[6,768]{1,0:T(8,128)} %param.33) | copy-start | bytes 55300
  570.8 53.9 %copy-start.43 = (f32[6,768]{1,0:T(8,128)S(1)}, f32[6,768]{1,0:T(8,128)}, u32[]{:S(2)}) copy-start(f32[6,768]{1,0:T(8,128)} %param.32) | copy-start | bytes 55300
  570.8 54.6 %copy-start.46 = (f32[1,1152]{1,0:T(1,128)S(1)}, f32[1,1152]{1,0:T(1,128)}, u32[]{:S(2)}) copy-start(f32[1,1152]{1,0:T(1,128)} %param.28) | copy-start | bytes 13828
  570.8 54.6 %copy-start.48 = (f32[1,1152]{1,0:T(1,128)S(1)}, f32[1,1152]{1,0:T(1,128)}, u32[]{:S(2)}) copy-start(f32[1,1152]{1,0:T(1,128)} %param.30) | copy-start | bytes 13828
  570.8 54.6 %copy-start.49 = (f32[1,1152]{1,0:T(1,128)S(1)}, f32[1,1152]{1,0:T(1,128)}, u32[]{:S(2)}) copy-start(f32[1,1152]{1,0:T(1,128)} %param.29) | copy-start | bytes 13828
  571.5 177.4 %copy-start.19 = (f32[1,24,96,96]{3,2,1,0:T(8,128)S(1)}, f32[1,24,96,96]{3,2,1,0:T(8,128)}, u32[]{:S(2)}) copy-start(f32[1,24,96,96]{3,2,1,0:T(8,128)} %param.27) | copy-start | bytes 2654212
  626.0 124.3 %copy-start.26 = (f32[1,24,96,96]{3,2,1,0:T(8,128)S(1)}, f32[1,24,96,96]{3,2,1,0:T(8,128)}, u32[]{:S(2)}) copy-start(f32[1,24,96,96]{3,2,1,0:T(8,128)} %param.25) | copy-start | bytes 2654212
  (47 other events, 126.8 us)
Sparse Core Ops, SparseCore 0:
  10.8 79.9 all-gather.1
  156.0 67.4 all-reduce.5
  242.2 68.4 all-reduce.7
  341.7 68.5 all-reduce.9
  509.3 68.5 all-reduce.11
  581.9 163.6 reduce-scatter.1
where the time goes:
time: 774 us; the launch traced here: 765 us
  waiting for transfers between devices  386 us (50%)
  matrix products  127 us (16%)
  local copies, waits for them, and re-layouts  100 us (13%)
  other arithmetic  87.7 us (11%)
  blocking collectives  43.9 us (6%)
  between operations  15 us (2%)
    reduce_scatter x1, waiting for transfers between devices, shards(): lax.psum_scatter(natural_grads[tile_order], 'dp', scatter_dimension=0, ti...  120 us
    all_gather x1, waiting for transfers between devices, shards(): gathered = lax.all_gather(master[0].astype(bf16), 'dp', axis=0, tiled=True)  78.4 us
    psum x1, waiting for transfers between devices, shards(): ffn_out = lax.psum(part_ffn.astype(jnp.bfloat16), 'mp').astype(jnp.float32)  68.5 us
    psum x1, waiting for transfers between devices, shards(): lax.psum(part_hidden.astype(jnp.bfloat16), 'mp').astype(jnp.float32)  59.6 us
    psum x1, waiting for transfers between devices, shards(): lax.psum(part_attn.astype(jnp.bfloat16), 'mp').astype(jnp.float32)  53.9 us
    psum x1, blocking collectives, shards(): spread_sum, shared_grad = lax.psum((spread, shared_terms), ('dp', 'mp'))  43.9 us
    reshape x6, local copies, waits for them, and re-layouts, to_tiles(): matrix.reshape(row_count // tile_edge, tile_edge, col_count // tile_edge,...  19.2 us
    dot_general x2, matrix products, attend_back(): jnp.einsum('qhd,khd->hqk', block[:, 0], block[:, 1], preferred_element_ty...  17 us
  transfers between devices with their start and end apart: 6, of which 6 were waited for; matrix products, arithmetic and copies ran while one was open for 12% of the time, Pallas kernels for 0%

commit v1 on v0

v1 whole, which is shorter than its diff:
```python
import functools
import jax
import jax.numpy as jnp
from jax import lax
from jax.experimental import pallas as pl
from jax.experimental.pallas import tpu as pltpu
from jax.sharding import PartitionSpec as P

MESH = pl.DeviceIdType.MESH
f32 = jnp.float32
bf16 = jnp.bfloat16


def lanes_of(shape):
    return lax.broadcasted_iota(jnp.int32, shape, len(shape) - 1)


def turn(v, amount):
    return pltpu.roll(v, amount, v.ndim - 1)


def pack_four(tiles):
    lane = lanes_of(tiles[0].shape)
    return [
        jnp.where(lane < 96, tiles[k], turn(tiles[3], 96 - 32 * k)) for k in range(3)
    ]


def fourth_of(blocks):
    lane = lanes_of(blocks[0].shape)
    first, second, third = (turn(blocks[k], 32 + 32 * k) for k in range(3))
    return jnp.where(lane < 32, first, jnp.where(lane < 64, second, third))


def join_four(tiles):
    lane = lanes_of(tiles[0].shape)
    b, c, d = turn(tiles[1], 96), turn(tiles[2], 64), turn(tiles[3], 32)
    return [
        jnp.where(lane < 96, tiles[0], b),
        jnp.where(lane < 64, b, c),
        jnp.where(lane < 32, c, d),
    ]


def split_four(pieces):
    lane = lanes_of(pieces[0].shape)
    return [
        pieces[0],
        jnp.where(lane < 32, turn(pieces[0], 32), turn(pieces[1], 32)),
        jnp.where(lane < 64, turn(pieces[1], 64), turn(pieces[2], 64)),
        turn(pieces[2], 96),
    ]


def place():
    d, m = lax.axis_index("dp"), lax.axis_index("mp")
    return d // 2, d % 2, m // 2, m % 2


class Net:
    def __init__(self, nz):
        self.nz = nz
        self.z, self.x, self.y, self.c = place()
        self.d = self.z * 2 + self.x
        self.m = self.y * 2 + self.c
        self.xn = (self.z * 2 + 1 - self.x, self.m)
        self.yn = (self.d, (1 - self.y) * 2 + self.c)
        self.cn = (self.d, self.y * 2 + 1 - self.c)
        self.up = (self.d + 2, self.m)
        self.dn = (self.d - 2, self.m)
        self.has_up = self.z < nz - 1
        self.has_dn = self.z > 0

    def enter(self):
        bar = pltpu.get_barrier_semaphore()
        others = [(lax.rem(self.z + k, self.nz) * 2 + self.x, self.m) for k in range(1, self.nz)]
        peers = [self.xn, self.yn, self.cn] + others
        for peer in peers:
            pl.semaphore_signal(bar, inc=1, device_id=peer, device_id_type=MESH)
        pl.semaphore_wait(bar, len(peers))


def send(src, dst, ss, rs, peer):
    return pltpu.make_async_remote_copy(
        src_ref=src, dst_ref=dst, send_sem=ss, recv_sem=rs, device_id=peer, device_id_type=MESH
    )


def tile_qkv(r, j):
    return (j % 8) // 2, r * 6 + (j // 8) * 2 + j % 2


def tile_out(r, j):
    return r // 2, 48 + (r % 2) * 8 + j


def tile_up(r, j):
    return j // 8, 64 + r * 8 + j % 8


def tile_down(r, j):
    return r // 8, 128 + (r % 8) * 8 + j


GRIDS = ((8, 24, tile_qkv), (8, 8, tile_out), (8, 32, tile_up), (32, 8, tile_down))


def gather_kernel(
    nz, src_ref, master_ref, local_ref, o_qkv, o_out, o_up, o_down, o_local,
    G, LV, d_qkv, d_out, d_up, d_down,
    zs, zr, xs, xr, ys, yr, xds, xdr, yds, ydr, cs, cr, outs, lvs, lvr,
):
    net = Net(nz)
    z, x, y, c, m = net.z, net.x, net.y, net.c, net.m
    my = (1 - y) * 2 + c
    net.enter()
    full = 18
    half = 9
    LV[m] = local_ref[...]
    lv_y = send(LV.at[m], LV.at[m], lvs.at[0], lvr.at[0], net.yn)
    lv_c = send(LV.at[m], LV.at[m], lvs.at[1], lvr.at[1], net.cn)
    lv_d = send(LV.at[my], LV.at[my], lvs.at[2], lvr.at[2], net.cn)
    lv_y.start()
    lv_c.start()

    def slot(mo, zo, xo, lo=0, n=full):
        return G.at[mo, pl.ds((zo * 2 + xo) * 24 + lo, n)]

    for q in range(6):
        tiles = [
            jnp.concatenate([master_ref[4 * q + k], jnp.zeros((96, 32), f32)], axis=-1)
            for k in range(4)
        ]
        for k, block in enumerate(pack_four(tiles)):
            G[m, net.d * 24 + 3 * q + k] = block.astype(bf16)

    def z_copy(zo, direction):
        s = slot(m, zo, x)
        peer = net.up if direction == 0 else net.dn
        return send(s, s, zs.at[zo, direction], zr.at[zo], peer)

    def c_copy(zo, kind):
        mo = (m, m, my, my)[kind]
        xo = (x, 1 - x, x, 1 - x)[kind]
        s = slot(mo, zo, xo)
        return send(s, s, cs.at[zo, kind], cr.at[zo, kind], net.cn)

    def c_arrival(zo, kind):
        mo = (m, m, my, my)[kind] + 1 - 2 * c
        xo = (x, 1 - x, x, 1 - x)[kind]
        s = slot(mo, zo, xo)
        return send(s, s, cs.at[zo, kind], cr.at[zo, kind], net.cn)

    def x_copy(zo, xo):
        s = slot(m, zo, xo)
        return send(s, s, xs.at[zo], xr.at[zo], net.xn)

    def y_copy(zo, mo):
        s = slot(mo, zo, x)
        return send(s, s, ys.at[zo], yr.at[zo], net.yn)

    def xd_copy(zo, xo):
        s = slot(my, zo, xo, 0, half)
        return send(s, s, xds.at[zo], xdr.at[zo], net.xn)

    def yd_copy(zo, mo):
        s = slot(mo, zo, 1 - x, half, half)
        return send(s, s, yds.at[zo], ydr.at[zo], net.yn)

    def fan(zo):
        x_copy(zo, x).start()
        y_copy(zo, m).start()
        c_copy(zo, 0).start()

    def diag(zo):
        x_copy(zo, 1 - x).wait_recv()
        yd_copy(zo, m).start()
        c_copy(zo, 1).start()
        y_copy(zo, my).wait_recv()
        xd_copy(zo, x).start()
        c_copy(zo, 2).start()

    def fin(zo):
        xd_copy(zo, 1 - x).wait_recv()
        yd_copy(zo, my).wait_recv()
        c_copy(zo, 3).start()

    def each(step, fn):
        if step == 0:
            fn(z, 0)
            return

        @pl.when(z >= step)
        def _():
            fn(z - step, 1)

        @pl.when(z + step < nz)
        def _():
            fn(z + step, -1)

    def arrive(zo, side):
        if isinstance(side, int) and side == 0:
            @pl.when(net.has_up)
            def _():
                z_copy(zo, 0).start()

            @pl.when(net.has_dn)
            def _():
                z_copy(zo, 1).start()
        elif side == 1:
            z_copy(zo, 0).wait_recv()

            @pl.when(net.has_up)
            def _():
                z_copy(zo, 0).start()
        else:
            z_copy(zo, 1).wait_recv()

            @pl.when(net.has_dn)
            def _():
                z_copy(zo, 1).start()
        fan(zo)

    for step in range(nz + 2):
        if step < nz:
            each(step, arrive)
        if 0 <= step - 1 < nz:
            each(step - 1, lambda zo, side: diag(zo))
        if 0 <= step - 2:
            each(step - 2, lambda zo, side: fin(zo))
    send(LV.at[my], LV.at[my], lvs.at[0], lvr.at[0], net.yn).wait_recv()
    lv_d.start()
    mc = m + 1 - 2 * c
    send(LV.at[mc], LV.at[mc], lvs.at[1], lvr.at[1], net.cn).wait_recv()
    mc = my + 1 - 2 * c
    send(LV.at[mc], LV.at[mc], lvs.at[2], lvr.at[2], net.cn).wait_recv()
    o_local[...] = LV[...]
    lv_y.wait_send()
    lv_c.wait_send()
    lv_d.wait_send()
    for zo in range(nz):
        for kind in range(4):
            c_arrival(zo, kind).wait_recv()

    def sent(zo, side):
        x_copy(zo, x).wait_send()
        y_copy(zo, m).wait_send()
        yd_copy(zo, m).wait_send()
        xd_copy(zo, x).wait_send()
        for kind in range(4):
            c_copy(zo, kind).wait_send()
        if side == 0 or side == 1:
            @pl.when(net.has_up)
            def _():
                z_copy(zo, 0).wait_send()
        if side == 0 or side == -1:
            @pl.when(net.has_dn)
            def _():
                z_copy(zo, 1).wait_send()

    for step in range(nz):
        each(step, sent)

    def fourth(i, _):
        mo, rest = i // (2 * nz), i % (2 * nz)
        for q in range(6):
            tile = fourth_of([G[mo, rest * 24 + 3 * q + k].astype(f32) for k in range(3)])
            G[mo, rest * 24 + 18 + q] = tile.astype(bf16)
        return 0

    lax.fori_loop(0, 4 * 2 * nz, fourth, 0)

    copies = []
    for i, ((rows, cols, where), dense, out) in enumerate(
        zip(GRIDS, (d_qkv, d_out, d_up, d_down), (o_qkv, o_out, o_up, o_down))
    ):
        def fill(r, _):
            for g in range(cols // 4):
                tiles = []
                for t in range(4):
                    p, n = where(r, 4 * g + t)
                    tiles.append(G[p, src_ref[n]].astype(f32))
                for k, piece in enumerate(join_four(tiles)):
                    dense[pl.ds(pl.multiple_of(r * 96, 96), 96), pl.ds(384 * g + 128 * k, 128)] = (
                        piece.astype(bf16)
                    )
            return 0

        lax.fori_loop(0, rows, fill, 0)
        copy = pltpu.make_async_copy(dense, out, outs.at[i])
        copy.start()
        copies.append(copy)
    for copy in copies:
        copy.wait()


def gather_weights(nz, src, master, local):
    dma = pltpu.SemaphoreType.DMA
    shapes = [(r * 96, c * 96) for r, c, _ in GRIDS]
    return pl.pallas_call(
        functools.partial(gather_kernel, nz),
        out_shape=[jax.ShapeDtypeStruct(s, bf16) for s in shapes]
        + [jax.ShapeDtypeStruct((4, *local.shape), f32)],
        in_specs=[pl.BlockSpec(memory_space=pltpu.SMEM)]
        + [pl.BlockSpec(memory_space=pltpu.VMEM)] * 2,
        out_specs=[pl.BlockSpec(memory_space=pl.ANY)] * 4 + [pl.BlockSpec(memory_space=pltpu.VMEM)],
        scratch_shapes=[pltpu.VMEM((4, 2 * nz * 24, 96, 128), bf16), pltpu.VMEM((4, *local.shape), f32)]
        + [pltpu.VMEM(s, bf16) for s in shapes]
        + [dma((nz, 2)), dma((nz,))]
        + [dma((nz,))] * 8
        + [dma((nz, 4)), dma((nz, 4)), dma((4,)), dma((3,)), dma((3,))],
        compiler_params=pltpu.CompilerParams(
            collective_id=0, has_side_effects=True, vmem_limit_bytes=56 << 20
        ),
        name="gather_weights",
    )(src, master, local)


def slot_sources(tile_order, per_owner):
    count = tile_order.shape[0]
    hit = tile_order[None, :] == jnp.arange(count, dtype=jnp.int32)[:, None]
    at = jnp.sum(jnp.where(hit, jnp.arange(count, dtype=jnp.int32)[None, :], 0), 1)
    owner, pos = at // per_owner, at % per_owner
    quad, k = pos // 4, pos % 4
    return owner * 24 + jnp.where(k < 3, 3 * quad + k, 18 + quad)
NEG_BIG = -1e30
NORM_EPS = 1e-05
ROOT_HALF = 0.7071067811865476
PHI_SCALE = 0.3989422804014327


def nt(a, b):
    return lax.dot_general(a, b, (((1,), (1,)), ((), ())), preferred_element_type=f32)


def tn(a, b):
    return lax.dot_general(a, b, (((0,), (0,)), ((), ())), preferred_element_type=f32)


def nn(a, b):
    return jnp.dot(a, b, preferred_element_type=f32)


def edges(info_ref):
    length = info_ref[2]
    return 64 * ((length + 127) // 128), length, info_ref[1]


def chosen_rows(info_ref, rows):
    bound, _, part = edges(info_ref)
    row = lax.broadcasted_iota(jnp.int32, (rows, 128), 0) + part * rows
    lane = lax.broadcasted_iota(jnp.int32, (rows, 128), 1)
    return (row < bound) == (lane < 64)


def chosen_cols(info_ref, rows):
    bound, _, part = edges(info_ref)
    row = lax.broadcasted_iota(jnp.int32, (128, rows), 1) + part * rows
    lane = lax.broadcasted_iota(jnp.int32, (128, rows), 0)
    return (row < bound) == (lane < 64)


def attend_kernel(info_ref, x_ref, w_ref, b_ref, q_ref, k_ref, v_ref, p_ref, o_ref):
    pair = pl.program_id(0)
    rows = q_ref.shape[0]
    width = q_ref.shape[1]
    bound, length, part = edges(info_ref)
    zero = jnp.zeros((), bf16)

    @pl.when(pair == 0)
    def _():
        def project(lo, at, count):
            def body(r, _):
                base = pl.multiple_of(at + r * rows, rows)
                out = nn(x_ref[pl.ds(base, rows), :], w_ref[:, lo : lo + 256]) + b_ref[:, lo : lo + 256]
                lane = lo % width
                if lo < width:
                    q_ref[:, lane : lane + 256] = out.astype(bf16) * jnp.asarray(0.125, bf16)
                elif lo < 2 * width:
                    k_ref[pl.ds(base, rows), lane : lane + 256] = out.astype(bf16)
                else:
                    v_ref[pl.ds(base, rows), lane : lane + 256] = out.astype(bf16)
                return 0

            lax.fori_loop(0, count, body, 0)

        for lo in range(0, width, 256):
            project(lo, part * rows, 1)
        for lo in range(width, 3 * width, 256):
            project(lo, 0, x_ref.shape[0] // rows)

    cols = pl.ds(pl.multiple_of(pair * 128, 128), 128)
    queries = q_ref[:, cols]
    pick = chosen_rows(info_ref, rows)
    outs = []
    for w in range(2):
        start = 0 if w == 0 else pl.multiple_of(bound, 64)
        limit = bound if w == 0 else length - bound
        keys = k_ref[pl.ds(start, rows), cols]
        values = v_ref[pl.ds(start, rows), cols]
        these = jnp.where(pick, queries, zero) if w == 0 else jnp.where(pick, zero, queries)
        scores = nt(keys, these)
        inside = lax.broadcasted_iota(jnp.int32, scores.shape, 0) < limit
        scores = jnp.where(inside, scores, NEG_BIG)
        top = jnp.max(scores, 0, keepdims=True)
        weight = jnp.exp(scores - top)
        probs = (weight * (1.0 / jnp.sum(weight, 0, keepdims=True))).astype(bf16)
        p_ref[0, w] = probs
        outs.append(tn(values, probs))
    o_ref[...] = jnp.where(chosen_cols(info_ref, rows), outs[0], outs[1]).astype(bf16)


def attend(info, tokens, w_qkv, bias, seq_len, rows):
    width = w_qkv.shape[0]
    pairs = width // 128
    whole = lambda shape: pl.BlockSpec(shape, lambda i, s: (0,) * len(shape))
    return pl.pallas_call(
        attend_kernel,
        grid_spec=pltpu.PrefetchScalarGridSpec(
            num_scalar_prefetch=1,
            grid=(pairs,),
            in_specs=[
                pl.BlockSpec((seq_len, width), lambda i, s: (s[0], 0)),
                whole((width, 3 * width)),
                whole((1, 3 * width)),
            ],
            out_specs=[
                whole((rows, width)),
                whole((seq_len, width)),
                whole((seq_len, width)),
                pl.BlockSpec((1, 2, rows, rows), lambda i, s: (i, 0, 0, 0)),
                pl.BlockSpec((128, rows), lambda i, s: (i, 0)),
            ],
        ),
        out_shape=[
            jax.ShapeDtypeStruct((rows, width), bf16),
            jax.ShapeDtypeStruct((seq_len, width), bf16),
            jax.ShapeDtypeStruct((seq_len, width), bf16),
            jax.ShapeDtypeStruct((pairs, 2, rows, rows), bf16),
            jax.ShapeDtypeStruct((width, rows), bf16),
        ],
        compiler_params=pltpu.CompilerParams(vmem_limit_bytes=56 << 20),
        name="attend",
    )(info, tokens, w_qkv, bias)


def standard(values):
    centre = values - jnp.mean(values, -1, keepdims=True)
    scale = lax.rsqrt(jnp.mean(centre * centre, -1, keepdims=True) + NORM_EPS)
    return centre * scale, scale


def standard_back(grad, normed, scale, gain):
    inner = grad * gain
    return scale * (
        inner - jnp.mean(inner, -1, keepdims=True) - normed * jnp.mean(inner * normed, -1, keepdims=True)
    )


def col_sum(values):
    return jnp.sum(values, 0, keepdims=True)


def middle_kernel(
    info_ref, o_ref, wo_ref, x_ref, cot_ref, sv_ref, wu_ref, wd_ref, bu_ref,
    out_ref, tu_ref, td_ref, to_ref, go_ref, gz_ref, db_ref, ds_ref,
    hid, low, low_t, n_one, r_one, acc, act, slope, g_low,
):
    step = pl.program_id(0)
    chunks = pl.num_programs(0) // 2
    rows, width = hid.shape
    piece = 128

    def by_rows(fn):
        def body(r, _):
            fn(pl.ds(pl.multiple_of(r * piece, piece), piece), r)
            return 0

        lax.fori_loop(0, rows // piece, body, 0)

    @pl.when(step == 0)
    def _():
        acc[...] = tn(o_ref[...], wo_ref[...])

        def norm(at, r):
            z_one = x_ref[at, :].astype(f32) + acc[at, :] + sv_ref[0:1, :]
            normed, scale = standard(z_one)
            hidden = normed * sv_ref[2:3, :] + sv_ref[3:4, :]
            n_one[at, :] = normed
            r_one[at, :] = jnp.broadcast_to(scale, (piece, 128))
            hid[at, :] = hidden
            low[at, :] = hidden.astype(bf16)
            acc[at, :] = jnp.zeros((piece, width), f32)

        by_rows(norm)
        low_t[...] = low[...].T

    @pl.when(step < chunks)
    def _():
        pre = nn(low[...], wu_ref[...]) + bu_ref[...]
        phi = 0.5 * (1.0 + lax.erf(pre * ROOT_HALF))
        density = jnp.exp(-0.5 * pre * pre) * PHI_SCALE
        here = (pre * phi).astype(bf16)
        act[step] = here
        slope[step] = (phi + pre * density).astype(bf16)
        acc[...] += nn(here, wd_ref[...])

    @pl.when(step == chunks)
    def _():
        ds_ref[...] = jnp.zeros_like(ds_ref)
        _, length, part = edges(info_ref)

        def norm(at, r):
            z_two = hid[at, :] + acc[at, :] + sv_ref[1:2, :]
            normed, scale = standard(z_two)
            row = lax.broadcasted_iota(jnp.int32, (piece, 1), 0) + part * rows + r * piece
            valid = (row < length).astype(f32)
            out_ref[at, :] = ((normed * sv_ref[4:5, :] + sv_ref[5:6, :]) * valid).astype(bf16)
            grad = cot_ref[at, :].astype(f32) * valid
            back = standard_back(grad, normed, scale, sv_ref[4:5, :])
            ds_ref[4:5, :] += col_sum(grad * normed)
            ds_ref[5:6, :] += col_sum(grad)
            ds_ref[1:2, :] += col_sum(back)
            g_low[at, :] = back.astype(bf16)
            acc[at, :] = back

        by_rows(norm)

    @pl.when(step >= chunks)
    def _():
        at = step - chunks
        grad_act = nt(g_low[...], wd_ref[...])
        grad_pre = grad_act * slope[at].astype(f32)
        grad_low = grad_pre.astype(bf16)
        db_ref[...] = col_sum(grad_low.astype(f32))
        acc[...] += nt(grad_low, wu_ref[...])
        down = tn(act[at], g_low[...])
        for r in range(4):
            for g in range(width // 384):
                cut = [
                    down[96 * r : 96 * r + 96, 384 * g + 128 * k : 384 * g + 128 * k + 128]
                    for k in range(3)
                ]
                for t, tile in enumerate(split_four(cut)):
                    td_ref[0, 0, r * (width // 96) + 4 * g + t] = tile.astype(bf16)
        up = nn(low_t[...], grad_low)
        for r in range(width // 96):
            cut = [up[96 * r : 96 * r + 96, 128 * k : 128 * k + 128] for k in range(3)]
            for t, tile in enumerate(split_four(cut)):
                tu_ref[0, r, 0, t] = tile.astype(bf16)

    @pl.when(step == 2 * chunks - 1)
    def _():
        def norm(at, r):
            grad = acc[at, :]
            normed = n_one[at, :]
            back = standard_back(grad, normed, r_one[at, 0:1], sv_ref[2:3, :])
            ds_ref[2:3, :] += col_sum(grad * normed)
            ds_ref[3:4, :] += col_sum(grad)
            ds_ref[0:1, :] += col_sum(back)
            gz_ref[at, :] = back
            g_low[at, :] = back.astype(bf16)

        by_rows(norm)
        go_ref[...] = nt(g_low[...], wo_ref[...]).astype(bf16)
        for g in range(width // 384):
            outer = nn(o_ref[...], g_low[:, 384 * g : 384 * g + 384])
            for r in range(width // 96):
                cut = [outer[96 * r : 96 * r + 96, 128 * k : 128 * k + 128] for k in range(3)]
                for t, tile in enumerate(split_four(cut)):
                    to_ref[r, 4 * g + t] = tile.astype(bf16)


def middle(info, o_t, w_out, tokens, cotangent, shared, w_up, w_down, bias_up, rows):
    width = w_out.shape[0]
    hidden = w_up.shape[1]
    cut = 384
    chunks = hidden // cut
    groups = hidden // 768
    whole = lambda shape: pl.BlockSpec(shape, lambda i, s: (0,) * len(shape))
    back = lambda i: jnp.maximum(i - chunks, 0)
    dma_rows = pl.BlockSpec((rows, width), lambda i, s: (s[3], 0))
    tiles = width // 96
    return pl.pallas_call(
        middle_kernel,
        grid_spec=pltpu.PrefetchScalarGridSpec(
            num_scalar_prefetch=1,
            grid=(2 * chunks,),
            in_specs=[
                whole((width, rows)),
                whole((width, width)),
                dma_rows,
                dma_rows,
                whole((6, width)),
                pl.BlockSpec((width, cut), lambda i, s: (0, i % chunks)),
                pl.BlockSpec((cut, width), lambda i, s: (i % chunks, 0)),
                pl.BlockSpec((1, cut), lambda i, s: (0, i % chunks)),
            ],
            out_specs=[
                whole((rows, width)),
                pl.BlockSpec(
                    (1, tiles, 1, 4, 96, 128), lambda i, s: (back(i) // 2, 0, back(i) % 2, 0, 0, 0)
                ),
                pl.BlockSpec(
                    (1, 1, 4 * tiles, 96, 128), lambda i, s: (back(i) // 2, back(i) % 2, 0, 0, 0)
                ),
                whole((tiles, tiles, 96, 128)),
                whole((rows, width)),
                whole((rows, width)),
                pl.BlockSpec((1, cut), lambda i, s: (0, back(i))),
                whole((6, width)),
            ],
            scratch_shapes=[
                pltpu.VMEM((rows, width), f32),
                pltpu.VMEM((rows, width), bf16),
                pltpu.VMEM((width, rows), bf16),
                pltpu.VMEM((rows, width), f32),
                pltpu.VMEM((rows, 128), f32),
                pltpu.VMEM((rows, width), f32),
                pltpu.VMEM((chunks, rows, cut), bf16),
                pltpu.VMEM((chunks, rows, cut), bf16),
                pltpu.VMEM((rows, width), bf16),
            ],
        ),
        out_shape=[
            jax.ShapeDtypeStruct((rows, width), bf16),
            jax.ShapeDtypeStruct((groups, tiles, 2, 4, 96, 128), bf16),
            jax.ShapeDtypeStruct((groups, 2, 4 * tiles, 96, 128), bf16),
            jax.ShapeDtypeStruct((tiles, tiles, 96, 128), bf16),
            jax.ShapeDtypeStruct((rows, width), bf16),
            jax.ShapeDtypeStruct((rows, width), f32),
            jax.ShapeDtypeStruct((1, hidden), f32),
            jax.ShapeDtypeStruct((6, width), f32),
        ],
        compiler_params=pltpu.CompilerParams(vmem_limit_bytes=56 << 20),
        name="middle",
    )(info, o_t, w_out, tokens, cotangent, shared, w_up, w_down, bias_up)


def attend_back_kernel(
    info_ref, go_ref, q_ref, k_ref, v_ref, p_ref, o_ref, x_ref, w_ref, gz_ref,
    tq_ref, own_ref, other_ref, bias_ref, dq, dk, dv,
):
    pair = pl.program_id(0)
    rows, width = dq.shape
    seq_len = dk.shape[0]
    bound, length, part = edges(info_ref)
    zero = jnp.zeros((), bf16)
    cols = pl.ds(pl.multiple_of(pair * 128, 128), 128)
    pick = chosen_rows(info_ref, rows)
    pick_t = chosen_cols(info_ref, rows)
    queries = q_ref[:, cols]
    grads = go_ref[...]
    grads_t = grads.astype(f32).T
    inner = grads_t * o_ref[...].astype(f32)
    outs = []
    dk[rows:, cols] = jnp.zeros((seq_len - rows, 128), bf16)
    dv[rows:, cols] = jnp.zeros((seq_len - rows, 128), bf16)
    for w in range(2):
        start = 0 if w == 0 else pl.multiple_of(bound, 64)
        keys = k_ref[pl.ds(start, rows), cols]
        values = v_ref[pl.ds(start, rows), cols]
        mine = (lambda a: jnp.where(pick, a, zero)) if w == 0 else (lambda a: jnp.where(pick, zero, a))
        mine_t = (lambda a: jnp.where(pick_t, a, 0.0)) if w == 0 else (lambda a: jnp.where(pick_t, 0.0, a))
        dot_sum = jnp.sum(mine_t(inner), 0, keepdims=True)
        grad_probs = nn(values, mine_t(grads_t).astype(bf16))
        probs = p_ref[0, w]
        grad_scores = (probs.astype(f32) * (grad_probs - dot_sum)).astype(bf16)
        dv[pl.ds(start, rows), cols] = nn(probs, mine(grads)).astype(bf16)
        dk[pl.ds(start, rows), cols] = nn(grad_scores, mine(queries)).astype(bf16)
        outs.append(tn(keys, grad_scores))
    dq[:, cols] = (jnp.where(pick_t, outs[0], outs[1]) * 0.125).T.astype(bf16)

    @pl.when(pair == pl.num_programs(0) - 1)
    def _():
        here = pl.ds(pl.multiple_of(part * rows, rows), rows)
        there = pl.ds(pl.multiple_of((1 - part) * rows, rows), rows)
        bias_ref[0:1, :] = col_sum(dq[...].astype(f32))
        bias_ref[1:2, :] = col_sum(dv[...].astype(f32))
        own_ref[...] = (
            gz_ref[...]
            + nt(dq[...], w_ref[:, :width])
            + nt(dk[here, :], w_ref[:, width : 2 * width])
            + nt(dv[here, :], w_ref[:, 2 * width :])
        )
        other_ref[...] = (
            nt(dk[there, :], w_ref[:, width : 2 * width]) + nt(dv[there, :], w_ref[:, 2 * width :])
        ).astype(bf16)
        for index, (grad, source) in enumerate(((dq, here), (dk, pl.ds(0, seq_len)), (dv, pl.ds(0, seq_len)))):
            for g in range(width // 384):
                outer = tn(x_ref[source, :], grad[:, 384 * g : 384 * g + 384])
                for r in range(width // 96):
                    cut = [outer[96 * r : 96 * r + 96, 128 * k : 128 * k + 128] for k in range(3)]
                    for t, tile in enumerate(split_four(cut)):
                        p, n = tile_qkv(r, index * (width // 96) + 4 * g + t)
                        tq_ref[p, n] = tile.astype(bf16)


def attend_back(info, g_o, q, k, v, probs, o_t, tokens, w_qkv, g_z):
    rows, width = q.shape
    seq_len = k.shape[0]
    pairs = width // 128
    whole = lambda shape: pl.BlockSpec(shape, lambda i, s: (0,) * len(shape))
    return pl.pallas_call(
        attend_back_kernel,
        grid_spec=pltpu.PrefetchScalarGridSpec(
            num_scalar_prefetch=1,
            grid=(pairs,),
            in_specs=[
                pl.BlockSpec((rows, 128), lambda i, s: (0, i)),
                whole((rows, width)),
                whole((seq_len, width)),
                whole((seq_len, width)),
                pl.BlockSpec((1, 2, rows, rows), lambda i, s: (i, 0, 0, 0)),
                pl.BlockSpec((128, rows), lambda i, s: (i, 0)),
                pl.BlockSpec((seq_len, width), lambda i, s: (s[0], 0)),
                whole((width, 3 * width)),
                whole((rows, width)),
            ],
            out_specs=[
                whole((4, 48, 96, 128)),
                whole((rows, width)),
                whole((rows, width)),
                whole((2, width)),
            ],
            scratch_shapes=[
                pltpu.VMEM((rows, width), bf16),
                pltpu.VMEM((seq_len, width), bf16),
                pltpu.VMEM((seq_len, width), bf16),
            ],
        ),
        out_shape=[
            jax.ShapeDtypeStruct((4, 48, 96, 128), bf16),
            jax.ShapeDtypeStruct((rows, width), f32),
            jax.ShapeDtypeStruct((rows, width), bf16),
            jax.ShapeDtypeStruct((2, width), f32),
        ],
        compiler_params=pltpu.CompilerParams(vmem_limit_bytes=56 << 20),
        name="attend_back",
    )(info, g_o, q, k, v, probs, o_t, tokens, w_qkv, g_z)
def pack_kernel(order_ref, tq_ref, to_ref, tu_ref, td_ref, w_ref, tiles, sems):
    p, d = pl.program_id(0), pl.program_id(1)
    slot = p % 2

    def loads(group, at):
        first = 0
        for i, src in enumerate((tq_ref, to_ref, tu_ref, td_ref)):
            count = src.shape[1]
            yield pltpu.make_async_copy(
                src.at[group], tiles.at[at, pl.ds(first, count)], sems.at[at, i]
            )
            first += count

    @pl.when((p == 0) & (d == 0))
    def _():
        for copy in loads(0, 0):
            copy.start()

    @pl.when(d == 0)
    def _():
        for copy in loads(p, slot):
            copy.wait()

        @pl.when(p + 1 < pl.num_programs(0))
        def _():
            for copy in loads(p + 1, 1 - slot):
                copy.start()

    for q in range(6):
        four = [tiles[slot, order_ref[d * 24 + 4 * q + t]].astype(f32) for t in range(4)]
        for k, block in enumerate(pack_four(four)):
            w_ref[0, 0, 3 * q + k] = block.astype(bf16)


def pack(order, tq, to, tu, td):
    owners = order.shape[0] // 24
    anywhere = pl.BlockSpec(memory_space=pl.ANY)
    return pl.pallas_call(
        pack_kernel,
        grid_spec=pltpu.PrefetchScalarGridSpec(
            num_scalar_prefetch=1,
            grid=(4, owners),
            in_specs=[anywhere] * 4,
            out_specs=pl.BlockSpec((1, 1, 18, 96, 128), lambda p, d, s: (p, d, 0, 0, 0)),
            scratch_shapes=[
                pltpu.VMEM((2, order.shape[0], 96, 128), bf16),
                pltpu.SemaphoreType.DMA((2, 4)),
            ],
        ),
        out_shape=jax.ShapeDtypeStruct((4, owners, 18, 96, 128), bf16),
        compiler_params=pltpu.CompilerParams(vmem_limit_bytes=40 << 20),
        name="pack",
    )(order, tq, to, tu, td)


def scatter_kernel(
    nz, w_ref, own_ref, other_ref, local_ref, shared_ref,
    tile_o, dx_o, local_o, shared_o,
    A, R, XD, YD, X, Y, Z, dx_in, la, lb, sa, sb,
    lsem, cs, cr, xds, xdr, yds, ydr, xs, xr, ys, yr, zs, zr, dxs, vs, vr,
):
    net = Net(nz)
    z, x, y, c, m, d = net.z, net.x, net.y, net.c, net.m, net.d
    my = (1 - y) * 2 + c
    far = (lax.rem(z + 2, nz) * 2 + x, m)
    near = ((z + 1 - 2 * (z % 2)) * 2 + x, m)
    net.enter()
    half = 9
    low, high = pl.ds(0, half), pl.ds(half, half)
    kinds = ((m, x), (m, 1 - x), (my, x), (my, 1 - x))
    flip = 1 - 2 * c

    def load(zo, kind):
        mo, xo = kinds[kind]
        return pltpu.make_async_copy(w_ref.at[mo, zo * 2 + xo], A.at[zo, kind], lsem.at[zo, kind])

    def c_copy(zo, kind):
        mo, xo = kinds[kind]
        return send(
            w_ref.at[mo + flip, zo * 2 + xo], R.at[zo, kind], cs.at[zo, kind], cr.at[zo, kind], net.cn
        )

    def xd_copy(zo):
        return send(A.at[zo, 3, low], XD.at[zo], xds.at[zo], xdr.at[zo], net.xn)

    def yd_copy(zo):
        return send(A.at[zo, 3, high], YD.at[zo], yds.at[zo], ydr.at[zo], net.yn)

    def x_copy(zo):
        return send(A.at[zo, 1], X.at[zo], xs.at[zo], xr.at[zo], net.xn)

    def y_copy(zo):
        return send(A.at[zo, 2], Y.at[zo], ys.at[zo], yr.at[zo], net.yn)

    def z_copy(zo, direction):
        return send(
            A.at[zo, 0], Z.at[zo, direction], zs.at[zo], zr.at[zo, direction],
            net.up if direction == 0 else net.dn,
        )

    dx_copy = send(other_ref, dx_in, dxs.at[0], dxs.at[1], net.cn)
    peers = (net.cn, net.xn, net.yn, near, far)

    def v_copies(k):
        return (
            send(la.at[k], lb.at[k], vs.at[k, 0], vr.at[k, 0], peers[k]),
            send(sa.at[k], sb.at[k], vs.at[k, 1], vr.at[k, 1], peers[k]),
        )

    def v_start(k):
        for copy in v_copies(k):
            copy.start()

    def v_finish(k):
        for copy in v_copies(k):
            copy.wait_recv()
        la[k + 1] = la[k] + lb[k]
        sa[k + 1] = sa[k] + sb[k]

    def add(zo, kind, other, lo=0, n=18):
        def body(i, _):
            A[zo, kind, lo + i] = (A[zo, kind, lo + i].astype(f32) + other(i)).astype(bf16)
            return 0

        lax.fori_loop(0, n, body, 0)

    def each(step, fn):
        if step == 0:
            fn(z, 0)
            return

        @pl.when(z >= step)
        def _():
            fn(z - step, 1)

        @pl.when(z + step < nz)
        def _():
            fn(z + step, -1)

    def begin(zo, side):
        for kind in (3, 1, 2, 0):
            load(zo, kind).start()
            c_copy(zo, kind).start()

    def phase_one(zo, side):
        for kind in (3, 1, 2, 0):
            load(zo, kind).wait()
            c_copy(zo, kind).wait_recv()
            add(zo, kind, lambda i: R[zo, kind, i].astype(f32))
            if kind == 3:
                xd_copy(zo).start()
                yd_copy(zo).start()

    def phase_two(zo, side):
        yd_copy(zo).wait_recv()
        add(zo, 1, lambda i: YD[zo, i].astype(f32), half, half)
        x_copy(zo).start()
        xd_copy(zo).wait_recv()
        add(zo, 2, lambda i: XD[zo, i].astype(f32), 0, half)
        y_copy(zo).start()

    def phase_three(zo, side):
        x_copy(zo).wait_recv()
        y_copy(zo).wait_recv()
        add(zo, 0, lambda i: X[zo, i].astype(f32) + Y[zo, i].astype(f32))
        if isinstance(side, int) and side == 0:
            return
        if side == -1:
            @pl.when(net.has_dn)
            def _():
                z_copy(zo, 0).wait_recv()
                add(zo, 0, lambda i: Z[zo, 0, i].astype(f32))

            z_copy(zo, 0).start()
        else:
            @pl.when(net.has_up)
            def _():
                z_copy(zo, 1).wait_recv()
                add(zo, 0, lambda i: Z[zo, 1, i].astype(f32))

            z_copy(zo, 1).start()

    la[0] = local_ref[...]
    sa[0] = shared_ref[...]
    v_start(0)
    for step in range(nz - 1, -1, -1):
        each(step, begin)
    dx_copy.start()
    for turn_no in range(nz + 2):
        if turn_no < nz:
            each(nz - 1 - turn_no, phase_one)
        if 0 <= turn_no - 1 < nz:
            each(nz - turn_no, phase_two)
        if 0 <= turn_no - 2:
            each(nz + 1 - turn_no, phase_three)
        if turn_no < 5:
            v_finish(turn_no)
            if turn_no < 4:
                v_start(turn_no + 1)
    local_o[...] = la[5]
    shared_o[...] = sa[5]
    dx_copy.wait_recv()

    def join(r, _):
        at = pl.ds(pl.multiple_of(r * 128, 128), 128)
        dx_o[at, :] = own_ref[at, :] + dx_in[at, :].astype(f32)
        return 0

    lax.fori_loop(0, own_ref.shape[0] // 128, join, 0)

    @pl.when(net.has_dn)
    def _():
        z_copy(z, 0).wait_recv()

    @pl.when(net.has_up)
    def _():
        z_copy(z, 1).wait_recv()

    def finish(q, _):
        blocks = []
        for k in range(3):
            at = 3 * q + k
            total = A[z, 0, at].astype(f32)
            total = total + jnp.where(net.has_dn, Z[z, 0, at].astype(f32), 0.0)
            total = total + jnp.where(net.has_up, Z[z, 1, at].astype(f32), 0.0)
            tile_o[4 * q + k] = total
            blocks.append(total)
        tile_o[4 * q + 3] = fourth_of(blocks)
        return 0

    lax.fori_loop(0, 6, finish, 0)

    def sent(zo, side):
        for kind in range(4):
            c_copy(zo, kind).wait_send()
        xd_copy(zo).wait_send()
        yd_copy(zo).wait_send()
        x_copy(zo).wait_send()
        y_copy(zo).wait_send()
        if isinstance(side, int) and side == 0:
            return
        z_copy(zo, 0).wait_send()

    for step in range(nz):
        each(step, sent)
    dx_copy.wait_send()
    for k in range(5):
        for copy in v_copies(k):
            copy.wait_send()


def scatter_grads(nz, wire, own, other, local, shared):
    dma = pltpu.SemaphoreType.DMA
    vm = pl.BlockSpec(memory_space=pltpu.VMEM)
    block = lambda *lead: pltpu.VMEM((*lead, 96, 128), bf16)
    return pl.pallas_call(
        functools.partial(scatter_kernel, nz),
        out_shape=[
            jax.ShapeDtypeStruct((24, 96, 128), f32),
            jax.ShapeDtypeStruct(own.shape, f32),
            jax.ShapeDtypeStruct(local.shape, f32),
            jax.ShapeDtypeStruct(shared.shape, f32),
        ],
        in_specs=[pl.BlockSpec(memory_space=pl.ANY), vm, vm, vm, vm],
        out_specs=[vm] * 4,
        scratch_shapes=[
            block(nz, 4, 18), block(nz, 4, 18), block(nz, 9), block(nz, 9), block(nz, 18), block(nz, 18),
            block(nz, 2, 18), pltpu.VMEM(other.shape, bf16),
            pltpu.VMEM((6, *local.shape), f32), pltpu.VMEM((5, *local.shape), f32),
            pltpu.VMEM((6, *shared.shape), f32), pltpu.VMEM((5, *shared.shape), f32),
            dma((nz, 4)), dma((nz, 4)), dma((nz, 4)),
        ]
        + [dma((nz,))] * 9
        + [dma((nz, 2)), dma((2,)), dma((5, 2)), dma((5, 2))],
        compiler_params=pltpu.CompilerParams(
            collective_id=1, has_side_effects=True, vmem_limit_bytes=56 << 20
        ),
        name="scatter_grads",
    )(wire, own, other, local, shared)


STEP = 5
BETA_ONE = 0.5
BETA_TWO = 0.5
ADAM_EPS = 1e-08
RATE_TILES = 0.04
RATE_VECTORS = 0.2
DECAY = 0.01
HIGH = lax.Precision.HIGHEST


def adam(grad, first, second):
    first_new = BETA_ONE * first + (1.0 - BETA_ONE) * grad
    second_new = BETA_TWO * second + (1.0 - BETA_TWO) * grad * grad
    step_dir = (
        first_new
        / (1.0 - BETA_ONE**STEP)
        / (jnp.sqrt(second_new / (1.0 - BETA_TWO**STEP)) + ADAM_EPS)
    )
    return (first_new, second_new, step_dir)


def from_tiles(tile_set, row_count, col_count):
    edge = tile_set.shape[-1]
    return (
        tile_set.reshape(row_count // edge, col_count // edge, edge, edge)
        .transpose(0, 2, 1, 3)
        .reshape(row_count, col_count)
    )


def plain_weights(tile_order, master, local):
    tiles = lax.all_gather(master.astype(bf16), "dp", axis=0, tiled=True)
    tiles = lax.all_gather(tiles, "mp", axis=0)
    count = tile_order.shape[0]
    inverse = jnp.zeros((count,), jnp.int32).at[tile_order].set(jnp.arange(count, dtype=jnp.int32))
    natural = tiles[:, inverse]
    dense = []
    for rows, cols, where in GRIDS:
        pieces = []
        for r in range(rows):
            pick = [where(r, j) for j in range(cols)]
            groups = jnp.asarray([p for p, _ in pick], jnp.int32)
            numbers = jnp.asarray([n for _, n in pick], jnp.int32)
            pieces.append(natural[groups, numbers].transpose(1, 0, 2).reshape(96, cols * 96))
        dense.append(jnp.concatenate(pieces, 0))
    return (*dense, lax.all_gather(local, "mp", axis=0))


def plain_scatter(order, tq, to, tu, td, own, other, local, shared):
    tiles = jnp.concatenate([tq, to, tu, td], 1)[:, order, :, :96].astype(f32)
    mine = lax.psum_scatter(tiles, "mp", scatter_dimension=0, tiled=False)
    owned = lax.psum_scatter(mine, "dp", scatter_dimension=0, tiled=True)
    count = lax.axis_size("mp")
    swapped = lax.ppermute(other, "mp", [(i, i ^ 1) for i in range(count)])
    local_sum, shared_sum = lax.psum((local, shared), ("dp", "mp"))
    return owned, own + swapped.astype(f32), local_sum, shared_sum


def shards(
    tokens,
    cotangent,
    lengths,
    tile_order,
    master,
    first_moment,
    second_moment,
    basis_left,
    basis_right,
    local_vec,
    local_first,
    local_second,
    shared_vec,
    shared_first,
    shared_second,
):
    group_count = lax.axis_size("mp")
    group_index = lax.axis_index("mp")
    owners = lax.axis_size("dp")
    row_total, width = tokens.shape
    seq_len = row_total // lengths.shape[0]
    rows = row_total // group_count
    per_owner = master.shape[1]
    nz = owners // 2
    routed = per_owner == 24 and nz == 4 and group_count == 4

    seq = group_index * rows // seq_len
    part = group_index * rows % seq_len // rows
    length = lax.dynamic_index_in_dim(lengths, seq, 0, keepdims=False)
    info = jnp.stack([seq, part, length, group_index]).astype(jnp.int32)

    if routed:
        w_qkv, w_out, w_up, w_down, vectors = gather_weights(
            nz, slot_sources(tile_order, per_owner), master[0], local_vec
        )
    else:
        w_qkv, w_out, w_up, w_down, vectors = plain_weights(tile_order, master[0], local_vec)
    vectors = vectors[:, 0]
    attn = width // group_count
    bias_q = vectors[:, :attn].reshape(1, width)
    bias_v = vectors[:, attn : 2 * attn].reshape(1, width)
    bias_qkv = jnp.concatenate([bias_q, jnp.zeros_like(bias_q), bias_v], 1)
    bias_up = vectors[:, 2 * attn :].reshape(1, -1)

    q, k, v, probs, o_t = attend(info, tokens, w_qkv, bias_qkv, seq_len, rows)
    output, tu, td, to, g_o, g_z, d_up, shared_terms = middle(
        info, o_t, w_out, tokens, cotangent, shared_vec, w_up, w_down, bias_up, rows
    )
    tq, own, other, d_bias = attend_back(info, g_o, q, k, v, probs, o_t, tokens, w_qkv, g_z)
    local_terms = jnp.concatenate(
        [d_bias.reshape(2, group_count, attn)[0], d_bias.reshape(2, group_count, attn)[1],
         d_up.reshape(group_count, -1)], 1
    )
    to = to.reshape(4, 16, 96, 128)
    tu = tu.reshape(4, 64, 96, 128)
    td = td.reshape(4, 64, 96, 128)
    if routed:
        owned, input_grad, local_sum, shared_grad = scatter_grads(
            nz, pack(tile_order, tq, to, tu, td), own, other, local_terms, shared_terms
        )
        owned = owned[:, :, :96]
    else:
        owned, input_grad, local_sum, shared_grad = plain_scatter(
            tile_order, tq, to, tu, td, own, other, local_terms, shared_terms
        )
    local_grad = lax.dynamic_slice_in_dim(local_sum, group_index, 1, 0)
    left_basis = basis_left[0]
    right_basis = basis_right[0]
    rotated = jnp.einsum("ski,skl->sil", left_basis, owned, precision=HIGH)
    rotated = jnp.einsum("sil,slj->sij", rotated, right_basis, precision=HIGH)
    tile_first, tile_second, direction = adam(rotated, first_moment[0], second_moment[0])
    turned = jnp.einsum("sik,skl->sil", left_basis, direction, precision=HIGH)
    turned = jnp.einsum("sil,sjl->sij", turned, right_basis, precision=HIGH)
    tile_weight = master[0] - RATE_TILES * (turned + DECAY * master[0])
    local_first_new, local_second_new, local_dir = adam(local_grad, local_first, local_second)
    shared_first_new, shared_second_new, shared_dir = adam(shared_grad, shared_first, shared_second)
    return (
        output,
        input_grad,
        owned[None],
        tile_first[None],
        tile_second[None],
        tile_weight[None],
        local_grad,
        local_first_new,
        local_second_new,
        local_vec - RATE_VECTORS * local_dir,
        shared_grad,
        shared_first_new,
        shared_second_new,
        shared_vec - RATE_VECTORS * shared_dir,
    )


def solution(mesh):
    placed = (
        P("dp", None),
        P("dp", None),
        P("dp"),
        P(),
        P("mp", "dp", None, None),
        P("mp", "dp", None, None),
        P("mp", "dp", None, None),
        P("mp", "dp", None, None),
        P("mp", "dp", None, None),
        P("mp", None),
        P("mp", None),
        P("mp", None),
        P(),
        P(),
        P(),
    )
    return jax.shard_map(
        shards,
        mesh=mesh,
        in_specs=placed,
        out_specs=(
            P(("dp", "mp"), None),
            P(("dp", "mp"), None),
            P("mp", "dp", None, None),
            P("mp", "dp", None, None),
            P("mp", "dp", None, None),
            P("mp", "dp", None, None),
            P("mp", None),
            P("mp", None),
            P("mp", None),
            P("mp", None),
            P(),
            P(),
            P(),
            P(),
        ),
        check_vma=False,
    )
```

time: 774 us -> 290 us (0.37)
  waiting for transfers between devices: 386 us -> 0 us
  Pallas kernels: 0 us -> 256 us
  matrix products: 127 us -> 10.3 us
  local copies, waits for them, and re-layouts: 100 us -> 12.7 us
  other arithmetic: 87.7 us -> 7.95 us
  blocking collectives: 43.9 us -> 0 us
  between operations: 15 us -> 0.94 us
    pallas_call x0 -> x6, Pallas kernels: none -> 256 us  [the longest x1 82.7 us: gather_weights(): pl.pallas_call(functools.partial(gather_kernel, nz), out_shape=[jax.Shape...]
    psum x4 -> x0, waiting for transfers between devices: 188 us -> none  [the longest x1 68.5 us: shards(): ffn_out = lax.psum(part_ffn.astype(jnp.bfloat16), 'mp').astype(jnp.float32)]
    reduce_scatter x1 -> x0, waiting for transfers between devices: 120 us -> none  [shards(): lax.psum_scatter(natural_grads[tile_order], 'dp', scatter_dimension=0, ti...]
    dot_general x26 -> x0, matrix products: 117 us -> none  [the longest x2 17 us: attend_back(): jnp.einsum('qhd,khd->hqk', block[:, 0], block[:, 1], preferred_element_ty...]
    all_gather x1 -> x0, waiting for transfers between devices: 78.4 us -> none  [shards(): gathered = lax.all_gather(master[0].astype(bf16), 'dp', axis=0, tiled=True)]
    reduce_sum x13 -> x1, other arithmetic: 45.6 us -> 0.79 us  [slot_sources(): jnp.sum(jnp.where(hit, jnp.arange(count, dtype=jnp.int32)[None, :], 0), 1)]
    psum x1 -> x0, blocking collectives: 43.9 us -> none  [shards(): spread_sum, shared_grad = lax.psum((spread, shared_terms), ('dp', 'mp'))]
    reshape x17 -> x3, local copies, waits for them, and re-layouts: 43.2 us -> 0.18 us  [the longest x1 0.08 us: shards(): bias_q = vectors[:, :attn].reshape(1, width)]
  transfers between devices with their start and end apart: 6 -> 0, of which waited for: 6 -> 0; matrix products, arithmetic and copies ran while one was open for 12% -> 0% of each run, Pallas kernels for 0% -> 0%
where the time goes in v1:
time: 290 us; the launch traced here: 288 us
  Pallas kernels  256 us (88%)
  local copies, waits for them, and re-layouts  12.7 us (4%)
  matrix products  10.3 us (4%)
  other arithmetic  7.95 us (3%)
    pallas_call x1, Pallas kernels, gather_weights(): pl.pallas_call(functools.partial(gather_kernel, nz), out_shape=[jax.Shape...  82.7 us
    pallas_call x1, Pallas kernels, scatter_grads(): pl.pallas_call(functools.partial(scatter_kernel, nz), out_shape=[jax.Shap...  71.4 us
    pallas_call x1, Pallas kernels, middle(): pl.pallas_call(middle_kernel, grid_spec=pltpu.PrefetchScalarGridSpec(num_...  38.3 us
    pallas_call x1, Pallas kernels, attend_back(): pl.pallas_call(attend_back_kernel, grid_spec=pltpu.PrefetchScalarGridSpec...  24.9 us
    pallas_call x1, Pallas kernels, pack(): pl.pallas_call(pack_kernel, grid_spec=pltpu.PrefetchScalarGridSpec(num_sc...  19.9 us
    pallas_call x1, Pallas kernels, attend(): pl.pallas_call(attend_kernel, grid_spec=pltpu.PrefetchScalarGridSpec(num_...  19.3 us
    unnamed x43, local copies, waits for them, and re-layouts  8.93 us

profile of v1, /device:TPU:16, one launch (start us, length us, event | category | flops | bytes accessed | tf_op | source)
XLA Modules:
  0.0 288.3 jit_solution(11900669692984156525)
XLA Ops:
  0.7 1.3 dynamic_slice.7
  2.0 1.2 pad_add_fusion.info_ref
  3.3 0.8 select_reduce_fusion
  4.7 82.7 %gather_weights.1 = (bf16[768,2304]{1,0:T(8,128)(2,1)}, bf16[768,768]{1,0:T(8,128)(2,1)}, bf16[768,3072]{1,0:T(8,128)(2,1)}, bf16[3072,768]{1,0:T(8,128)(2,1)}, f32[4,1,1152]{2,1,0:T(1,128)}) custom-call(s32[192]{0:T(256)} %fusion.25.src_ref, f32[24,96,96]{2,1,0:T(8,128)} %bitcast.52, f32[1,1152]{1,0:T(1,128)} %local_ref.1), custom_call_target="tpu_custom_call" | custom-call | tf_op jit(solution)/shard_map/gather_weights/pallas_call | solution.py:300
  87.4 0.7 copy.32
  88.9 19.3 %attend.1 = (bf16[512,768]{1,0:T(8,128)(2,1)}, bf16[1024,768]{1,0:T(8,128)(2,1)}, bf16[1024,768]{1,0:T(8,128)(2,1)}, bf16[6,2,512,512]{3,2,1,0:T(8,128)(2,1)}, bf16[768,512]{1,0:T(8,128)(2,1)}) custom-call(s32[4]{0:T(128)} %pad_add_fusion.info_ref, bf16[2048,768]{1,0:T(8,128)(2,1)} %x_ref.5, bf16[768,2304]{1,0:T(8,128)(2,1)} %get-tuple-element.40.w_ref, ...), custom_call_target="tpu_custom_call" | custom-call | tf_op jit(solution)/shard_map/attend/pallas_call | solution.py:417
  108.2 0.6 copy.30
  108.8 38.3 %middle.1 = (bf16[512,768]{1,0:T(8,128)(2,1)}, bf16[4,8,2,4,96,128]{5,4,3,2,1,0:T(8,128)(2,1)}, bf16[4,2,32,96,128]{4,3,2,1,0:T(8,128)(2,1)}, bf16[8,8,96,128]{3...) custom-call(s32[4]{0:T(128)} %pad_add_fusion.info_ref, ...), custom_call_target="tpu_custom_call" | custom-call | tf_op jit(solution)/shard_map/middle/pallas_call | solution.py:584
  147.2 24.9 %attend_back.1 = (bf16[4,48,96,128]{3,2,1,0:T(8,128)(2,1)}, f32[512,768]{1,0:T(8,128)}, bf16[512,768]{1,0:T(8,128)(2,1)}, f32[2,768]{1,0:T(2,128)}) custom-call(s32[4]{0:T(128)} %pad_add_fusion.info_ref, bf16[512,768]{1,0:T(8,128)(2,1)} %get-tuple-element.47.go_ref, bf16[512,768]{1,0:T(8,128)(2,1)} %get-tuple-element.48.q_ref, ...), custom_call_target="tpu_custom_call" | custom-call | tf_op jit(solution)/shard_map/attend_back/pallas_call | solution.py:704
  172.1 0.8 slice_reduce_fusion
  173.5 0.7 reduce.7
  174.2 0.7 concatenate.7.local_ref
  174.9 2.8 copy-done.1
  177.7 2.3 copy-done.2
  180.0 19.9 %pack.1.w_ref = bf16[4,8,18,96,128]{4,3,2,1,0:T(8,128)(2,1)} custom-call(s32[192]{0:T(256)S(1)} %copy-done.4, bf16[4,48,96,128]{3,2,1,0:T(8,128)(2,1)S(1)} %copy-done.2, bf16[4,16,96,128]{3,2,1,0:T(8,128)(2,1)S(1)} %bitcast.50, bf16[4,64,96,128]{3,2,1,0:T(8,128)(2,1)S(1)} %bitcast.49, bf16[4,64,96,128]{3,2,1,0:T(8,128)(2,1)} %bitcast.51), custom_call_target="tpu_custom_call" | custom-call | tf_op jit(solution)/shard_map/pack/pallas_call | solution.py:778
  200.0 71.4 %scatter_grads.1 = (f32[24,96,128]{2,1,0:T(8,128)}, f32[512,768]{1,0:T(8,128)}, f32[4,1152]{1,0:T(4,128)}, f32[6,768]{1,0:T(8,128)}) custom-call(bf16[4,8,18,96,128]{4,3,2,1,0:T(8,128)(2,1)} %pack.1.w_ref, f32[512,768]{1,0:T(8,128)} %get-tuple-element.57.own_ref, bf16[512,768]{1,0:T(8,128)(2,1)} %get-tuple-element.58.other_ref, ...), custom_call_target="tpu_custom_call" | custom-call | tf_op jit(solution)/shard_map/scatter_grads/pallas_call | solution.py:996
  271.4 3.4 %fusion.9 = f32[24,96,96]{1,2,0:T(8,128)S(1)} fusion(f32[1,24,96,96]{3,2,1,0:T(8,128)S(1)} %copy-done, f32[24,96,128]{2,1,0:T(8,128)} %get-tuple-element.63), kind=kOutput, calls=%fused_computation.12 | convolution fusion | flops 254803968 | bytes 2949120 | tf_op jit(solution)/shard_map/ski,skl->sil/dot_general | solution.py:1149
  274.9 1.3 fusion.5
  276.8 2.0 fusion.21
  278.9 2.1 fusion.7
  281.1 3.5 %fusion.2 = f32[1,24,96,96]{3,2,1,0:T(8,128)} fusion(f32[24,96,96]{1,2,0:T(8,128)S(1)} %fusion.7, f32[1,24,96,96]{3,2,1,0:T(8,128)S(1)} %copy-done.5, f32[1,24,96,96]{3,2,1,0:T(8,128)S(1)} %copy-done.7), kind=kOutput, calls=%fused_computation.5 | convolution fusion | flops 255688704 | bytes 3538944 | tf_op jit(solution)/shard_map/sil,sjl->sij/dot_general | solution.py:1153
  284.6 0.6 multiply_subtract_fusion
  285.2 1.4 multiply_subtract_fusion.1
  286.6 1.1 copy.35
  (49 shorter events, 3.5 us)
Async XLA Ops:
  0.6 270.8 %copy-start = (f32[1,24,96,96]{3,2,1,0:T(8,128)S(1)}, f32[1,24,96,96]{3,2,1,0:T(8,128)}, u32[]{:S(2)}) copy-start(f32[1,24,96,96]{3,2,1,0:T(8,128)} %param.22) | copy-start | bytes 2654212
  147.2 26.3 %copy-start.16 = (f32[1,3072]{1,0:T(1,128)S(1)}, f32[1,3072]{1,0:T(1,128)}, u32[]{:S(2)}) copy-start(f32[1,3072]{1,0:T(1,128)} %get-tuple-element.60) | copy-start | bytes 36868
  147.2 27.7 %copy-start.3 = (bf16[8,8,96,128]{3,2,1,0:T(8,128)(2,1)S(1)}, bf16[8,8,96,128]{3,2,1,0:T(8,128)(2,1)}, u32[]{:S(2)}) copy-start(bf16[8,8,96,128]{3,2,1,0:T(8,128)(2,1)} %get-tuple-element.54) | copy-start | bytes 4718596
  147.2 27.7 %copy-start.4 = (s32[192]{0:T(256)S(1)}, s32[192]{0:T(256)}, u32[]{:S(2)}) copy-start(s32[192]{0:T(256)} %order_ref.1) | copy-start | bytes 2308
  174.9 2.8 copy-start.1
  177.7 2.3 copy-start.2
  271.4 3.4 %copy-start.5 = (f32[1,24,96,96]{3,2,1,0:T(8,128)S(1)}, f32[1,24,96,96]{3,2,1,0:T(8,128)}, u32[]{:S(2)}) copy-start(f32[1,24,96,96]{3,2,1,0:T(8,128)} %param.23) | copy-start | bytes 2654212
  274.9 1.4 copy-start.6
  274.9 1.6 copy-start.9
  274.9 2.0 copy-start.10
  278.9 2.1 copy-start.7
  281.0 3.6 %copy-start.11 = (f32[6,768]{1,0:T(8,128)S(1)}, f32[6,768]{1,0:T(8,128)}, u32[]{:S(2)}) copy-start(f32[6,768]{1,0:T(8,128)} %sv_ref.1) | copy-start | bytes 55300
  281.0 3.6 %copy-start.12 = (f32[6,768]{1,0:T(8,128)S(1)}, f32[6,768]{1,0:T(8,128)}, u32[]{:S(2)}) copy-start(f32[6,768]{1,0:T(8,128)} %get-tuple-element.104) | copy-start | bytes 55300
  281.0 3.6 %copy-start.13 = (f32[6,768]{1,0:T(8,128)S(1)}, f32[6,768]{1,0:T(8,128)}, u32[]{:S(2)}) copy-start(f32[6,768]{1,0:T(8,128)} %param.29) | copy-start | bytes 55300
  281.0 3.6 %copy-start.14 = (f32[6,768]{1,0:T(8,128)S(1)}, f32[6,768]{1,0:T(8,128)}, u32[]{:S(2)}) copy-start(f32[6,768]{1,0:T(8,128)} %param.28) | copy-start | bytes 55300
  281.0 4.2 %copy-start.15 = (f32[1,1152]{1,0:T(1,128)S(1)}, f32[1,1152]{1,0:T(1,128)}, u32[]{:S(2)}) copy-start(f32[1,1152]{1,0:T(1,128)} %local_ref.1) | copy-start | bytes 13828
  281.0 4.2 %copy-start.17 = (f32[1,1152]{1,0:T(1,128)S(1)}, f32[1,1152]{1,0:T(1,128)}, u32[]{:S(2)}) copy-start(f32[1,1152]{1,0:T(1,128)} %param.26) | copy-start | bytes 13828
  281.1 4.2 %copy-start.18 = (f32[1,1152]{1,0:T(1,128)S(1)}, f32[1,1152]{1,0:T(1,128)}, u32[]{:S(2)}) copy-start(f32[1,1152]{1,0:T(1,128)} %param.25) | copy-start | bytes 13828
  281.1 5.5 %copy-start.8 = (f32[512,768]{1,0:T(8,128)S(1)}, f32[512,768]{1,0:T(8,128)}, u32[]{:S(2)}) copy-start(f32[512,768]{1,0:T(8,128)} %get-tuple-element.95) | copy-start | bytes 4718596

commit v2 on v1

v2 whole, which is shorter than its diff:
```python
import functools
import jax
import jax.numpy as jnp
from jax import lax
from jax.experimental import pallas as pl
from jax.experimental.pallas import tpu as pltpu
from jax.sharding import PartitionSpec as P

MESH = pl.DeviceIdType.MESH
f32 = jnp.float32
bf16 = jnp.bfloat16


def lanes_of(shape):
    return lax.broadcasted_iota(jnp.int32, shape, len(shape) - 1)


def turn(v, amount):
    return pltpu.roll(v, amount, v.ndim - 1)


def free_of(j):
    return (3 * j + 3) % 4


def part_of(group, number):
    return jnp.where(number < 48, 2 * group + number % 2, number) % 4


def groups_of(shape):
    return lanes_of(shape) // 32


def to_wire(tile, free):
    rest = tile[72:96]
    side = jnp.concatenate([turn(rest, 96), turn(rest, 64), turn(rest, 32)], 0)
    return jnp.where(groups_of(side.shape) == free, side, tile[:72])


def rest_of(wire, free):
    group = groups_of((24, 128))
    first, second, third = turn(wire[:24], 32), turn(wire[24:48], 64), turn(wire[48:72], 96)
    return jnp.where(
        group == (free + 1) % 4, first, jnp.where(group == (free + 2) % 4, second, third)
    )


def turned(tile, j, sign):
    out = tile
    for k in range(1, 4):
        out = jnp.where(j == k, turn(tile, sign * 96 * k % 128), out)
    return out


def join_four(tiles):
    lane = lanes_of(tiles[0].shape)
    a, b, c, d = tiles
    return [jnp.where(lane < 96, a, b), jnp.where(lane < 64, b, c), jnp.where(lane < 32, c, d)]


def split_four(pieces):
    lane = lanes_of(pieces[0].shape)
    a, b, c = pieces
    return [a, jnp.where(lane < 64, b, a), jnp.where(lane < 32, c, b), c]


def place():
    d, m = lax.axis_index("dp"), lax.axis_index("mp")
    return d // 2, d % 2, m // 2, m % 2


class Net:
    def __init__(self, nz):
        self.nz = nz
        self.z, self.x, self.y, self.c = place()
        self.d = self.z * 2 + self.x
        self.m = self.y * 2 + self.c
        self.xn = (self.z * 2 + 1 - self.x, self.m)
        self.yn = (self.d, (1 - self.y) * 2 + self.c)
        self.cn = (self.d, self.y * 2 + 1 - self.c)
        self.up = (self.d + 2, self.m)
        self.dn = (self.d - 2, self.m)
        self.has_up = self.z < nz - 1
        self.has_dn = self.z > 0

    def enter(self):
        bar = pltpu.get_barrier_semaphore()
        others = [(lax.rem(self.z + k, self.nz) * 2 + self.x, self.m) for k in range(1, self.nz)]
        peers = [self.xn, self.yn, self.cn] + others
        for peer in peers:
            pl.semaphore_signal(bar, inc=1, device_id=peer, device_id_type=MESH)
        pl.semaphore_wait(bar, len(peers))


def send(src, dst, ss, rs, peer):
    return pltpu.make_async_remote_copy(
        src_ref=src, dst_ref=dst, send_sem=ss, recv_sem=rs, device_id=peer, device_id_type=MESH
    )


def tile_qkv(r, j):
    return (j % 8) // 2, r * 6 + (j // 8) * 2 + j % 2


def tile_out(r, j):
    return r // 2, 48 + (r % 2) * 8 + j


def tile_up(r, j):
    return j // 8, 64 + r * 8 + j % 8


def tile_down(r, j):
    return r // 8, 128 + (r % 8) * 8 + j


GRIDS = ((8, 24, tile_qkv), (8, 8, tile_out), (8, 32, tile_up), (32, 8, tile_down))


def gather_kernel(
    nz, order_ref, src_ref, master_ref, local_ref, o_qkv, o_out, o_up, o_down, o_local,
    G, H, LV, d_qkv, d_out, d_up, d_down,
    zs, zr, xs, xr, ys, yr, xds, xdr, yds, ydr, cs, cr, outs, lvs, lvr,
):
    net = Net(nz)
    z, x, y, c, m = net.z, net.x, net.y, net.c, net.m
    my = (1 - y) * 2 + c
    net.enter()
    full = 24
    half = 12
    LV[m] = local_ref[...]
    lv_y = send(LV.at[m], LV.at[m], lvs.at[0], lvr.at[0], net.yn)
    lv_c = send(LV.at[m], LV.at[m], lvs.at[1], lvr.at[1], net.cn)
    lv_d = send(LV.at[my], LV.at[my], lvs.at[2], lvr.at[2], net.cn)
    lv_y.start()
    lv_c.start()

    def slot(mo, zo, xo, lo=0, n=full):
        return G.at[mo, pl.ds((zo * 2 + xo) * full + lo, n)]

    def stage(i, _):
        tile = jnp.concatenate([master_ref[i], jnp.zeros((96, 32), f32)], axis=-1)
        j = part_of(m, order_ref[net.d * full + i])
        tile = turned(tile, j, 1)
        G[m, net.d * full + i] = to_wire(tile, free_of(j)).astype(bf16)
        H[m, net.d * full + i] = tile[72:96].astype(bf16)
        return 0

    lax.fori_loop(0, full, stage, 0)

    def unwrap(mo, zo, xo):
        base = (zo * 2 + xo) * full

        def body(i, _):
            for k in range(4):
                at = base + 4 * i + k
                free = free_of(part_of(mo, order_ref[at]))
                H[mo, at] = rest_of(G[mo, at].astype(f32), free).astype(bf16)
            return 0

        lax.fori_loop(0, full // 4, body, 0)

    def z_copy(zo, direction):
        s = slot(m, zo, x)
        peer = net.up if direction == 0 else net.dn
        return send(s, s, zs.at[zo, direction], zr.at[zo], peer)

    def c_copy(zo, kind):
        mo = (m, m, my, my)[kind]
        xo = (x, 1 - x, x, 1 - x)[kind]
        s = slot(mo, zo, xo)
        return send(s, s, cs.at[zo, kind], cr.at[zo, kind], net.cn)

    def c_arrival(zo, kind):
        mo = (m, m, my, my)[kind] + 1 - 2 * c
        xo = (x, 1 - x, x, 1 - x)[kind]
        s = slot(mo, zo, xo)
        return send(s, s, cs.at[zo, kind], cr.at[zo, kind], net.cn)

    def x_copy(zo, xo):
        s = slot(m, zo, xo)
        return send(s, s, xs.at[zo], xr.at[zo], net.xn)

    def y_copy(zo, mo):
        s = slot(mo, zo, x)
        return send(s, s, ys.at[zo], yr.at[zo], net.yn)

    def xd_copy(zo, xo):
        s = slot(my, zo, xo, 0, half)
        return send(s, s, xds.at[zo], xdr.at[zo], net.xn)

    def yd_copy(zo, mo):
        s = slot(mo, zo, 1 - x, half, half)
        return send(s, s, yds.at[zo], ydr.at[zo], net.yn)

    def fan(zo):
        x_copy(zo, x).start()
        y_copy(zo, m).start()
        c_copy(zo, 0).start()

    def diag(zo):
        x_copy(zo, 1 - x).wait_recv()
        yd_copy(zo, m).start()
        c_copy(zo, 1).start()
        y_copy(zo, my).wait_recv()
        xd_copy(zo, x).start()
        c_copy(zo, 2).start()

    def fin(zo):
        xd_copy(zo, 1 - x).wait_recv()
        yd_copy(zo, my).wait_recv()
        c_copy(zo, 3).start()

    def each(step, fn):
        if step == 0:
            fn(z, 0)
            return

        @pl.when(z >= step)
        def _():
            fn(z - step, 1)

        @pl.when(z + step < nz)
        def _():
            fn(z + step, -1)

    def arrive(zo, side):
        if isinstance(side, int) and side == 0:
            @pl.when(net.has_up)
            def _():
                z_copy(zo, 0).start()

            @pl.when(net.has_dn)
            def _():
                z_copy(zo, 1).start()
        elif side == 1:
            z_copy(zo, 0).wait_recv()

            @pl.when(net.has_up)
            def _():
                z_copy(zo, 0).start()
        else:
            z_copy(zo, 1).wait_recv()

            @pl.when(net.has_dn)
            def _():
                z_copy(zo, 1).start()
        fan(zo)

    def open_some(zo, side):
        if not (isinstance(side, int) and side == 0):
            unwrap(m, zo, x)
        unwrap(m, zo, 1 - x)
        unwrap(my, zo, x)
        for kind in range(3):
            c_arrival(zo, kind).wait_recv()
            mo, xo = ((m, x), (m, 1 - x), (my, x))[kind]
            unwrap(mo + 1 - 2 * c, zo, xo)

    def open_last(zo, side):
        unwrap(my, zo, 1 - x)
        c_arrival(zo, 3).wait_recv()
        unwrap(my + 1 - 2 * c, zo, 1 - x)

    for step in range(nz + 2):
        if step < nz:
            each(step, arrive)
        if 0 <= step - 1 < nz:
            each(step - 1, lambda zo, side: diag(zo))
        if 0 <= step - 2:
            each(step - 2, lambda zo, side: fin(zo))
        if 0 <= step - 1 < nz:
            each(step - 1, open_some)
        if 0 <= step - 2:
            each(step - 2, open_last)
    send(LV.at[my], LV.at[my], lvs.at[0], lvr.at[0], net.yn).wait_recv()
    lv_d.start()
    mc = m + 1 - 2 * c
    send(LV.at[mc], LV.at[mc], lvs.at[1], lvr.at[1], net.cn).wait_recv()
    mc = my + 1 - 2 * c
    send(LV.at[mc], LV.at[mc], lvs.at[2], lvr.at[2], net.cn).wait_recv()
    o_local[...] = LV[...]
    lv_y.wait_send()
    lv_c.wait_send()
    lv_d.wait_send()
    def sent(zo, side):
        x_copy(zo, x).wait_send()
        y_copy(zo, m).wait_send()
        yd_copy(zo, m).wait_send()
        xd_copy(zo, x).wait_send()
        for kind in range(4):
            c_copy(zo, kind).wait_send()
        if side == 0 or side == 1:
            @pl.when(net.has_up)
            def _():
                z_copy(zo, 0).wait_send()
        if side == 0 or side == -1:
            @pl.when(net.has_dn)
            def _():
                z_copy(zo, 1).wait_send()

    for step in range(nz):
        each(step, sent)

    copies = []
    for i, ((rows, cols, where), dense, out) in enumerate(
        zip(GRIDS, (d_qkv, d_out, d_up, d_down), (o_qkv, o_out, o_up, o_down))
    ):
        def fill(r, _):
            for g in range(cols // 4):
                tiles = []
                for t in range(4):
                    p, n = where(r, 4 * g + t)
                    at = src_ref[n]
                    tiles.append(
                        jnp.concatenate([G[p, at].astype(f32), H[p, at].astype(f32)], 0)
                    )
                for k, piece in enumerate(join_four(tiles)):
                    dense[pl.ds(pl.multiple_of(r * 96, 96), 96), pl.ds(384 * g + 128 * k, 128)] = (
                        piece.astype(bf16)
                    )
            return 0

        lax.fori_loop(0, rows, fill, 0)
        copy = pltpu.make_async_copy(dense, out, outs.at[i])
        copy.start()
        copies.append(copy)
    for copy in copies:
        copy.wait()


def gather_weights(nz, order, src, master, local):
    dma = pltpu.SemaphoreType.DMA
    shapes = [(r * 96, c * 96) for r, c, _ in GRIDS]
    return pl.pallas_call(
        functools.partial(gather_kernel, nz),
        out_shape=[jax.ShapeDtypeStruct(s, bf16) for s in shapes]
        + [jax.ShapeDtypeStruct((4, *local.shape), f32)],
        in_specs=[pl.BlockSpec(memory_space=pltpu.SMEM)] * 2
        + [pl.BlockSpec(memory_space=pltpu.VMEM)] * 2,
        out_specs=[pl.BlockSpec(memory_space=pl.ANY)] * 4 + [pl.BlockSpec(memory_space=pltpu.VMEM)],
        scratch_shapes=[pltpu.VMEM((4, 2 * nz * 24, 72, 128), bf16), pltpu.VMEM((4, 2 * nz * 24, 24, 128), bf16),
            pltpu.VMEM((4, *local.shape), f32)]
        + [pltpu.VMEM(s, bf16) for s in shapes]
        + [dma((nz, 2)), dma((nz,))]
        + [dma((nz,))] * 8
        + [dma((nz, 4)), dma((nz, 4)), dma((4,)), dma((3,)), dma((3,))],
        compiler_params=pltpu.CompilerParams(
            collective_id=0, has_side_effects=True, vmem_limit_bytes=56 << 20
        ),
        name="gather_weights",
    )(order, src, master, local)


def slot_of_tile(tile_order):
    count = tile_order.shape[0]
    slots = jnp.arange(count, dtype=jnp.int32)
    return jnp.sum(jnp.where(tile_order[None, :] == slots[:, None], slots[None, :], 0), 1)


NEG_BIG = -1e30
NORM_EPS = 1e-05
ROOT_HALF = 0.7071067811865476
PHI_SCALE = 0.3989422804014327


def nt(a, b):
    return lax.dot_general(a, b, (((1,), (1,)), ((), ())), preferred_element_type=f32)


def tn(a, b):
    return lax.dot_general(a, b, (((0,), (0,)), ((), ())), preferred_element_type=f32)


def nn(a, b):
    return jnp.dot(a, b, preferred_element_type=f32)


def standard(values):
    centre = values - jnp.mean(values, -1, keepdims=True)
    scale = lax.rsqrt(jnp.mean(centre * centre, -1, keepdims=True) + NORM_EPS)
    return centre * scale, scale


def standard_back(grad, normed, scale, gain):
    inner = grad * gain
    return scale * (
        inner - jnp.mean(inner, -1, keepdims=True) - normed * jnp.mean(inner * normed, -1, keepdims=True)
    )


def col_sum(values):
    return jnp.sum(values, 0, keepdims=True)


def layer_kernel(
    tokens_ref, cot_ref, lengths_ref, vec_ref, sv_ref, wq_ref, wo_ref, wu_ref, wd_ref,
    out_ref, tq_ref, to_ref, tu_ref, td_ref, own_ref, other_ref, dl_ref, ds_ref,
    x, cot, wqkv, wout, wup, wdown, bias, q, k, v, probs, o_t, hid, low, low_t, n_one, r_one, acc,
    act, slope, g_low, g_o, dq, dk, dv, out, other, su, sd, so, sq, loads, stores, su_sem, sd_sem, sq_sem,
):
    rows, width = q.shape
    seq_len = k.shape[0]
    chunks, _, cut = act.shape
    tiles = width // 96
    pairs = width // 128
    piece = 128
    zero = jnp.zeros((), bf16)
    member = lax.axis_index("mp")
    share = seq_len // rows
    seq, part = member // share, member % share
    length = lengths_ref[seq]
    bound = 64 * ((length + 127) // 128)
    start_b = pl.multiple_of(bound, 64)
    here = pl.ds(pl.multiple_of(part * rows, rows), rows)
    there = pl.ds(pl.multiple_of((1 - part) * rows, rows), rows)

    def load(src, dst, i):
        copy = pltpu.make_async_copy(src, dst, loads.at[i])
        copy.start()
        return copy

    get_x = load(tokens_ref.at[pl.ds(pl.multiple_of(seq * seq_len, seq_len), seq_len)], x, 0)
    get_q = load(wq_ref, wqkv, 1)
    get_o = load(wo_ref, wout, 2)
    get_u = load(wu_ref, wup, 3)
    get_d = load(wd_ref, wdown, 4)
    get_c = load(cot_ref.at[pl.ds(pl.multiple_of(member * rows, rows), rows)], cot, 5)

    groups = vec_ref.shape[0]
    third = width // groups
    bias[:, :width] = jnp.concatenate([vec_ref[p][:, :third] for p in range(groups)], 1)
    bias[:, width:] = jnp.concatenate([vec_ref[p][:, third : 2 * third] for p in range(groups)], 1)

    get_x.wait()
    get_q.wait()
    for lo in range(0, width, 256):
        got = nn(x[here, :], wqkv[:, lo : lo + 256]) + bias[:, lo : lo + 256]
        q[:, lo : lo + 256] = got.astype(bf16) * jnp.asarray(0.125, bf16)

    def project(r, _):
        at = pl.ds(pl.multiple_of(r * rows, rows), rows)
        for lo in range(0, width, 256):
            k[at, lo : lo + 256] = nn(x[at, :], wqkv[:, width + lo : width + lo + 256]).astype(bf16)
            got = nn(x[at, :], wqkv[:, 2 * width + lo : 2 * width + lo + 256])
            v[at, lo : lo + 256] = (got + bias[:, width + lo : width + lo + 256]).astype(bf16)
        return 0

    lax.fori_loop(0, share, project, 0)

    def picks(shape, rows_at):
        row = lax.broadcasted_iota(jnp.int32, shape, rows_at) + part * rows
        lane = lax.broadcasted_iota(jnp.int32, shape, 1 - rows_at)
        return (row < bound) == (lane < 64)

    windows = ((0, bound), (start_b, length - bound))

    def forward(pair, _):
        cols = pl.ds(pl.multiple_of(pair * 128, 128), 128)
        queries = q[:, cols]
        pick = picks((rows, 128), 0)
        outs = []
        for w, (start, limit) in enumerate(windows):
            these = jnp.where(pick, queries, zero) if w == 0 else jnp.where(pick, zero, queries)
            scores = nt(k[pl.ds(start, rows), cols], these)
            inside = lax.broadcasted_iota(jnp.int32, scores.shape, 0) < limit
            scores = jnp.where(inside, scores, NEG_BIG)
            weight = jnp.exp(scores - jnp.max(scores, 0, keepdims=True))
            low_probs = (weight * (1.0 / jnp.sum(weight, 0, keepdims=True))).astype(bf16)
            probs[2 * pair + w] = low_probs
            outs.append(tn(v[pl.ds(start, rows), cols], low_probs))
        o_t[cols, :] = jnp.where(picks((128, rows), 1), outs[0], outs[1]).astype(bf16)
        return 0

    lax.fori_loop(0, pairs, forward, 0)

    def by_rows(fn):
        def body(r, _):
            fn(pl.ds(pl.multiple_of(r * piece, piece), piece), r)
            return 0

        lax.fori_loop(0, rows // piece, body, 0)

    get_o.wait()
    acc[...] = tn(o_t[...], wout[...])

    def norm_one(at, r):
        mine = pl.ds(pl.multiple_of(part * rows + r * piece, piece), piece)
        z_one = x[mine, :].astype(f32) + acc[at, :] + sv_ref[0:1, :]
        normed, scale = standard(z_one)
        hidden = normed * sv_ref[2:3, :] + sv_ref[3:4, :]
        n_one[at, :] = normed
        r_one[at, :] = jnp.broadcast_to(scale, (piece, 128))
        hid[at, :] = hidden
        low[at, :] = hidden.astype(bf16)
        acc[at, :] = jnp.zeros((piece, width), f32)

    by_rows(norm_one)
    low_t[...] = low[...].T
    get_u.wait()
    get_d.wait()

    def feed(i, _):
        at = pl.ds(pl.multiple_of(i * cut, cut), cut)
        half = chunks // groups
        shift = pl.multiple_of(2 * third + (i % half) * cut, 128)
        pre = nn(low[...], wup[:, at]) + vec_ref[i // half, :, pl.ds(shift, cut)]
        phi = 0.5 * (1.0 + lax.erf(pre * ROOT_HALF))
        density = jnp.exp(-0.5 * pre * pre) * PHI_SCALE
        active = (pre * phi).astype(bf16)
        act[i] = active
        slope[i] = (phi + pre * density).astype(bf16)
        acc[...] += nn(active, wdown[at, :])
        return 0

    lax.fori_loop(0, chunks, feed, 0)
    get_c.wait()
    ds_ref[...] = jnp.zeros_like(ds_ref)

    def norm_two(at, r):
        z_two = hid[at, :] + acc[at, :] + sv_ref[1:2, :]
        normed, scale = standard(z_two)
        row = lax.broadcasted_iota(jnp.int32, (piece, 1), 0) + part * rows + r * piece
        valid = (row < length).astype(f32)
        out[at, :] = ((normed * sv_ref[4:5, :] + sv_ref[5:6, :]) * valid).astype(bf16)
        grad = cot[at, :].astype(f32) * valid
        back = standard_back(grad, normed, scale, sv_ref[4:5, :])
        ds_ref[4:5, :] += col_sum(grad * normed)
        ds_ref[5:6, :] += col_sum(grad)
        ds_ref[1:2, :] += col_sum(back)
        g_low[at, :] = back.astype(bf16)
        acc[at, :] = back

    by_rows(norm_two)
    put_out = pltpu.make_async_copy(out, out_ref, stores.at[0])
    put_out.start()

    def put_u(i):
        half = chunks // groups
        return pltpu.make_async_copy(su.at[i % 2], tu_ref.at[i // half, :, i % half], su_sem.at[i % 2])

    def put_d(i):
        half = chunks // groups
        return pltpu.make_async_copy(sd.at[i % 2], td_ref.at[i // half, i % half], sd_sem.at[i % 2])

    def cuts(full, r):
        return split_four(
            [full[96 * r : 96 * r + 96, 128 * n : 128 * n + 128].astype(bf16) for n in range(3)]
        )

    def feed_back(i, _):
        at = pl.ds(pl.multiple_of(i * cut, cut), cut)

        @pl.when(i >= 2)
        def _():
            put_u(i - 2).wait()
            put_d(i - 2).wait()

        half = chunks // groups
        shift = pl.multiple_of(2 * third + (i % half) * cut, 128)
        grad_low = (nt(g_low[...], wdown[at, :]) * slope[i].astype(f32)).astype(bf16)
        dl_ref[i // half, :, pl.ds(shift, cut)] = col_sum(grad_low.astype(f32))
        acc[...] += nt(grad_low, wup[:, at])
        for g in range(width // 384):
            down = tn(act[i], g_low[:, 384 * g : 384 * g + 384])
            for r in range(4):
                for t, tile in enumerate(cuts(down, r)):
                    sd[i % 2, r * tiles + 4 * g + t] = tile
        up = nn(low_t[...], grad_low)
        for r in range(tiles):
            for t, tile in enumerate(cuts(up, r)):
                su[i % 2, r, t] = tile
        put_u(i).start()
        put_d(i).start()
        return 0

    lax.fori_loop(0, chunks, feed_back, 0)

    def norm_back(at, r):
        grad = acc[at, :]
        normed = n_one[at, :]
        back = standard_back(grad, normed, r_one[at, 0:1], sv_ref[2:3, :])
        ds_ref[2:3, :] += col_sum(grad * normed)
        ds_ref[3:4, :] += col_sum(grad)
        ds_ref[0:1, :] += col_sum(back)
        acc[at, :] = back
        g_low[at, :] = back.astype(bf16)

    by_rows(norm_back)
    g_o[...] = nt(g_low[...], wout[...]).astype(bf16)
    for g in range(width // 384):
        outer = nn(o_t[...], g_low[:, 384 * g : 384 * g + 384])
        for r in range(tiles):
            for t, tile in enumerate(cuts(outer, r)):
                so[r, 4 * g + t] = tile
    put_o = pltpu.make_async_copy(so, to_ref, stores.at[1])
    put_o.start()
    dk[...] = jnp.zeros_like(dk)
    dv[...] = jnp.zeros_like(dv)

    def backward(pair, _):
        cols = pl.ds(pl.multiple_of(pair * 128, 128), 128)
        pick, pick_t = picks((rows, 128), 0), picks((128, rows), 1)
        queries, grads = q[:, cols], g_o[:, cols]
        grads_t = grads.astype(f32).T
        inner = grads_t * o_t[cols, :].astype(f32)
        outs = []
        for w, (start, _) in enumerate(windows):
            at = pl.ds(start, rows)
            mine = (lambda a: jnp.where(pick, a, zero)) if w == 0 else (lambda a: jnp.where(pick, zero, a))
            mine_t = (lambda a: jnp.where(pick_t, a, 0.0)) if w == 0 else (lambda a: jnp.where(pick_t, 0.0, a))
            dot_sum = jnp.sum(mine_t(inner), 0, keepdims=True)
            grad_probs = nn(v[at, cols], mine_t(grads_t).astype(bf16))
            these = probs[2 * pair + w]
            grad_scores = (these.astype(f32) * (grad_probs - dot_sum)).astype(bf16)
            dv[at, cols] = nn(these, mine(grads)).astype(bf16)
            dk[at, cols] = nn(grad_scores, mine(queries)).astype(bf16)
            outs.append(tn(k[at, cols], grad_scores))
        dq[:, cols] = (jnp.where(pick_t, outs[0], outs[1]) * 0.125).T.astype(bf16)
        return 0

    lax.fori_loop(0, pairs, backward, 0)

    other[...] = (
        nt(dk[there, :], wqkv[:, width : 2 * width]) + nt(dv[there, :], wqkv[:, 2 * width :])
    ).astype(bf16)
    put_x = pltpu.make_async_copy(other, other_ref, stores.at[2])
    put_x.start()
    hid[...] = (
        acc[...]
        + nt(dq[...], wqkv[:, :width])
        + nt(dk[here, :], wqkv[:, width : 2 * width])
        + nt(dv[here, :], wqkv[:, 2 * width :])
    )
    put_own = pltpu.make_async_copy(hid, own_ref, stores.at[3])
    put_own.start()
    sum_q = col_sum(dq[...].astype(f32))
    sum_v = col_sum(dv[...].astype(f32))
    for p in range(groups):
        dl_ref[p, :, :third] = sum_q[:, third * p : third * p + third]
        dl_ref[p, :, third : 2 * third] = sum_v[:, third * p : third * p + third]

    everyone = pl.ds(0, seq_len)
    puts = []
    for index, (grad, source) in enumerate(((dq, here), (dk, everyone), (dv, everyone))):
        for g in range(width // 384):
            outer = tn(x[source, :], grad[:, 384 * g : 384 * g + 384])
            count = index * (width // 384) + g
            if count >= 2:
                puts[count - 2].wait()
            for r in range(tiles):
                for t, tile in enumerate(cuts(outer, r)):
                    sq[count % 2, t // 2, r, t % 2] = tile
            put = pltpu.make_async_copy(
                sq.at[count % 2], tq_ref.at[pl.ds(2 * g, 2), :, index], sq_sem.at[count % 2]
            )
            put.start()
            puts.append(put)
    for i in (chunks - 2, chunks - 1):
        put_u(i).wait()
        put_d(i).wait()
    for put in (put_out, put_o, put_x, put_own, puts[-2], puts[-1]):
        put.wait()


def layer(tokens, cotangent, lengths, vectors, shared, w_qkv, w_out, w_up, w_down, rows):
    width = w_out.shape[0]
    hidden = w_up.shape[1]
    seq_len = tokens.shape[0] // lengths.shape[0]
    cut = 384
    chunks = hidden // cut
    groups = vectors.shape[0]
    half = chunks // groups
    tiles = width // 96
    anywhere = pl.BlockSpec(memory_space=pl.ANY)
    vm = pl.BlockSpec(memory_space=pltpu.VMEM)
    smem = pl.BlockSpec(memory_space=pltpu.SMEM)
    out = jax.ShapeDtypeStruct
    V = pltpu.VMEM
    dma = pltpu.SemaphoreType.DMA
    tall, wide, long = (rows, width), (width, rows), (seq_len, width)
    return pl.pallas_call(
        layer_kernel,
        in_specs=[anywhere, anywhere, smem, vm, vm] + [anywhere] * 4,
        out_specs=[anywhere] * 7 + [vm, vm],
        out_shape=[
            out(tall, bf16),
            out((groups, tiles, 3, 2, 96, 128), bf16),
            out((tiles, tiles, 96, 128), bf16),
            out((groups, tiles, half, 4, 96, 128), bf16),
            out((groups, half, 4 * tiles, 96, 128), bf16),
            out(tall, f32),
            out(tall, bf16),
            out(vectors.shape, f32),
            out(shared.shape, f32),
        ],
        scratch_shapes=[
            V(long, bf16), V(tall, bf16), V(w_qkv.shape, bf16), V(w_out.shape, bf16), V(w_up.shape, bf16),
            V(w_down.shape, bf16), V((1, 2 * width), f32), V(tall, bf16), V(long, bf16), V(long, bf16),
            V((width // 64, rows, rows), bf16), V(wide, bf16), V(tall, f32), V(tall, bf16), V(wide, bf16),
            V(tall, f32), V((rows, 128), f32), V(tall, f32), V((chunks, rows, cut), bf16),
            V((chunks, rows, cut), bf16), V(tall, bf16), V(tall, bf16), V(tall, bf16), V(long, bf16),
            V(long, bf16), V(tall, bf16), V(tall, bf16), V((2, tiles, 4, 96, 128), bf16),
            V((2, 4 * tiles, 96, 128), bf16), V((tiles, tiles, 96, 128), bf16),
            V((2, 2, tiles, 2, 96, 128), bf16), dma((6,)), dma((4,)), dma((2,)), dma((2,)), dma((2,)),
        ],
        compiler_params=pltpu.CompilerParams(vmem_limit_bytes=60 << 20),
        name="layer",
    )(tokens, cotangent, lengths, vectors, shared, w_qkv, w_out, w_up, w_down)


def scatter_kernel(
    nz, order_ref, tq_ref, to_ref, tu_ref, td_ref, own_ref, other_ref, local_ref, shared_ref,
    tile_o, dx_o, local_o, shared_o,
    T, S, A, R, XD, YD, X, Y, Z, dx_in, la, lb, sa, sb,
    tsem, cs, cr, xds, xdr, yds, ydr, xs, xr, ys, yr, zs, zr, dxs, vs, vr,
):
    net = Net(nz)
    z, x, y, c, m, d = net.z, net.x, net.y, net.c, net.m, net.d
    my = (1 - y) * 2 + c
    far = (lax.rem(z + 2, nz) * 2 + x, m)
    near = ((z + 1 - 2 * (z % 2)) * 2 + x, m)
    full, half = 24, 12
    low, high = pl.ds(0, half), pl.ds(half, half)
    loads = []
    first = 0
    for i, src in enumerate((tq_ref, to_ref, tu_ref, td_ref)):
        copy = pltpu.make_async_copy(src, T.at[:, pl.ds(first, src.shape[1])], tsem.at[i])
        copy.start()
        loads.append(copy)
        first += src.shape[1]
    net.enter()
    kinds = ((m, x), (m, 1 - x), (my, x), (my, 1 - x))
    flip = 1 - 2 * c

    def c_copy(zo, kind):
        return send(S.at[zo, kind], R.at[zo, kind], cs.at[zo, kind], cr.at[zo, kind], net.cn)

    def fill(ref, zo, kind, shift):
        mo, xo = kinds[kind]
        base = (zo * 2 + xo) * full

        def body(i, _):
            for j in range(4):
                number = order_ref[base + 4 * i + j]
                tile = T[mo + shift, number].astype(f32)
                ref[zo, kind, 4 * i + j] = to_wire(
                    tile, free_of(part_of(mo + shift, number))
                ).astype(bf16)
            return 0

        lax.fori_loop(0, full // 4, body, 0)

    def xd_copy(zo):
        return send(A.at[zo, 3, low], XD.at[zo], xds.at[zo], xdr.at[zo], net.xn)

    def yd_copy(zo):
        return send(A.at[zo, 3, high], YD.at[zo], yds.at[zo], ydr.at[zo], net.yn)

    def x_copy(zo):
        return send(A.at[zo, 1], X.at[zo], xs.at[zo], xr.at[zo], net.xn)

    def y_copy(zo):
        return send(A.at[zo, 2], Y.at[zo], ys.at[zo], yr.at[zo], net.yn)

    def z_copy(zo, direction):
        return send(
            A.at[zo, 0], Z.at[zo, direction], zs.at[zo], zr.at[zo, direction],
            net.up if direction == 0 else net.dn,
        )

    dx_copy = send(other_ref, dx_in, dxs.at[0], dxs.at[1], net.cn)
    peers = (net.cn, net.xn, net.yn, near, far)

    def v_copies(k):
        return (
            send(la.at[k], lb.at[k], vs.at[k, 0], vr.at[k, 0], peers[k]),
            send(sa.at[k], sb.at[k], vs.at[k, 1], vr.at[k, 1], peers[k]),
        )

    def v_start(k):
        for copy in v_copies(k):
            copy.start()

    def v_finish(k):
        for copy in v_copies(k):
            copy.wait_recv()
        la[k + 1] = la[k] + lb[k]
        sa[k + 1] = sa[k] + sb[k]

    def add(zo, kind, other, lo=0, n=24):
        def body(i, _):
            A[zo, kind, lo + i] = (A[zo, kind, lo + i].astype(f32) + other(i)).astype(bf16)
            return 0

        lax.fori_loop(0, n, body, 0)

    def each(step, fn):
        if step == 0:
            fn(z, 0)
            return

        @pl.when(z >= step)
        def _():
            fn(z - step, 1)

        @pl.when(z + step < nz)
        def _():
            fn(z + step, -1)

    def begin(zo, side):
        for kind in (3, 1, 2, 0):
            fill(S, zo, kind, flip)
            c_copy(zo, kind).start()

    def phase_one(zo, side):
        for kind in (3, 1, 2, 0):
            fill(A, zo, kind, 0)
            c_copy(zo, kind).wait_recv()
            add(zo, kind, lambda i: R[zo, kind, i].astype(f32))
            if kind == 3:
                xd_copy(zo).start()
                yd_copy(zo).start()

    def phase_two(zo, side):
        yd_copy(zo).wait_recv()
        add(zo, 1, lambda i: YD[zo, i].astype(f32), half, half)
        x_copy(zo).start()
        xd_copy(zo).wait_recv()
        add(zo, 2, lambda i: XD[zo, i].astype(f32), 0, half)
        y_copy(zo).start()

    def phase_three(zo, side):
        x_copy(zo).wait_recv()
        y_copy(zo).wait_recv()
        add(zo, 0, lambda i: X[zo, i].astype(f32) + Y[zo, i].astype(f32))
        if isinstance(side, int) and side == 0:
            return
        if side == -1:
            @pl.when(net.has_dn)
            def _():
                z_copy(zo, 0).wait_recv()
                add(zo, 0, lambda i: Z[zo, 0, i].astype(f32))

            z_copy(zo, 0).start()
        else:
            @pl.when(net.has_up)
            def _():
                z_copy(zo, 1).wait_recv()
                add(zo, 0, lambda i: Z[zo, 1, i].astype(f32))

            z_copy(zo, 1).start()

    la[0] = local_ref[...]
    sa[0] = shared_ref[...]
    v_start(0)
    for copy in loads:
        copy.wait()
    for step in range(nz - 1, -1, -1):
        each(step, begin)
    dx_copy.start()
    for turn_no in range(nz + 2):
        if turn_no < nz:
            each(nz - 1 - turn_no, phase_one)
        if 0 <= turn_no - 1 < nz:
            each(nz - turn_no, phase_two)
        if 0 <= turn_no - 2:
            each(nz + 1 - turn_no, phase_three)
        if turn_no < 5:
            v_finish(turn_no)
            if turn_no < 4:
                v_start(turn_no + 1)
    local_o[...] = la[5]
    shared_o[...] = sa[5]
    dx_copy.wait_recv()

    def join(r, _):
        at = pl.ds(pl.multiple_of(r * 128, 128), 128)
        dx_o[at, :] = own_ref[at, :] + dx_in[at, :].astype(f32)
        return 0

    lax.fori_loop(0, own_ref.shape[0] // 128, join, 0)

    @pl.when(net.has_dn)
    def _():
        z_copy(z, 0).wait_recv()

    @pl.when(net.has_up)
    def _():
        z_copy(z, 1).wait_recv()

    def finish(i, _):
        total = A[z, 0, i].astype(f32)
        total = total + jnp.where(net.has_dn, Z[z, 0, i].astype(f32), 0.0)
        total = total + jnp.where(net.has_up, Z[z, 1, i].astype(f32), 0.0)
        j = part_of(m, order_ref[d * full + i])
        tile = jnp.concatenate([total, rest_of(total, free_of(j))], 0)
        tile_o[i] = turned(tile, j, -1)
        return 0

    lax.fori_loop(0, full, finish, 0)

    def sent(zo, side):
        for kind in range(4):
            c_copy(zo, kind).wait_send()
        xd_copy(zo).wait_send()
        yd_copy(zo).wait_send()
        x_copy(zo).wait_send()
        y_copy(zo).wait_send()
        if isinstance(side, int) and side == 0:
            return
        z_copy(zo, 0).wait_send()

    for step in range(nz):
        each(step, sent)
    dx_copy.wait_send()
    for k in range(5):
        for copy in v_copies(k):
            copy.wait_send()


def scatter_grads(nz, order, parts, own, other, local, shared):
    dma = pltpu.SemaphoreType.DMA
    vm = pl.BlockSpec(memory_space=pltpu.VMEM)
    block = lambda *lead: pltpu.VMEM((*lead, 72, 128), bf16)
    anywhere = pl.BlockSpec(memory_space=pl.ANY)
    return pl.pallas_call(
        functools.partial(scatter_kernel, nz),
        out_shape=[
            jax.ShapeDtypeStruct((24, 96, 128), f32),
            jax.ShapeDtypeStruct(own.shape, f32),
            jax.ShapeDtypeStruct(local.shape, f32),
            jax.ShapeDtypeStruct(shared.shape, f32),
        ],
        in_specs=[pl.BlockSpec(memory_space=pltpu.SMEM)] + [anywhere] * 4 + [vm] * 4,
        out_specs=[vm] * 4,
        scratch_shapes=[
            pltpu.VMEM((4, 48 * nz, 96, 128), bf16), block(nz, 4, 24), block(nz, 4, 24), block(nz, 4, 24),
            block(nz, 12), block(nz, 12), block(nz, 24), block(nz, 24), block(nz, 2, 24), pltpu.VMEM(other.shape, bf16),
            pltpu.VMEM((6, *local.shape), f32), pltpu.VMEM((5, *local.shape), f32),
            pltpu.VMEM((6, *shared.shape), f32), pltpu.VMEM((5, *shared.shape), f32),
            dma((4,)), dma((nz, 4)), dma((nz, 4)),
        ]
        + [dma((nz,))] * 9
        + [dma((nz, 2)), dma((2,)), dma((5, 2)), dma((5, 2))],
        compiler_params=pltpu.CompilerParams(
            collective_id=1, has_side_effects=True, vmem_limit_bytes=56 << 20
        ),
        name="scatter_grads",
    )(order, *parts, own, other, local, shared)


STEP = 5
BETA_ONE = 0.5
BETA_TWO = 0.5
ADAM_EPS = 1e-08
RATE_TILES = 0.04
RATE_VECTORS = 0.2
DECAY = 0.01
HIGH = lax.Precision.HIGHEST


def adam(grad, first, second):
    first_new = BETA_ONE * first + (1.0 - BETA_ONE) * grad
    second_new = BETA_TWO * second + (1.0 - BETA_TWO) * grad * grad
    step_dir = (
        first_new
        / (1.0 - BETA_ONE**STEP)
        / (jnp.sqrt(second_new / (1.0 - BETA_TWO**STEP)) + ADAM_EPS)
    )
    return (first_new, second_new, step_dir)


def from_tiles(tile_set, row_count, col_count):
    edge = tile_set.shape[-1]
    return (
        tile_set.reshape(row_count // edge, col_count // edge, edge, edge)
        .transpose(0, 2, 1, 3)
        .reshape(row_count, col_count)
    )


def plain_weights(tile_order, master, local):
    tiles = lax.all_gather(master.astype(bf16), "dp", axis=0, tiled=True)
    tiles = lax.all_gather(tiles, "mp", axis=0)
    count = tile_order.shape[0]
    inverse = jnp.zeros((count,), jnp.int32).at[tile_order].set(jnp.arange(count, dtype=jnp.int32))
    natural = tiles[:, inverse]
    dense = []
    for rows, cols, where in GRIDS:
        pieces = []
        for r in range(rows):
            pick = [where(r, j) for j in range(cols)]
            groups = jnp.asarray([p for p, _ in pick], jnp.int32)
            numbers = jnp.asarray([n for _, n in pick], jnp.int32)
            pieces.append(natural[groups, numbers].transpose(1, 0, 2).reshape(96, cols * 96))
        dense.append(jnp.concatenate(pieces, 0))
    return (*dense, lax.all_gather(local, "mp", axis=0))


def plain_scatter(order, parts, own, other, local, shared):
    tiles = jnp.concatenate(parts, 1)[:, order]
    mine = lax.psum_scatter(tiles, "mp", scatter_dimension=0, tiled=False).astype(f32)
    turns = part_of(lax.axis_index("mp"), order)[:, None, None]
    back = mine
    for k in range(1, 4):
        back = jnp.where(turns == k, jnp.roll(mine, -96 * k, -1), back)
    owned = lax.psum_scatter(back[..., :96], "dp", scatter_dimension=0, tiled=True)
    count = lax.axis_size("mp")
    swapped = lax.ppermute(other, "mp", [(i, i ^ 1) for i in range(count)])
    local_sum, shared_sum = lax.psum((local, shared), ("dp", "mp"))
    return owned, own + swapped.astype(f32), local_sum, shared_sum


def shards(
    tokens,
    cotangent,
    lengths,
    tile_order,
    master,
    first_moment,
    second_moment,
    basis_left,
    basis_right,
    local_vec,
    local_first,
    local_second,
    shared_vec,
    shared_first,
    shared_second,
):
    group_count = lax.axis_size("mp")
    group_index = lax.axis_index("mp")
    owners = lax.axis_size("dp")
    row_total, width = tokens.shape
    rows = row_total // group_count
    per_owner = master.shape[1]
    nz = owners // 2
    routed = per_owner == 24 and nz == 4 and group_count == 4

    if routed:
        w_qkv, w_out, w_up, w_down, vectors = gather_weights(
            nz, tile_order, slot_of_tile(tile_order), master[0], local_vec
        )
    else:
        w_qkv, w_out, w_up, w_down, vectors = plain_weights(tile_order, master[0], local_vec)
    output, tq, to, tu, td, own, other, local_terms, shared_terms = layer(
        tokens, cotangent, lengths, vectors, shared_vec, w_qkv, w_out, w_up, w_down, rows
    )
    parts = [t.reshape(group_count, -1, 96, 128) for t in (tq, to, tu, td)]
    if routed:
        owned, input_grad, local_sum, shared_grad = scatter_grads(
            nz, tile_order, parts, own, other, local_terms, shared_terms
        )
        owned = owned[:, :, :96]
    else:
        owned, input_grad, local_sum, shared_grad = plain_scatter(
            tile_order, parts, own, other, local_terms, shared_terms
        )
    local_grad = lax.dynamic_slice_in_dim(local_sum[:, 0], group_index, 1, 0)
    left_basis = basis_left[0]
    right_basis = basis_right[0]
    rotated = jnp.einsum("ski,skl->sil", left_basis, owned, precision=HIGH)
    rotated = jnp.einsum("sil,slj->sij", rotated, right_basis, precision=HIGH)
    tile_first, tile_second, direction = adam(rotated, first_moment[0], second_moment[0])
    turned = jnp.einsum("sik,skl->sil", left_basis, direction, precision=HIGH)
    turned = jnp.einsum("sil,sjl->sij", turned, right_basis, precision=HIGH)
    tile_weight = master[0] - RATE_TILES * (turned + DECAY * master[0])
    local_first_new, local_second_new, local_dir = adam(local_grad, local_first, local_second)
    shared_first_new, shared_second_new, shared_dir = adam(shared_grad, shared_first, shared_second)
    return (
        output,
        input_grad,
        owned[None],
        tile_first[None],
        tile_second[None],
        tile_weight[None],
        local_grad,
        local_first_new,
        local_second_new,
        local_vec - RATE_VECTORS * local_dir,
        shared_grad,
        shared_first_new,
        shared_second_new,
        shared_vec - RATE_VECTORS * shared_dir,
    )


def solution(mesh):
    placed = (
        P("dp", None),
        P("dp", None),
        P("dp"),
        P(),
        P("mp", "dp", None, None),
        P("mp", "dp", None, None),
        P("mp", "dp", None, None),
        P("mp", "dp", None, None),
        P("mp", "dp", None, None),
        P("mp", None),
        P("mp", None),
        P("mp", None),
        P(),
        P(),
        P(),
    )
    return jax.shard_map(
        shards,
        mesh=mesh,
        in_specs=placed,
        out_specs=(
            P(("dp", "mp"), None),
            P(("dp", "mp"), None),
            P("mp", "dp", None, None),
            P("mp", "dp", None, None),
            P("mp", "dp", None, None),
            P("mp", "dp", None, None),
            P("mp", None),
            P("mp", None),
            P("mp", None),
            P("mp", None),
            P(),
            P(),
            P(),
            P(),
        ),
        check_vma=False,
    )
```

time: 290 us -> 257 us (0.89)
  Pallas kernels: 256 us -> 233 us
  local copies, waits for them, and re-layouts: 12.7 us -> 2.45 us
    pallas_call x4 -> x1, Pallas kernels: 102 us -> 65 us  [layer(): pl.pallas_call(layer_kernel, in_specs=[anywhere, anywhere, smem, vm, vm]...]
    pallas_call x1, Pallas kernels: 71.4 us -> 88 us  [scatter_grads(): pl.pallas_call(functools.partial(scatter_kernel, nz), out_shape=[jax.Shap...]
    unnamed x43 -> x30, local copies, waits for them, and re-layouts: 8.93 us -> 2.45 us
where the time goes in v2:
time: 257 us; the launch traced here: 253 us
  Pallas kernels  233 us (91%)
  matrix products  10.3 us (4%)
  other arithmetic  5.46 us (2%)
    pallas_call x1, Pallas kernels, scatter_grads(): pl.pallas_call(functools.partial(scatter_kernel, nz), out_shape=[jax.Shap...  88 us
    pallas_call x1, Pallas kernels, gather_weights(): pl.pallas_call(functools.partial(gather_kernel, nz), out_shape=[jax.Shape...  80.1 us
    pallas_call x1, Pallas kernels, layer(): pl.pallas_call(layer_kernel, in_specs=[anywhere, anywhere, smem, vm, vm]...  65 us

profile of v2, /device:TPU:16, one launch (start us, length us, event | category | flops | bytes accessed | tf_op | source)
XLA Modules:
  0.0 252.7 jit_solution(6242246854892489847)
XLA Ops:
  0.6 0.0 copy-start
  0.7 1.5 select_reduce_fusion.src_ref
  2.1 80.1 %gather_weights.1 = (bf16[768,2304]{1,0:T(8,128)(2,1)}, bf16[768,768]{1,0:T(8,128)(2,1)}, bf16[768,3072]{1,0:T(8,128)(2,1)}, bf16[3072,768]{1,0:T(8,128)(2,1)}, f32[4,1,1152]{2,1,0:T(1,128)}) custom-call(s32[192]{0:T(256)} %order_ref.3, s32[192]{0:T(256)} %select_reduce_fusion.src_ref, f32[24,96,96]{2,1,0:T(8,128)} %bitcast.45, f32[1,1152]{1,0:T(1,128)} %local_ref.1), custom_call_target="tpu_custom_call" | custom-call | tf_op jit(solution)/shard_map/gather_weights/pallas_call | solution.py:335
  82.3 65.0 %layer.1 = (bf16[512,768]{1,0:T(8,128)(2,1)}, bf16[4,8,3,2,96,128]{5,4,3,2,1,0:T(8,128)(2,1)}, bf16[8,8,96,128]{3,2,1,0:T(8,128)(2,1)}, bf16[4,8,2,4,96,128]{5,4...) custom-call(bf16[2048,768]{1,0:T(8,128)(2,1)} %tokens_ref.1, ...), custom_call_target="tpu_custom_call" | custom-call | tf_op jit(solution)/shard_map/layer/pallas_call | solution.py:682
  147.3 88.0 %scatter_grads.1 = (f32[24,96,128]{2,1,0:T(8,128)}, f32[512,768]{1,0:T(8,128)}, f32[4,1,1152]{2,1,0:T(1,128)}, f32[6,768]{1,0:T(8,128)}) custom-call(s32[192]{0:T(256)} %order_ref.3, bf16[4,48,96,128]{3,2,1,0:T(8,128)(2,1)} %bitcast.46, bf16[4,16,96,128]{3,2,1,0:T(8,128)(2,1)} %bitcast.47, bf16[4,64,96,128]{3,2,1,0:T(8,128)(2,1)} %bitcast.43, ...), custom_call_target="tpu_custom_call" | custom-call | tf_op jit(solution)/shard_map/scatter_grads/pallas_call | solution.py:927
  235.4 0.0 copy-start.1
  235.4 3.4 %fusion.9 = f32[24,96,96]{1,2,0:T(8,128)S(1)} fusion(f32[1,24,96,96]{3,2,1,0:T(8,128)S(1)} %copy-done, f32[24,96,128]{2,1,0:T(8,128)} %get-tuple-element.47), kind=kOutput, calls=%fused_computation.12 | convolution fusion | flops 254803968 | bytes 2949120 | tf_op jit(solution)/shard_map/ski,skl->sil/dot_general | solution.py:1063
  238.8 0.0 copy-start.5
  238.8 0.0 copy-start.6
  238.8 1.3 fusion.5
  240.1 0.3 copy-done.5
  240.4 0.4 copy-done.6
  240.8 2.0 fusion.21
  242.8 2.1 fusion.7
  244.9 0.0 copy-start.7
  244.9 0.0 copy-start.9
  244.9 0.0 copy-start.10
  245.0 0.0 copy-start.11
  245.0 0.0 copy-start.12
  245.0 3.5 %fusion.2 = f32[1,24,96,96]{3,2,1,0:T(8,128)} fusion(f32[24,96,96]{1,2,0:T(8,128)S(1)} %fusion.7, f32[1,24,96,96]{3,2,1,0:T(8,128)S(1)} %copy-done.1, f32[1,24,96,96]{3,2,1,0:T(8,128)S(1)} %copy-done.3), kind=kOutput, calls=%fused_computation.5 | convolution fusion | flops 255688704 | bytes 3538944 | tf_op jit(solution)/shard_map/sil,sjl->sij/dot_general | solution.py:1067
  248.5 0.6 multiply_subtract_fusion
  249.2 1.3 multiply_subtract_fusion.1
  250.5 1.1 copy.31
  251.6 0.6 copy.32
  (17 shorter events, 0.0 us)
Async XLA Ops:
  0.6 234.7 %copy-start = (f32[1,24,96,96]{3,2,1,0:T(8,128)S(1)}, f32[1,24,96,96]{3,2,1,0:T(8,128)}, u32[]{:S(2)}) copy-start(f32[1,24,96,96]{3,2,1,0:T(8,128)} %param.22) | copy-start | bytes 2654212
  235.4 3.4 %copy-start.1 = (f32[1,24,96,96]{3,2,1,0:T(8,128)S(1)}, f32[1,24,96,96]{3,2,1,0:T(8,128)}, u32[]{:S(2)}) copy-start(f32[1,24,96,96]{3,2,1,0:T(8,128)} %param.23) | copy-start | bytes 2654212
  238.8 1.4 copy-start.2
  238.8 1.6 copy-start.5
  238.8 2.0 copy-start.6
  242.8 2.1 copy-start.3
  244.9 3.6 %copy-start.7 = (f32[6,768]{1,0:T(8,128)S(1)}, f32[6,768]{1,0:T(8,128)}, u32[]{:S(2)}) copy-start(f32[6,768]{1,0:T(8,128)} %sv_ref.1) | copy-start | bytes 55300
  244.9 3.6 %copy-start.8 = (f32[6,768]{1,0:T(8,128)S(1)}, f32[6,768]{1,0:T(8,128)}, u32[]{:S(2)}) copy-start(f32[6,768]{1,0:T(8,128)} %get-tuple-element.84) | copy-start | bytes 55300
  244.9 3.6 %copy-start.9 = (f32[6,768]{1,0:T(8,128)S(1)}, f32[6,768]{1,0:T(8,128)}, u32[]{:S(2)}) copy-start(f32[6,768]{1,0:T(8,128)} %param.29) | copy-start | bytes 55300
  244.9 3.6 %copy-start.10 = (f32[6,768]{1,0:T(8,128)S(1)}, f32[6,768]{1,0:T(8,128)}, u32[]{:S(2)}) copy-start(f32[6,768]{1,0:T(8,128)} %param.28) | copy-start | bytes 55300
  245.0 4.2 %copy-start.11 = (f32[1,1152]{1,0:T(1,128)S(1)}, f32[1,1152]{1,0:T(1,128)}, u32[]{:S(2)}) copy-start(f32[1,1152]{1,0:T(1,128)} %local_ref.1) | copy-start | bytes 13828
  245.0 4.2 %copy-start.12 = (f32[1,1152]{1,0:T(1,128)S(1)}, f32[1,1152]{1,0:T(1,128)}, u32[]{:S(2)}) copy-start(f32[1,1152]{1,0:T(1,128)} %param.26) | copy-start | bytes 13828
  245.0 4.2 %copy-start.13 = (f32[1,1152]{1,0:T(1,128)S(1)}, f32[1,1152]{1,0:T(1,128)}, u32[]{:S(2)}) copy-start(f32[1,1152]{1,0:T(1,128)} %param.25) | copy-start | bytes 13828
  245.0 5.5 %copy-start.4 = (f32[512,768]{1,0:T(8,128)S(1)}, f32[512,768]{1,0:T(8,128)}, u32[]{:S(2)}) copy-start(f32[512,768]{1,0:T(8,128)} %get-tuple-element.75) | copy-start | bytes 4718596

commit v3 on v2

--- a/solution.py
+++ b/solution.py
@@ -52,16 +52,40 @@
     return out
 
 
-def join_four(tiles):
-    lane = lanes_of(tiles[0].shape)
-    a, b, c, d = tiles
-    return [jnp.where(lane < 96, a, b), jnp.where(lane < 64, b, c), jnp.where(lane < 32, c, d)]
+def join_four(wires):
+    lane, group = lanes_of((72, 128)), groups_of((24, 128))
+    a, b, c, d = wires
+    tops = [jnp.where(lane < 96, a, b), jnp.where(lane < 64, b, c), jnp.where(lane < 32, c, d)]
+    rests = []
+    for i in range(3):
+        at = slice(24 * i, 24 * i + 24)
+        mixed = jnp.where(
+            group == 3, a[at], jnp.where(group == 2, b[at], jnp.where(group == 1, c[at], d[at]))
+        )
+        rests.append(turn(mixed, 32 * (i + 1)))
+    pieces = []
+    for k in range(3):
+        index = (group + k) % 3
+        rest = jnp.where(index == 0, rests[0], jnp.where(index == 1, rests[1], rests[2]))
+        pieces.append(jnp.concatenate([tops[k], rest], 0))
+    return pieces
 
 
 def split_four(pieces):
-    lane = lanes_of(pieces[0].shape)
-    a, b, c = pieces
-    return [a, jnp.where(lane < 64, b, a), jnp.where(lane < 32, c, b), c]
+    lane, group = lanes_of((72, 128)), groups_of((24, 128))
+    a, b, c = (p[:72] for p in pieces)
+    rests = [p[72:] for p in pieces]
+    sides = []
+    for i in range(3):
+        mixed = jnp.where(
+            group % 3 == 0,
+            rests[i],
+            jnp.where(group == 1, rests[(i - 1) % 3], rests[(i - 2) % 3]),
+        )
+        sides.append(turn(mixed, 96 - 32 * i))
+    side = jnp.concatenate(sides, 0)
+    tops = [a, jnp.where(lane < 64, b, a), jnp.where(lane < 32, c, b), c]
+    return [jnp.where(lane // 32 == 3 - t, side, tops[t]) for t in range(4)]
 
 
 def place():
@@ -83,13 +107,18 @@
         self.has_up = self.z < nz - 1
         self.has_dn = self.z > 0
 
-    def enter(self):
-        bar = pltpu.get_barrier_semaphore()
+    def peers(self):
         others = [(lax.rem(self.z + k, self.nz) * 2 + self.x, self.m) for k in range(1, self.nz)]
-        peers = [self.xn, self.yn, self.cn] + others
-        for peer in peers:
-            pl.semaphore_signal(bar, inc=1, device_id=peer, device_id_type=MESH)
-        pl.semaphore_wait(bar, len(peers))
+        return [self.xn, self.yn, self.cn] + others
+
+    def greet(self):
+        for peer in self.peers():
+            pl.semaphore_signal(
+                pltpu.get_barrier_semaphore(), inc=1, device_id=peer, device_id_type=MESH
+            )
+
+    def await_all(self):
+        pl.semaphore_wait(pltpu.get_barrier_semaphore(), len(self.peers()))
 
 
 def send(src, dst, ss, rs, peer):
@@ -119,97 +148,80 @@
 
 def gather_kernel(
     nz, order_ref, src_ref, master_ref, local_ref, o_qkv, o_out, o_up, o_down, o_local,
-    G, H, LV, d_qkv, d_out, d_up, d_down,
-    zs, zr, xs, xr, ys, yr, xds, xdr, yds, ydr, cs, cr, outs, lvs, lvr,
+    G, LV, d_qkv, d_out, d_up, d_down,
+    zs, zr, xs, xr, ys, yr, xds, xdr, yds, ydr, cs, cr, zxs, zxr, cxs, cxr, outs, lvs, lvr,
 ):
     net = Net(nz)
     z, x, y, c, m = net.z, net.x, net.y, net.c, net.m
     my = (1 - y) * 2 + c
-    net.enter()
-    full = 24
-    half = 12
-    LV[m] = local_ref[...]
-    lv_y = send(LV.at[m], LV.at[m], lvs.at[0], lvr.at[0], net.yn)
-    lv_c = send(LV.at[m], LV.at[m], lvs.at[1], lvr.at[1], net.cn)
-    lv_d = send(LV.at[my], LV.at[my], lvs.at[2], lvr.at[2], net.cn)
-    lv_y.start()
-    lv_c.start()
-
-    def slot(mo, zo, xo, lo=0, n=full):
-        return G.at[mo, pl.ds((zo * 2 + xo) * full + lo, n)]
+    full, late = 24, 5
+    early = full - late
+    net.greet()
 
     def stage(i, _):
         tile = jnp.concatenate([master_ref[i], jnp.zeros((96, 32), f32)], axis=-1)
         j = part_of(m, order_ref[net.d * full + i])
         tile = turned(tile, j, 1)
         G[m, net.d * full + i] = to_wire(tile, free_of(j)).astype(bf16)
-        H[m, net.d * full + i] = tile[72:96].astype(bf16)
         return 0
 
     lax.fori_loop(0, full, stage, 0)
-
-    def unwrap(mo, zo, xo):
-        base = (zo * 2 + xo) * full
-
-        def body(i, _):
-            for k in range(4):
-                at = base + 4 * i + k
-                free = free_of(part_of(mo, order_ref[at]))
-                H[mo, at] = rest_of(G[mo, at].astype(f32), free).astype(bf16)
-            return 0
-
-        lax.fori_loop(0, full // 4, body, 0)
+    LV[m] = local_ref[...]
+    net.await_all()
+    lv_y = send(LV.at[m], LV.at[m], lvs.at[0], lvr.at[0], net.yn)
+    lv_c = send(LV.at[m], LV.at[m], lvs.at[1], lvr.at[1], net.cn)
+    lv_d = send(LV.at[my], LV.at[my], lvs.at[2], lvr.at[2], net.cn)
+
+    def slot(mo, zo, xo, lo=0, n=full):
+        return G.at[mo, pl.ds((zo * 2 + xo) * full + lo, n)]
+
+    def is_own(side):
+        return isinstance(side, int) and side == 0
+
+    def split(side):
+        return (full, full // 2) if is_own(side) else (early, early // 2 + 1)
+
+    kinds = ((m, x), (m, 1 - x), (my, x), (my, 1 - x))
+    flip = 1 - 2 * c
 
     def z_copy(zo, direction):
         s = slot(m, zo, x)
         peer = net.up if direction == 0 else net.dn
         return send(s, s, zs.at[zo, direction], zr.at[zo], peer)
 
-    def c_copy(zo, kind):
-        mo = (m, m, my, my)[kind]
-        xo = (x, 1 - x, x, 1 - x)[kind]
-        s = slot(mo, zo, xo)
+    def late_copies(zo, direction):
+        peer = net.up if direction == 0 else net.dn
+        for k in range(3):
+            mo, xo = kinds[k + 1]
+            s = slot(mo, zo, xo, early, late)
+            yield send(s, s, zxs.at[zo, k, direction], zxr.at[zo, k], peer)
+
+    def c_copy(zo, kind, side, shift=0):
+        mo, xo = kinds[kind]
+        s = slot(mo + shift, zo, xo, 0, full if kind == 0 or is_own(side) else early)
         return send(s, s, cs.at[zo, kind], cr.at[zo, kind], net.cn)
 
-    def c_arrival(zo, kind):
-        mo = (m, m, my, my)[kind] + 1 - 2 * c
-        xo = (x, 1 - x, x, 1 - x)[kind]
-        s = slot(mo, zo, xo)
-        return send(s, s, cs.at[zo, kind], cr.at[zo, kind], net.cn)
-
-    def x_copy(zo, xo):
-        s = slot(m, zo, xo)
+    def c_late(zo, k, shift=0):
+        mo, xo = kinds[k + 1]
+        s = slot(mo + shift, zo, xo, early, late)
+        return send(s, s, cxs.at[zo, k], cxr.at[zo, k], net.cn)
+
+    def x_copy(zo, xo, side):
+        s = slot(m, zo, xo, 0, split(side)[0])
         return send(s, s, xs.at[zo], xr.at[zo], net.xn)
 
-    def y_copy(zo, mo):
-        s = slot(mo, zo, x)
+    def y_copy(zo, mo, side):
+        s = slot(mo, zo, x, 0, split(side)[0])
         return send(s, s, ys.at[zo], yr.at[zo], net.yn)
 
-    def xd_copy(zo, xo):
-        s = slot(my, zo, xo, 0, half)
+    def xd_copy(zo, xo, side):
+        s = slot(my, zo, xo, 0, split(side)[1])
         return send(s, s, xds.at[zo], xdr.at[zo], net.xn)
 
-    def yd_copy(zo, mo):
-        s = slot(mo, zo, 1 - x, half, half)
+    def yd_copy(zo, mo, side):
+        count, lo = split(side)
+        s = slot(mo, zo, 1 - x, lo, count - lo)
         return send(s, s, yds.at[zo], ydr.at[zo], net.yn)
-
-    def fan(zo):
-        x_copy(zo, x).start()
-        y_copy(zo, m).start()
-        c_copy(zo, 0).start()
-
-    def diag(zo):
-        x_copy(zo, 1 - x).wait_recv()
-        yd_copy(zo, m).start()
-        c_copy(zo, 1).start()
-        y_copy(zo, my).wait_recv()
-        xd_copy(zo, x).start()
-        c_copy(zo, 2).start()
-
-    def fin(zo):
-        xd_copy(zo, 1 - x).wait_recv()
-        yd_copy(zo, my).wait_recv()
-        c_copy(zo, 3).start()
 
     def each(step, fn):
         if step == 0:
@@ -224,83 +236,82 @@
         def _():
             fn(z + step, -1)
 
-    def arrive(zo, side):
-        if isinstance(side, int) and side == 0:
+    def onward(side, copies):
+        if is_own(side) or side == 1:
             @pl.when(net.has_up)
             def _():
-                z_copy(zo, 0).start()
-
+                for copy in copies(0):
+                    copy.start()
+
+        if is_own(side) or side == -1:
             @pl.when(net.has_dn)
             def _():
-                z_copy(zo, 1).start()
-        elif side == 1:
+                for copy in copies(1):
+                    copy.start()
+
+    def arrive(zo, side):
+        if not is_own(side):
             z_copy(zo, 0).wait_recv()
-
-            @pl.when(net.has_up)
-            def _():
-                z_copy(zo, 0).start()
-        else:
-            z_copy(zo, 1).wait_recv()
-
-            @pl.when(net.has_dn)
-            def _():
-                z_copy(zo, 1).start()
-        fan(zo)
-
-    def open_some(zo, side):
-        if not (isinstance(side, int) and side == 0):
-            unwrap(m, zo, x)
-        unwrap(m, zo, 1 - x)
-        unwrap(my, zo, x)
-        for kind in range(3):
-            c_arrival(zo, kind).wait_recv()
-            mo, xo = ((m, x), (m, 1 - x), (my, x))[kind]
-            unwrap(mo + 1 - 2 * c, zo, xo)
-
-    def open_last(zo, side):
-        unwrap(my, zo, 1 - x)
-        c_arrival(zo, 3).wait_recv()
-        unwrap(my + 1 - 2 * c, zo, 1 - x)
-
-    for step in range(nz + 2):
-        if step < nz:
-            each(step, arrive)
-        if 0 <= step - 1 < nz:
-            each(step - 1, lambda zo, side: diag(zo))
-        if 0 <= step - 2:
-            each(step - 2, lambda zo, side: fin(zo))
-        if 0 <= step - 1 < nz:
-            each(step - 1, open_some)
-        if 0 <= step - 2:
-            each(step - 2, open_last)
+        onward(side, lambda direction: [z_copy(zo, direction)])
+        x_copy(zo, x, side).start()
+        y_copy(zo, m, side).start()
+        c_copy(zo, 0, side).start()
+
+    def diag(zo, side):
+        x_copy(zo, 1 - x, side).wait_recv()
+        yd_copy(zo, m, side).start()
+        c_copy(zo, 1, side).start()
+        y_copy(zo, my, side).wait_recv()
+        xd_copy(zo, x, side).start()
+        c_copy(zo, 2, side).start()
+
+    def fin(zo, side):
+        xd_copy(zo, 1 - x, side).wait_recv()
+        yd_copy(zo, my, side).wait_recv()
+        c_copy(zo, 3, side).start()
+
+    def last(zo, side):
+        if not is_own(side):
+            for copy in late_copies(zo, 0):
+                copy.wait_recv()
+        onward(side, lambda direction: late_copies(zo, direction))
+        if not is_own(side):
+            for k in range(3):
+                c_late(zo, k).start()
+
+    def other_core(zo, side):
+        for kind in range(4):
+            c_copy(zo, kind, side, flip).wait_recv()
+            if kind and not is_own(side):
+                c_late(zo, kind - 1, flip).wait_recv()
+
+    each(0, arrive)
+    lv_y.start()
+    lv_c.start()
+    each(1, arrive)
+    each(0, diag)
     send(LV.at[my], LV.at[my], lvs.at[0], lvr.at[0], net.yn).wait_recv()
     lv_d.start()
-    mc = m + 1 - 2 * c
+    each(2, arrive)
+    each(1, diag)
+    each(0, fin)
+    each(0, last)
+    each(3, arrive)
+    each(1, fin)
+    each(1, last)
+    each(2, diag)
+    each(2, last)
+    each(2, fin)
+    each(3, diag)
+    each(3, last)
+    each(3, fin)
+    for step in range(nz):
+        each(step, other_core)
+    mc = m + flip
     send(LV.at[mc], LV.at[mc], lvs.at[1], lvr.at[1], net.cn).wait_recv()
-    mc = my + 1 - 2 * c
+    mc = my + flip
     send(LV.at[mc], LV.at[mc], lvs.at[2], lvr.at[2], net.cn).wait_recv()
     o_local[...] = LV[...]
-    lv_y.wait_send()
-    lv_c.wait_send()
-    lv_d.wait_send()
-    def sent(zo, side):
-        x_copy(zo, x).wait_send()
-        y_copy(zo, m).wait_send()
-        yd_copy(zo, m).wait_send()
-        xd_copy(zo, x).wait_send()
-        for kind in range(4):
-            c_copy(zo, kind).wait_send()
-        if side == 0 or side == 1:
-            @pl.when(net.has_up)
-            def _():
-                z_copy(zo, 0).wait_send()
-        if side == 0 or side == -1:
-            @pl.when(net.has_dn)
-            def _():
-                z_copy(zo, 1).wait_send()
-
-    for step in range(nz):
-        each(step, sent)
 
     copies = []
     for i, ((rows, cols, where), dense, out) in enumerate(
@@ -311,10 +322,7 @@
                 tiles = []
                 for t in range(4):
                     p, n = where(r, 4 * g + t)
-                    at = src_ref[n]
-                    tiles.append(
-                        jnp.concatenate([G[p, at].astype(f32), H[p, at].astype(f32)], 0)
-                    )
+                    tiles.append(G[p, src_ref[n]].astype(f32))
                 for k, piece in enumerate(join_four(tiles)):
                     dense[pl.ds(pl.multiple_of(r * 96, 96), 96), pl.ds(384 * g + 128 * k, 128)] = (
                         piece.astype(bf16)
@@ -325,6 +333,33 @@
         copy = pltpu.make_async_copy(dense, out, outs.at[i])
         copy.start()
         copies.append(copy)
+
+    def sent(zo, side):
+        x_copy(zo, x, side).wait_send()
+        y_copy(zo, m, side).wait_send()
+        yd_copy(zo, m, side).wait_send()
+        xd_copy(zo, x, side).wait_send()
+        for kind in range(4):
+            c_copy(zo, kind, side).wait_send()
+        if not is_own(side):
+            for k in range(3):
+                c_late(zo, k).wait_send()
+
+        def done(direction):
+            z_copy(zo, direction).wait_send()
+            for copy in late_copies(zo, direction):
+                copy.wait_send()
+
+        if is_own(side) or side == 1:
+            pl.when(net.has_up)(lambda: done(0))
+        if is_own(side) or side == -1:
+            pl.when(net.has_dn)(lambda: done(1))
+
+    for step in range(nz):
+        each(step, sent)
+    lv_y.wait_send()
+    lv_c.wait_send()
+    lv_d.wait_send()
     for copy in copies:
         copy.wait()
 
@@ -339,12 +374,12 @@
         in_specs=[pl.BlockSpec(memory_space=pltpu.SMEM)] * 2
         + [pl.BlockSpec(memory_space=pltpu.VMEM)] * 2,
         out_specs=[pl.BlockSpec(memory_space=pl.ANY)] * 4 + [pl.BlockSpec(memory_space=pltpu.VMEM)],
-        scratch_shapes=[pltpu.VMEM((4, 2 * nz * 24, 72, 128), bf16), pltpu.VMEM((4, 2 * nz * 24, 24, 128), bf16),
-            pltpu.VMEM((4, *local.shape), f32)]
+        scratch_shapes=[pltpu.VMEM((4, 2 * nz * 24, 72, 128), bf16), pltpu.VMEM((4, *local.shape), f32)]
         + [pltpu.VMEM(s, bf16) for s in shapes]
         + [dma((nz, 2)), dma((nz,))]
         + [dma((nz,))] * 8
-        + [dma((nz, 4)), dma((nz, 4)), dma((4,)), dma((3,)), dma((3,))],
+        + [dma((nz, 4)), dma((nz, 4)), dma((nz, 3, 2)), dma((nz, 3)), dma((nz, 3)), dma((nz, 3))]
+        + [dma((4,)), dma((3,)), dma((3,))],
         compiler_params=pltpu.CompilerParams(
             collective_id=0, has_side_effects=True, vmem_limit_bytes=56 << 20
         ),
@@ -544,9 +579,8 @@
         return pltpu.make_async_copy(sd.at[i % 2], td_ref.at[i // half, i % half], sd_sem.at[i % 2])
 
     def cuts(full, r):
-        return split_four(
-            [full[96 * r : 96 * r + 96, 128 * n : 128 * n + 128].astype(bf16) for n in range(3)]
-        )
+        pieces = [full[96 * r : 96 * r + 96, 128 * n : 128 * n + 128] for n in range(3)]
+        return [wire.astype(bf16) for wire in split_four(pieces)]
 
     def feed_back(i, _):
         at = pl.ds(pl.multiple_of(i * cut, cut), cut)
@@ -685,10 +719,10 @@
         out_specs=[anywhere] * 7 + [vm, vm],
         out_shape=[
             out(tall, bf16),
-            out((groups, tiles, 3, 2, 96, 128), bf16),
-            out((tiles, tiles, 96, 128), bf16),
-            out((groups, tiles, half, 4, 96, 128), bf16),
-            out((groups, half, 4 * tiles, 96, 128), bf16),
+            out((groups, tiles, 3, 2, 72, 128), bf16),
+            out((tiles, tiles, 72, 128), bf16),
+            out((groups, tiles, half, 4, 72, 128), bf16),
+            out((groups, half, 4 * tiles, 72, 128), bf16),
             out(tall, f32),
             out(tall, bf16),
             out(vectors.shape, f32),
@@ -700,9 +734,9 @@
             V((width // 64, rows, rows), bf16), V(wide, bf16), V(tall, f32), V(tall, bf16), V(wide, bf16),
             V(tall, f32), V((rows, 128), f32), V(tall, f32), V((chunks, rows, cut), bf16),
             V((chunks, rows, cut), bf16), V(tall, bf16), V(tall, bf16), V(tall, bf16), V(long, bf16),
-            V(long, bf16), V(tall, bf16), V(tall, bf16), V((2, tiles, 4, 96, 128), bf16),
-            V((2, 4 * tiles, 96, 128), bf16), V((tiles, tiles, 96, 128), bf16),
-            V((2, 2, tiles, 2, 96, 128), bf16), dma((6,)), dma((4,)), dma((2,)), dma((2,)), dma((2,)),
+            V(long, bf16), V(tall, bf16), V(tall, bf16), V((2, tiles, 4, 72, 128), bf16),
+            V((2, 4 * tiles, 72, 128), bf16), V((tiles, tiles, 72, 128), bf16),
+            V((2, 2, tiles, 2, 72, 128), bf16), dma((6,)), dma((4,)), dma((2,)), dma((2,)), dma((2,)),
         ],
         compiler_params=pltpu.CompilerParams(vmem_limit_bytes=60 << 20),
         name="layer",
@@ -712,62 +746,87 @@
 def scatter_kernel(
     nz, order_ref, tq_ref, to_ref, tu_ref, td_ref, own_ref, other_ref, local_ref, shared_ref,
     tile_o, dx_o, local_o, shared_o,
-    T, S, A, R, XD, YD, X, Y, Z, dx_in, la, lb, sa, sb,
-    tsem, cs, cr, xds, xdr, yds, ydr, xs, xr, ys, yr, zs, zr, dxs, vs, vr,
+    TA, TB, S, A, R, XD, YD, X, Y, Z, ZX, dx_in, la, lb, sa, sb,
+    tsem, cs, cr, xds, xdr, yds, ydr, xs, xr, ys, yr, zs, zr, zxs, zxr, dxs, vs, vr,
 ):
     net = Net(nz)
     z, x, y, c, m, d = net.z, net.x, net.y, net.c, net.m, net.d
     my = (1 - y) * 2 + c
     far = (lax.rem(z + 2, nz) * 2 + x, m)
     near = ((z + 1 - 2 * (z % 2)) * 2 + x, m)
-    full, half = 24, 12
-    low, high = pl.ds(0, half), pl.ds(half, half)
-    loads = []
-    first = 0
-    for i, src in enumerate((tq_ref, to_ref, tu_ref, td_ref)):
-        copy = pltpu.make_async_copy(src, T.at[:, pl.ds(first, src.shape[1])], tsem.at[i])
+    full, late = 24, 5
+    early = full - late
+    flip = 1 - 2 * c
+
+    def loads(held, core):
+        for group in range(2):
+            first = 0
+            for i, src in enumerate((tq_ref, to_ref, tu_ref, td_ref)):
+                count = src.shape[1]
+                yield pltpu.make_async_copy(
+                    src.at[2 * group + core], held.at[group, pl.ds(first, count)],
+                    tsem.at[2 * group + core, i],
+                )
+                first += count
+
+    for copy in (*loads(TB, 1 - c), *loads(TA, c)):
         copy.start()
-        loads.append(copy)
-        first += src.shape[1]
-    net.enter()
+    net.greet()
+    net.await_all()
     kinds = ((m, x), (m, 1 - x), (my, x), (my, 1 - x))
-    flip = 1 - 2 * c
 
     def c_copy(zo, kind):
         return send(S.at[zo, kind], R.at[zo, kind], cs.at[zo, kind], cr.at[zo, kind], net.cn)
 
-    def fill(ref, zo, kind, shift):
+    def fill(ref, zo, kind, held):
         mo, xo = kinds[kind]
         base = (zo * 2 + xo) * full
 
         def body(i, _):
             for j in range(4):
-                number = order_ref[base + 4 * i + j]
-                tile = T[mo + shift, number].astype(f32)
-                ref[zo, kind, 4 * i + j] = to_wire(
-                    tile, free_of(part_of(mo + shift, number))
-                ).astype(bf16)
+                ref[zo, kind, 4 * i + j] = held[mo // 2, order_ref[base + 4 * i + j]]
             return 0
 
         lax.fori_loop(0, full // 4, body, 0)
 
-    def xd_copy(zo):
-        return send(A.at[zo, 3, low], XD.at[zo], xds.at[zo], xdr.at[zo], net.xn)
-
-    def yd_copy(zo):
-        return send(A.at[zo, 3, high], YD.at[zo], yds.at[zo], ydr.at[zo], net.yn)
-
-    def x_copy(zo):
-        return send(A.at[zo, 1], X.at[zo], xs.at[zo], xr.at[zo], net.xn)
-
-    def y_copy(zo):
-        return send(A.at[zo, 2], Y.at[zo], ys.at[zo], yr.at[zo], net.yn)
+    def is_own(side):
+        return isinstance(side, int) and side == 0
+
+    def split(side):
+        return (full, full // 2) if is_own(side) else (early, early // 2 + 1)
+
+    def xd_copy(zo, side):
+        n = split(side)[1]
+        return send(
+            A.at[zo, 3, pl.ds(0, n)], XD.at[zo, pl.ds(0, n)], xds.at[zo], xdr.at[zo], net.xn
+        )
+
+    def yd_copy(zo, side):
+        count, lo = split(side)
+        n = count - lo
+        return send(
+            A.at[zo, 3, pl.ds(lo, n)], YD.at[zo, pl.ds(0, n)], yds.at[zo], ydr.at[zo], net.yn
+        )
+
+    def x_copy(zo, side):
+        n = split(side)[0]
+        return send(A.at[zo, 1, pl.ds(0, n)], X.at[zo, pl.ds(0, n)], xs.at[zo], xr.at[zo], net.xn)
+
+    def y_copy(zo, side):
+        n = split(side)[0]
+        return send(A.at[zo, 2, pl.ds(0, n)], Y.at[zo, pl.ds(0, n)], ys.at[zo], yr.at[zo], net.yn)
 
     def z_copy(zo, direction):
-        return send(
-            A.at[zo, 0], Z.at[zo, direction], zs.at[zo], zr.at[zo, direction],
-            net.up if direction == 0 else net.dn,
-        )
+        peer = net.up if direction == 0 else net.dn
+        return send(A.at[zo, 0], Z.at[zo, direction], zs.at[zo], zr.at[zo, direction], peer)
+
+    def late_copies(zo, direction):
+        peer = net.up if direction == 0 else net.dn
+        for k in range(3):
+            yield send(
+                A.at[zo, k + 1, pl.ds(early, late)], ZX.at[zo, direction, k],
+                zxs.at[zo, k], zxr.at[zo, direction, k], peer,
+            )
 
     dx_copy = send(other_ref, dx_in, dxs.at[0], dxs.at[1], net.cn)
     peers = (net.cn, net.xn, net.yn, near, far)
@@ -788,7 +847,7 @@
         la[k + 1] = la[k] + lb[k]
         sa[k + 1] = sa[k] + sb[k]
 
-    def add(zo, kind, other, lo=0, n=24):
+    def add(zo, kind, other, lo=0, n=full):
         def body(i, _):
             A[zo, kind, lo + i] = (A[zo, kind, lo + i].astype(f32) + other(i)).astype(bf16)
             return 0
@@ -810,31 +869,58 @@
 
     def begin(zo, side):
         for kind in (3, 1, 2, 0):
-            fill(S, zo, kind, flip)
+            fill(S, zo, kind, TB)
             c_copy(zo, kind).start()
+
+    def begin_own(zo, side):
+        for kind in (3, 1, 2, 0):
+            fill(A, zo, kind, TA)
+
+    def late_add(zo, direction):
+        for k, copy in enumerate(late_copies(zo, direction)):
+            copy.wait_recv()
+            add(zo, k + 1, lambda i: ZX[zo, direction, k, i].astype(f32), early, late)
+
+    def diagonal(zo, side):
+        xd_copy(zo, side).start()
+        yd_copy(zo, side).start()
 
     def phase_one(zo, side):
         for kind in (3, 1, 2, 0):
-            fill(A, zo, kind, 0)
             c_copy(zo, kind).wait_recv()
             add(zo, kind, lambda i: R[zo, kind, i].astype(f32))
-            if kind == 3:
-                xd_copy(zo).start()
-                yd_copy(zo).start()
+            if kind == 3 and not is_own(side):
+                diagonal(zo, side)
+        if is_own(side) or side == -1:
+            @pl.when(net.has_dn)
+            def _():
+                late_add(zo, 0)
+
+        if is_own(side) or side == 1:
+            @pl.when(net.has_up)
+            def _():
+                late_add(zo, 1)
+
+        if is_own(side):
+            diagonal(zo, side)
+        else:
+            for copy in late_copies(zo, 0 if side == -1 else 1):
+                copy.start()
 
     def phase_two(zo, side):
-        yd_copy(zo).wait_recv()
-        add(zo, 1, lambda i: YD[zo, i].astype(f32), half, half)
-        x_copy(zo).start()
-        xd_copy(zo).wait_recv()
-        add(zo, 2, lambda i: XD[zo, i].astype(f32), 0, half)
-        y_copy(zo).start()
+        count, lo = split(side)
+        yd_copy(zo, side).wait_recv()
+        add(zo, 1, lambda i: YD[zo, i].astype(f32), lo, count - lo)
+        x_copy(zo, side).start()
+        xd_copy(zo, side).wait_recv()
+        add(zo, 2, lambda i: XD[zo, i].astype(f32), 0, lo)
+        y_copy(zo, side).start()
 
     def phase_three(zo, side):
-        x_copy(zo).wait_recv()
-        y_copy(zo).wait_recv()
-        add(zo, 0, lambda i: X[zo, i].astype(f32) + Y[zo, i].astype(f32))
-        if isinstance(side, int) and side == 0:
+        x_copy(zo, side).wait_recv()
+        y_copy(zo, side).wait_recv()
+        add(zo, 0, lambda i: X[zo, i].astype(f32) + Y[zo, i].astype(f32), 0, split(side)[0])
+        if is_own(side):
             return
         if side == -1:
             @pl.when(net.has_dn)
@@ -854,14 +940,21 @@
     la[0] = local_ref[...]
     sa[0] = shared_ref[...]
     v_start(0)
-    for copy in loads:
+    for copy in loads(TB, 1 - c):
         copy.wait()
-    for step in range(nz - 1, -1, -1):
-        each(step, begin)
-    dx_copy.start()
+    each(nz - 1, begin)
+    for copy in loads(TA, c):
+        copy.wait()
+    each(nz - 1, begin_own)
     for turn_no in range(nz + 2):
+        if turn_no + 1 < nz:
+            each(nz - 2 - turn_no, begin)
         if turn_no < nz:
             each(nz - 1 - turn_no, phase_one)
+        if turn_no + 1 < nz:
+            each(nz - 2 - turn_no, begin_own)
+        if turn_no == 0:
+            dx_copy.start()
         if 0 <= turn_no - 1 < nz:
             each(nz - turn_no, phase_two)
         if 0 <= turn_no - 2:
@@ -903,13 +996,15 @@
     def sent(zo, side):
         for kind in range(4):
             c_copy(zo, kind).wait_send()
-        xd_copy(zo).wait_send()
-        yd_copy(zo).wait_send()
-        x_copy(zo).wait_send()
-        y_copy(zo).wait_send()
-        if isinstance(side, int) and side == 0:
+        xd_copy(zo, side).wait_send()
+        yd_copy(zo, side).wait_send()
+        x_copy(zo, side).wait_send()
+        y_copy(zo, side).wait_send()
+        if is_own(side):
             return
         z_copy(zo, 0).wait_send()
+        for copy in late_copies(zo, 0):
+            copy.wait_send()
 
     for step in range(nz):
         each(step, sent)
@@ -935,16 +1030,17 @@
         in_specs=[pl.BlockSpec(memory_space=pltpu.SMEM)] + [anywhere] * 4 + [vm] * 4,
         out_specs=[vm] * 4,
         scratch_shapes=[
-            pltpu.VMEM((4, 48 * nz, 96, 128), bf16), block(nz, 4, 24), block(nz, 4, 24), block(nz, 4, 24),
-            block(nz, 12), block(nz, 12), block(nz, 24), block(nz, 24), block(nz, 2, 24), pltpu.VMEM(other.shape, bf16),
+            block(2, 48 * nz), block(2, 48 * nz), block(nz, 4, 24), block(nz, 4, 24), block(nz, 4, 24),
+            block(nz, 12), block(nz, 12), block(nz, 24), block(nz, 24), block(nz, 2, 24),
+            block(nz, 2, 3, 5), pltpu.VMEM(other.shape, bf16),
             pltpu.VMEM((6, *local.shape), f32), pltpu.VMEM((5, *local.shape), f32),
             pltpu.VMEM((6, *shared.shape), f32), pltpu.VMEM((5, *shared.shape), f32),
-            dma((4,)), dma((nz, 4)), dma((nz, 4)),
+            dma((4, 4)), dma((nz, 4)), dma((nz, 4)),
         ]
         + [dma((nz,))] * 9
-        + [dma((nz, 2)), dma((2,)), dma((5, 2)), dma((5, 2))],
+        + [dma((nz, 2)), dma((nz, 3)), dma((nz, 2, 3)), dma((2,)), dma((5, 2)), dma((5, 2))],
         compiler_params=pltpu.CompilerParams(
-            collective_id=1, has_side_effects=True, vmem_limit_bytes=56 << 20
+            collective_id=1, has_side_effects=True, vmem_limit_bytes=60 << 20
         ),
         name="scatter_grads",
     )(order, *parts, own, other, local, shared)
@@ -957,7 +1053,6 @@
 RATE_TILES = 0.04
 RATE_VECTORS = 0.2
 DECAY = 0.01
-HIGH = lax.Precision.HIGHEST
 
 
 def adam(grad, first, second):
@@ -969,6 +1064,62 @@
         / (jnp.sqrt(second_new / (1.0 - BETA_TWO**STEP)) + ADAM_EPS)
     )
     return (first_new, second_new, step_dir)
+
+
+def update_kernel(
+    grad_ref, first_ref, second_ref, left_ref, right_ref, master_ref,
+    lg_ref, lv_ref, lf_ref, ls_ref, sg_ref, sv_ref, sf_ref, ss_ref,
+    o_grad, o_first, o_second, o_weight, o_lg, o_lf, o_ls, o_lv, o_sg, o_sf, o_ss, o_sv,
+):
+    @pl.when(pl.program_id(0) == 0)
+    def _():
+        local = lg_ref[lax.axis_index("mp")]
+        first, second, step_dir = adam(local, lf_ref[...], ls_ref[...])
+        o_lg[...] = local
+        o_lf[...] = first
+        o_ls[...] = second
+        o_lv[...] = lv_ref[...] - RATE_VECTORS * step_dir
+        shared = sg_ref[...]
+        first, second, step_dir = adam(shared, sf_ref[...], ss_ref[...])
+        o_sg[...] = shared
+        o_sf[...] = first
+        o_ss[...] = second
+        o_sv[...] = sv_ref[...] - RATE_VECTORS * step_dir
+
+    every = range(grad_ref.shape[0])
+    edge = left_ref.shape[-1]
+    left = [left_ref[i].astype(bf16) for i in every]
+    right = [right_ref[i].astype(bf16) for i in every]
+    for i in every:
+        o_grad[i] = grad_ref[i][:, :edge]
+    half = [nn(grad_ref[i][:, :edge].astype(bf16), right[i]).astype(bf16) for i in every]
+    rotated = [tn(left[i], half[i]) for i in every]
+    moved = [adam(rotated[i], first_ref[i], second_ref[i]) for i in every]
+    for i in every:
+        o_first[i] = moved[i][0]
+        o_second[i] = moved[i][1]
+    half = [nn(left[i], moved[i][2].astype(bf16)).astype(bf16) for i in every]
+    for i in every:
+        turn_back = nt(half[i], right[i])
+        master = master_ref[i]
+        o_weight[i] = master - RATE_TILES * (turn_back + DECAY * master)
+
+
+def update(grad, first, second, left, right, master, local, shared):
+    count, edge, wide = grad.shape
+    part = 6 if count % 6 == 0 else count
+    tile = lambda w: pl.BlockSpec((part, edge, w), lambda i: (i, 0, 0))
+    whole = lambda v: pl.BlockSpec(v.shape, lambda i: (0,) * v.ndim)
+    out = lambda v: jax.ShapeDtypeStruct(v.shape, f32)
+    return pl.pallas_call(
+        update_kernel,
+        grid=(count // part,),
+        in_specs=[tile(wide)] + [tile(edge)] * 5 + [whole(v) for v in (*local, *shared)],
+        out_specs=[tile(edge)] * 4 + [whole(local[1])] * 4 + [whole(shared[1])] * 4,
+        out_shape=[out(first)] * 4 + [out(local[1])] * 4 + [out(shared[1])] * 4,
+        compiler_params=pltpu.CompilerParams(vmem_limit_bytes=58 << 20),
+        name="update",
+    )(grad, first, second, left, right, master, *local, *shared)
 
 
 def from_tiles(tile_set, row_count, col_count):
@@ -1005,7 +1156,9 @@
     back = mine
     for k in range(1, 4):
         back = jnp.where(turns == k, jnp.roll(mine, -96 * k, -1), back)
-    owned = lax.psum_scatter(back[..., :96], "dp", scatter_dimension=0, tiled=True)
+    rest = back[..., 96:].reshape(-1, 3, 24, 32).transpose(0, 2, 1, 3).reshape(-1, 24, 96)
+    tiles = jnp.concatenate([back[..., :96], rest], 1)
+    owned = lax.psum_scatter(tiles, "dp", scatter_dimension=0, tiled=True)
     count = lax.axis_size("mp")
     swapped = lax.ppermute(other, "mp", [(i, i ^ 1) for i in range(count)])
     local_sum, shared_sum = lax.psum((local, shared), ("dp", "mp"))
@@ -1047,43 +1200,21 @@
     output, tq, to, tu, td, own, other, local_terms, shared_terms = layer(
         tokens, cotangent, lengths, vectors, shared_vec, w_qkv, w_out, w_up, w_down, rows
     )
-    parts = [t.reshape(group_count, -1, 96, 128) for t in (tq, to, tu, td)]
+    parts = [t.reshape(group_count, -1, 72, 128) for t in (tq, to, tu, td)]
     if routed:
         owned, input_grad, local_sum, shared_grad = scatter_grads(
             nz, tile_order, parts, own, other, local_terms, shared_terms
         )
-        owned = owned[:, :, :96]
     else:
         owned, input_grad, local_sum, shared_grad = plain_scatter(
             tile_order, parts, own, other, local_terms, shared_terms
         )
-    local_grad = lax.dynamic_slice_in_dim(local_sum[:, 0], group_index, 1, 0)
-    left_basis = basis_left[0]
-    right_basis = basis_right[0]
-    rotated = jnp.einsum("ski,skl->sil", left_basis, owned, precision=HIGH)
-    rotated = jnp.einsum("sil,slj->sij", rotated, right_basis, precision=HIGH)
-    tile_first, tile_second, direction = adam(rotated, first_moment[0], second_moment[0])
-    turned = jnp.einsum("sik,skl->sil", left_basis, direction, precision=HIGH)
-    turned = jnp.einsum("sil,sjl->sij", turned, right_basis, precision=HIGH)
-    tile_weight = master[0] - RATE_TILES * (turned + DECAY * master[0])
-    local_first_new, local_second_new, local_dir = adam(local_grad, local_first, local_second)
-    shared_first_new, shared_second_new, shared_dir = adam(shared_grad, shared_first, shared_second)
-    return (
-        output,
-        input_grad,
-        owned[None],
-        tile_first[None],
-        tile_second[None],
-        tile_weight[None],
-        local_grad,
-        local_first_new,
-        local_second_new,
-        local_vec - RATE_VECTORS * local_dir,
-        shared_grad,
-        shared_first_new,
-        shared_second_new,
-        shared_vec - RATE_VECTORS * shared_dir,
+    tiles = update(
+        owned, first_moment[0], second_moment[0], basis_left[0], basis_right[0], master[0],
+        (local_sum, local_vec, local_first, local_second),
+        (shared_grad, shared_vec, shared_first, shared_second),
     )
+    return (output, input_grad, *(t[None] for t in tiles[:4]), *tiles[4:])
 
 
 def solution(mesh):

time: 257 us -> 229 us (0.89); the launches traced: 253 us -> 228 us
  matrix products: 10.3 us -> 0 us
  Pallas kernels: 233 us -> 225 us
  other arithmetic: 5.46 us -> 1.36 us
    dot_general x4 -> x0, matrix products: 10.3 us -> none  [the longest x1 3.5 us: shards(): turned = jnp.einsum('sil,sjl->sij', turned, right_basis, precision=HIGH)]
    pallas_call x1, Pallas kernels: 80.1 us -> 70 us  [gather_weights(): pl.pallas_call(functools.partial(gather_kernel, nz), out_shape=[jax.Shape...]
    pallas_call x0 -> x1, Pallas kernels: none -> 6.82 us  [update(): pl.pallas_call(update_kernel, grid=(count // part,), in_specs=[tile(wide)...]
    pallas_call x1, Pallas kernels: 88 us -> 81.7 us  [scatter_grads(): pl.pallas_call(functools.partial(scatter_kernel, nz), out_shape=[jax.Shap...]
where the time goes in v3:
time: 229 us; the launch traced here: 228 us
  Pallas kernels  225 us (98%)
    pallas_call x1, Pallas kernels, scatter_grads(): pl.pallas_call(functools.partial(scatter_kernel, nz), out_shape=[jax.Shap...  81.7 us
    pallas_call x1, Pallas kernels, gather_weights(): pl.pallas_call(functools.partial(gather_kernel, nz), out_shape=[jax.Shape...  70 us
    pallas_call x1, Pallas kernels, layer(): pl.pallas_call(layer_kernel, in_specs=[anywhere, anywhere, smem, vm, vm]...  66.1 us
    pallas_call x1, Pallas kernels, update(): pl.pallas_call(update_kernel, grid=(count // part,), in_specs=[tile(wide)...  6.82 us

profile of v3, /device:TPU:16, one launch (start us, length us, event | category | flops | bytes accessed | tf_op | source)
XLA Modules:
  0.0 227.8 jit_solution(7075281160520032179)
XLA Ops:
  0.6 1.4 select_reduce_fusion.src_ref
  2.0 70.0 %gather_weights.1 = (bf16[768,2304]{1,0:T(8,128)(2,1)}, bf16[768,768]{1,0:T(8,128)(2,1)}, bf16[768,3072]{1,0:T(8,128)(2,1)}, bf16[3072,768]{1,0:T(8,128)(2,1)}, f32[4,1,1152]{2,1,0:T(1,128)}) custom-call(s32[192]{0:T(256)} %order_ref.3, s32[192]{0:T(256)} %select_reduce_fusion.src_ref, f32[24,96,96]{2,1,0:T(8,128)} %bitcast.13, f32[1,1152]{1,0:T(1,128)} %lv_ref.1), custom_call_target="tpu_custom_call" | custom-call | tf_op jit(solution)/shard_map/gather_weights/pallas_call | solution.py:370
  72.0 66.1 %layer.1 = (bf16[512,768]{1,0:T(8,128)(2,1)}, bf16[4,8,3,2,72,128]{5,4,3,2,1,0:T(8,128)(2,1)}, bf16[8,8,72,128]{3,2,1,0:T(8,128)(2,1)}, bf16[4,8,2,4,72,128]{5,4...) custom-call(bf16[2048,768]{1,0:T(8,128)(2,1)} %tokens_ref.1, ...), custom_call_target="tpu_custom_call" | custom-call | tf_op jit(solution)/shard_map/layer/pallas_call | solution.py:716
  138.0 81.7 %scatter_grads.1 = (f32[24,96,128]{2,1,0:T(8,128)}, f32[512,768]{1,0:T(8,128)}, f32[4,1,1152]{2,1,0:T(1,128)}, f32[6,768]{1,0:T(8,128)}) custom-call(s32[192]{0:T(256)} %order_ref.3, bf16[4,48,72,128]{3,2,1,0:T(8,128)(2,1)} %bitcast.17, bf16[4,16,72,128]{3,2,1,0:T(8,128)(2,1)} %bitcast.18, bf16[4,64,72,128]{3,2,1,0:T(8,128)(2,1)} %bitcast.15, ...), custom_call_target="tpu_custom_call" | custom-call | tf_op jit(solution)/shard_map/scatter_grads/pallas_call | solution.py:1022
  219.8 0.0 copy-start
  219.8 6.8 %update.1 = (f32[24,96,96]{2,1,0:T(8,128)}, f32[24,96,96]{2,1,0:T(8,128)}, f32[24,96,96]{2,1,0:T(8,128)}, f32[24,96,96]{2,1,0:T(8,128)}, f32[1,1152]{1,0:T(1,128...) custom-call(f32[24,96,128]{2,1,0:T(8,128)} %get-tuple-element.59.gra, ...), custom_call_target="tpu_custom_call" | custom-call | tf_op jit(solution)/shard_map/update/pallas_call | solution.py:1114
  226.6 0.0 copy-done
  226.6 1.1 copy.30
Async XLA Ops:
  219.8 6.8 %copy-start = (f32[512,768]{1,0:T(8,128)S(1)}, f32[512,768]{1,0:T(8,128)}, u32[]{:S(2)}) copy-start(f32[512,768]{1,0:T(8,128)} %get-tuple-element.89) | copy-start | bytes 4718596

commit v4 on v3

--- a/solution.py
+++ b/solution.py
@@ -146,16 +146,163 @@
 GRIDS = ((8, 24, tile_qkv), (8, 8, tile_out), (8, 32, tile_up), (32, 8, tile_down))
 
 
+CHUNKS = ((24, 4),)
+
+
+def is_own(side):
+    return isinstance(side, int) and side == 0
+
+
+def each(net, step, fn):
+    if step == 0:
+        fn(net.z, 0)
+        return
+
+    @pl.when(net.z >= step)
+    def _():
+        fn(net.z - step, 1)
+
+    @pl.when(net.z + step < net.nz)
+    def _():
+        fn(net.z + step, -1)
+
+
+class Part:
+    def __init__(self, net, kinds, index, sems):
+        self.net, self.kinds, self.index, self.sems = net, kinds, index, sems
+        self.size, self.late = CHUNKS[index]
+        self.base = sum(n for n, _ in CHUNKS[:index])
+        self.early = self.size - self.late
+
+    def sem(self, i, *at):
+        return self.sems[i].at[(self.index, *at)]
+
+    def split(self, side):
+        count = self.size if is_own(side) else self.early
+        return count, (count + self.index % 2) // 2
+
+
+class GatherPart(Part):
+    def __init__(self, net, kinds, index, G, sems):
+        super().__init__(net, kinds, index, sems)
+        self.G = G
+
+    def slot(self, kind, zo, lo=0, n=None, shift=0):
+        mo, xo = self.kinds[kind]
+        n = self.size if n is None else n
+        return self.G.at[mo + shift, pl.ds((zo * 2 + xo) * 24 + self.base + lo, n)]
+
+    def go(self, s, i, i_at, j, j_at, peer):
+        return send(s, s, self.sem(i, *i_at), self.sem(j, *j_at), peer)
+
+    def toward(self, direction):
+        return self.net.up if direction == 0 else self.net.dn
+
+    def z_copy(self, zo, direction):
+        return self.go(self.slot(0, zo), 0, (zo, direction), 1, (zo,), self.toward(direction))
+
+    def late_copies(self, zo, direction):
+        for k in range(3):
+            s = self.slot(k + 1, zo, self.early, self.late)
+            yield self.go(s, 12, (zo, k, direction), 13, (zo, k), self.toward(direction))
+
+    def c_copy(self, zo, kind, side, shift=0):
+        n = self.size if kind == 0 or is_own(side) else self.early
+        return self.go(self.slot(kind, zo, 0, n, shift), 10, (zo, kind), 11, (zo, kind), self.net.cn)
+
+    def c_late(self, zo, k, shift=0):
+        s = self.slot(k + 1, zo, self.early, self.late, shift)
+        return self.go(s, 14, (zo, k), 15, (zo, k), self.net.cn)
+
+    def x_copy(self, zo, kind, side):
+        return self.go(self.slot(kind, zo, 0, self.split(side)[0]), 2, (zo,), 3, (zo,), self.net.xn)
+
+    def y_copy(self, zo, kind, side):
+        return self.go(self.slot(kind, zo, 0, self.split(side)[0]), 4, (zo,), 5, (zo,), self.net.yn)
+
+    def xd_copy(self, zo, kind, side):
+        return self.go(self.slot(kind, zo, 0, self.split(side)[1]), 6, (zo,), 7, (zo,), self.net.xn)
+
+    def yd_copy(self, zo, kind, side):
+        count, lo = self.split(side)
+        return self.go(self.slot(kind, zo, lo, count - lo), 8, (zo,), 9, (zo,), self.net.yn)
+
+    def onward(self, side, act):
+        if is_own(side) or side == 1:
+            pl.when(self.net.has_up)(lambda: act(0))
+        if is_own(side) or side == -1:
+            pl.when(self.net.has_dn)(lambda: act(1))
+
+    def arrive(self, zo, side):
+        if not is_own(side):
+            self.z_copy(zo, 0).wait_recv()
+        self.onward(side, lambda direction: self.z_copy(zo, direction).start())
+        self.x_copy(zo, 0, side).start()
+        self.y_copy(zo, 0, side).start()
+        self.c_copy(zo, 0, side).start()
+
+    def diag(self, zo, side):
+        self.x_copy(zo, 1, side).wait_recv()
+        self.yd_copy(zo, 1, side).start()
+        self.c_copy(zo, 1, side).start()
+        self.y_copy(zo, 2, side).wait_recv()
+        self.xd_copy(zo, 2, side).start()
+        self.c_copy(zo, 2, side).start()
+
+    def fin(self, zo, side):
+        self.xd_copy(zo, 3, side).wait_recv()
+        self.yd_copy(zo, 3, side).wait_recv()
+        self.c_copy(zo, 3, side).start()
+
+    def last(self, zo, side):
+        if not is_own(side):
+            for copy in self.late_copies(zo, 0):
+                copy.wait_recv()
+
+        def act(direction):
+            for copy in self.late_copies(zo, direction):
+                copy.start()
+
+        self.onward(side, act)
+        if not is_own(side):
+            for k in range(3):
+                self.c_late(zo, k).start()
+
+    def other_core(self, zo, side):
+        flip = 1 - 2 * self.net.c
+        for kind in range(4):
+            self.c_copy(zo, kind, side, flip).wait_recv()
+            if kind and not is_own(side):
+                self.c_late(zo, kind - 1, flip).wait_recv()
+
+    def sent(self, zo, side):
+        self.x_copy(zo, 0, side).wait_send()
+        self.y_copy(zo, 0, side).wait_send()
+        self.yd_copy(zo, 1, side).wait_send()
+        self.xd_copy(zo, 2, side).wait_send()
+        for kind in range(4):
+            self.c_copy(zo, kind, side).wait_send()
+        if not is_own(side):
+            for k in range(3):
+                self.c_late(zo, k).wait_send()
+
+        def done(direction):
+            self.z_copy(zo, direction).wait_send()
+            for copy in self.late_copies(zo, direction):
+                copy.wait_send()
+
+        self.onward(side, done)
+
+
 def gather_kernel(
     nz, order_ref, src_ref, master_ref, local_ref, o_qkv, o_out, o_up, o_down, o_local,
     G, LV, d_qkv, d_out, d_up, d_down,
-    zs, zr, xs, xr, ys, yr, xds, xdr, yds, ydr, cs, cr, zxs, zxr, cxs, cxr, outs, lvs, lvr,
+    outs, lvs, lvr, *sems,
 ):
     net = Net(nz)
     z, x, y, c, m = net.z, net.x, net.y, net.c, net.m
     my = (1 - y) * 2 + c
-    full, late = 24, 5
-    early = full - late
+    full = 24
     net.greet()
 
     def stage(i, _):
@@ -172,141 +319,43 @@
     lv_c = send(LV.at[m], LV.at[m], lvs.at[1], lvr.at[1], net.cn)
     lv_d = send(LV.at[my], LV.at[my], lvs.at[2], lvr.at[2], net.cn)
 
-    def slot(mo, zo, xo, lo=0, n=full):
-        return G.at[mo, pl.ds((zo * 2 + xo) * full + lo, n)]
-
-    def is_own(side):
-        return isinstance(side, int) and side == 0
-
-    def split(side):
-        return (full, full // 2) if is_own(side) else (early, early // 2 + 1)
-
     kinds = ((m, x), (m, 1 - x), (my, x), (my, 1 - x))
     flip = 1 - 2 * c
-
-    def z_copy(zo, direction):
-        s = slot(m, zo, x)
-        peer = net.up if direction == 0 else net.dn
-        return send(s, s, zs.at[zo, direction], zr.at[zo], peer)
-
-    def late_copies(zo, direction):
-        peer = net.up if direction == 0 else net.dn
-        for k in range(3):
-            mo, xo = kinds[k + 1]
-            s = slot(mo, zo, xo, early, late)
-            yield send(s, s, zxs.at[zo, k, direction], zxr.at[zo, k], peer)
-
-    def c_copy(zo, kind, side, shift=0):
-        mo, xo = kinds[kind]
-        s = slot(mo + shift, zo, xo, 0, full if kind == 0 or is_own(side) else early)
-        return send(s, s, cs.at[zo, kind], cr.at[zo, kind], net.cn)
-
-    def c_late(zo, k, shift=0):
-        mo, xo = kinds[k + 1]
-        s = slot(mo + shift, zo, xo, early, late)
-        return send(s, s, cxs.at[zo, k], cxr.at[zo, k], net.cn)
-
-    def x_copy(zo, xo, side):
-        s = slot(m, zo, xo, 0, split(side)[0])
-        return send(s, s, xs.at[zo], xr.at[zo], net.xn)
-
-    def y_copy(zo, mo, side):
-        s = slot(mo, zo, x, 0, split(side)[0])
-        return send(s, s, ys.at[zo], yr.at[zo], net.yn)
-
-    def xd_copy(zo, xo, side):
-        s = slot(my, zo, xo, 0, split(side)[1])
-        return send(s, s, xds.at[zo], xdr.at[zo], net.xn)
-
-    def yd_copy(zo, mo, side):
-        count, lo = split(side)
-        s = slot(mo, zo, 1 - x, lo, count - lo)
-        return send(s, s, yds.at[zo], ydr.at[zo], net.yn)
-
-    def each(step, fn):
-        if step == 0:
-            fn(z, 0)
-            return
-
-        @pl.when(z >= step)
-        def _():
-            fn(z - step, 1)
-
-        @pl.when(z + step < nz)
-        def _():
-            fn(z + step, -1)
-
-    def onward(side, copies):
-        if is_own(side) or side == 1:
-            @pl.when(net.has_up)
-            def _():
-                for copy in copies(0):
-                    copy.start()
-
-        if is_own(side) or side == -1:
-            @pl.when(net.has_dn)
-            def _():
-                for copy in copies(1):
-                    copy.start()
-
-    def arrive(zo, side):
-        if not is_own(side):
-            z_copy(zo, 0).wait_recv()
-        onward(side, lambda direction: [z_copy(zo, direction)])
-        x_copy(zo, x, side).start()
-        y_copy(zo, m, side).start()
-        c_copy(zo, 0, side).start()
-
-    def diag(zo, side):
-        x_copy(zo, 1 - x, side).wait_recv()
-        yd_copy(zo, m, side).start()
-        c_copy(zo, 1, side).start()
-        y_copy(zo, my, side).wait_recv()
-        xd_copy(zo, x, side).start()
-        c_copy(zo, 2, side).start()
-
-    def fin(zo, side):
-        xd_copy(zo, 1 - x, side).wait_recv()
-        yd_copy(zo, my, side).wait_recv()
-        c_copy(zo, 3, side).start()
-
-    def last(zo, side):
-        if not is_own(side):
-            for copy in late_copies(zo, 0):
-                copy.wait_recv()
-        onward(side, lambda direction: late_copies(zo, direction))
-        if not is_own(side):
-            for k in range(3):
-                c_late(zo, k).start()
-
-    def other_core(zo, side):
-        for kind in range(4):
-            c_copy(zo, kind, side, flip).wait_recv()
-            if kind and not is_own(side):
-                c_late(zo, kind - 1, flip).wait_recv()
-
-    each(0, arrive)
+    parts = [GatherPart(net, kinds, i, G, sems) for i in range(len(CHUNKS))]
+
+    def step_of(distance, name, reverse=False):
+        def run(zo, side):
+            for part in parts:
+                getattr(part, name)(zo, side)
+
+        each(net, distance, run)
+
+    def forwarded(zo, side):
+        for part in parts:
+            part.other_core(zo, side)
+
+    step_of(0, "arrive")
     lv_y.start()
     lv_c.start()
-    each(1, arrive)
-    each(0, diag)
+    step_of(1, "arrive")
+    step_of(0, "diag")
     send(LV.at[my], LV.at[my], lvs.at[0], lvr.at[0], net.yn).wait_recv()
     lv_d.start()
-    each(2, arrive)
-    each(1, diag)
-    each(0, fin)
-    each(0, last)
-    each(3, arrive)
-    each(1, fin)
-    each(1, last)
-    each(2, diag)
-    each(2, last)
-    each(2, fin)
-    each(3, diag)
-    each(3, last)
-    each(3, fin)
+    step_of(2, "arrive")
+    step_of(1, "diag")
+    step_of(0, "fin")
+    step_of(0, "last")
+    step_of(3, "arrive")
+    step_of(1, "fin")
+    step_of(1, "last")
+    step_of(2, "diag")
+    step_of(2, "last")
+    step_of(2, "fin")
+    step_of(3, "diag")
+    step_of(3, "last")
+    step_of(3, "fin")
     for step in range(nz):
-        each(step, other_core)
+        step_of(step, "other_core")
     mc = m + flip
     send(LV.at[mc], LV.at[mc], lvs.at[1], lvr.at[1], net.cn).wait_recv()
     mc = my + flip
@@ -334,29 +383,8 @@
         copy.start()
         copies.append(copy)
 
-    def sent(zo, side):
-        x_copy(zo, x, side).wait_send()
-        y_copy(zo, m, side).wait_send()
-        yd_copy(zo, m, side).wait_send()
-        xd_copy(zo, x, side).wait_send()
-        for kind in range(4):
-            c_copy(zo, kind, side).wait_send()
-        if not is_own(side):
-            for k in range(3):
-                c_late(zo, k).wait_send()
-
-        def done(direction):
-            z_copy(zo, direction).wait_send()
-            for copy in late_copies(zo, direction):
-                copy.wait_send()
-
-        if is_own(side) or side == 1:
-            pl.when(net.has_up)(lambda: done(0))
-        if is_own(side) or side == -1:
-            pl.when(net.has_dn)(lambda: done(1))
-
     for step in range(nz):
-        each(step, sent)
+        step_of(step, "sent")
     lv_y.wait_send()
     lv_c.wait_send()
     lv_d.wait_send()
@@ -376,10 +404,8 @@
         out_specs=[pl.BlockSpec(memory_space=pl.ANY)] * 4 + [pl.BlockSpec(memory_space=pltpu.VMEM)],
         scratch_shapes=[pltpu.VMEM((4, 2 * nz * 24, 72, 128), bf16), pltpu.VMEM((4, *local.shape), f32)]
         + [pltpu.VMEM(s, bf16) for s in shapes]
-        + [dma((nz, 2)), dma((nz,))]
-        + [dma((nz,))] * 8
-        + [dma((nz, 4)), dma((nz, 4)), dma((nz, 3, 2)), dma((nz, 3)), dma((nz, 3)), dma((nz, 3))]
-        + [dma((4,)), dma((3,)), dma((3,))],
+        + [dma((4,)), dma((3,)), dma((3,))]
+        + [dma((len(CHUNKS), nz, *tail)) for tail in ((2,), (), *([()] * 8), (4,), (4,), (3, 2), (3,), (3,), (3,))],
         compiler_params=pltpu.CompilerParams(
             collective_id=0, has_side_effects=True, vmem_limit_bytes=56 << 20
         ),
@@ -432,14 +458,14 @@
     tokens_ref, cot_ref, lengths_ref, vec_ref, sv_ref, wq_ref, wo_ref, wu_ref, wd_ref,
     out_ref, tq_ref, to_ref, tu_ref, td_ref, own_ref, other_ref, dl_ref, ds_ref,
     x, cot, wqkv, wout, wup, wdown, bias, q, k, v, probs, o_t, hid, low, low_t, n_one, r_one, acc,
-    act, slope, g_low, g_o, dq, dk, dv, out, other, su, sd, so, sq, loads, stores, su_sem, sd_sem, sq_sem,
+    act, slope, g_low, g_o, dq, dk, dv, x_t, out, other, su, sd, sq, loads, stores, su_sem, sd_sem, sq_sem,
 ):
     rows, width = q.shape
     seq_len = k.shape[0]
     chunks, _, cut = act.shape
     tiles = width // 96
     pairs = width // 128
-    piece = 128
+    piece = 512
     zero = jnp.zeros((), bf16)
     member = lax.axis_index("mp")
     share = seq_len // rows
@@ -481,7 +507,7 @@
             v[at, lo : lo + 256] = (got + bias[:, width + lo : width + lo + 256]).astype(bf16)
         return 0
 
-    lax.fori_loop(0, share, project, 0)
+    lax.fori_loop(0, share, project, 0, unroll=True)
 
     def picks(shape, rows_at):
         row = lax.broadcasted_iota(jnp.int32, shape, rows_at) + part * rows
@@ -494,20 +520,20 @@
         cols = pl.ds(pl.multiple_of(pair * 128, 128), 128)
         queries = q[:, cols]
         pick = picks((rows, 128), 0)
+        mine = (jnp.where(pick, queries, zero), jnp.where(pick, zero, queries))
+        scores = [nt(k[pl.ds(start, rows), cols], mine[w]) for w, (start, _) in enumerate(windows)]
         outs = []
         for w, (start, limit) in enumerate(windows):
-            these = jnp.where(pick, queries, zero) if w == 0 else jnp.where(pick, zero, queries)
-            scores = nt(k[pl.ds(start, rows), cols], these)
-            inside = lax.broadcasted_iota(jnp.int32, scores.shape, 0) < limit
-            scores = jnp.where(inside, scores, NEG_BIG)
-            weight = jnp.exp(scores - jnp.max(scores, 0, keepdims=True))
+            inside = lax.broadcasted_iota(jnp.int32, scores[w].shape, 0) < limit
+            masked = jnp.where(inside, scores[w], NEG_BIG)
+            weight = jnp.exp(masked - jnp.max(masked, 0, keepdims=True))
             low_probs = (weight * (1.0 / jnp.sum(weight, 0, keepdims=True))).astype(bf16)
             probs[2 * pair + w] = low_probs
             outs.append(tn(v[pl.ds(start, rows), cols], low_probs))
         o_t[cols, :] = jnp.where(picks((128, rows), 1), outs[0], outs[1]).astype(bf16)
         return 0
 
-    lax.fori_loop(0, pairs, forward, 0)
+    lax.fori_loop(0, pairs, forward, 0, unroll=2)
 
     def by_rows(fn):
         def body(r, _):
@@ -537,9 +563,7 @@
 
     def feed(i, _):
         at = pl.ds(pl.multiple_of(i * cut, cut), cut)
-        half = chunks // groups
-        shift = pl.multiple_of(2 * third + (i % half) * cut, 128)
-        pre = nn(low[...], wup[:, at]) + vec_ref[i // half, :, pl.ds(shift, cut)]
+        pre = nn(low[...], wup[:, at]) + vec_ref[i, :, 2 * third :]
         phi = 0.5 * (1.0 + lax.erf(pre * ROOT_HALF))
         density = jnp.exp(-0.5 * pre * pre) * PHI_SCALE
         active = (pre * phi).astype(bf16)
@@ -548,7 +572,7 @@
         acc[...] += nn(active, wdown[at, :])
         return 0
 
-    lax.fori_loop(0, chunks, feed, 0)
+    lax.fori_loop(0, chunks, feed, 0, unroll=4)
     get_c.wait()
     ds_ref[...] = jnp.zeros_like(ds_ref)
 
@@ -571,16 +595,20 @@
     put_out.start()
 
     def put_u(i):
-        half = chunks // groups
-        return pltpu.make_async_copy(su.at[i % 2], tu_ref.at[i // half, :, i % half], su_sem.at[i % 2])
+        return pltpu.make_async_copy(su.at[i % 2], tu_ref.at[i], su_sem.at[i % 2])
 
     def put_d(i):
-        half = chunks // groups
-        return pltpu.make_async_copy(sd.at[i % 2], td_ref.at[i // half, i % half], sd_sem.at[i % 2])
-
-    def cuts(full, r):
-        pieces = [full[96 * r : 96 * r + 96, 128 * n : 128 * n + 128] for n in range(3)]
-        return [wire.astype(bf16) for wire in split_four(pieces)]
+        return pltpu.make_async_copy(sd.at[i % 2], td_ref.at[i], sd_sem.at[i % 2])
+
+    def cut_up(grad, keep):
+        for r in range(grad.shape[0] // 96):
+            for g in range(grad.shape[1] // 384):
+                pieces = [
+                    grad[96 * r : 96 * r + 96, 384 * g + 128 * n : 384 * g + 128 * n + 128]
+                    for n in range(3)
+                ]
+                for t, wire in enumerate(split_four(pieces)):
+                    keep(r, 4 * g + t, wire.astype(bf16))
 
     def feed_back(i, _):
         at = pl.ds(pl.multiple_of(i * cut, cut), cut)
@@ -590,20 +618,18 @@
             put_u(i - 2).wait()
             put_d(i - 2).wait()
 
-        half = chunks // groups
-        shift = pl.multiple_of(2 * third + (i % half) * cut, 128)
         grad_low = (nt(g_low[...], wdown[at, :]) * slope[i].astype(f32)).astype(bf16)
-        dl_ref[i // half, :, pl.ds(shift, cut)] = col_sum(grad_low.astype(f32))
+        dl_ref[i, :, 2 * third :] = col_sum(grad_low.astype(f32))
         acc[...] += nt(grad_low, wup[:, at])
-        for g in range(width // 384):
-            down = tn(act[i], g_low[:, 384 * g : 384 * g + 384])
-            for r in range(4):
-                for t, tile in enumerate(cuts(down, r)):
-                    sd[i % 2, r * tiles + 4 * g + t] = tile
-        up = nn(low_t[...], grad_low)
-        for r in range(tiles):
-            for t, tile in enumerate(cuts(up, r)):
-                su[i % 2, r, t] = tile
+
+        def keep_down(r, j, wire):
+            sd[i % 2, r * tiles + j] = wire
+
+        def keep_up(r, j, wire):
+            su[i % 2, r * tiles + j] = wire
+
+        cut_up(tn(act[i], g_low[...]), keep_down)
+        cut_up(nn(low_t[...], grad_low), keep_up)
         put_u(i).start()
         put_d(i).start()
         return 0
@@ -622,12 +648,13 @@
 
     by_rows(norm_back)
     g_o[...] = nt(g_low[...], wout[...]).astype(bf16)
-    for g in range(width // 384):
-        outer = nn(o_t[...], g_low[:, 384 * g : 384 * g + 384])
-        for r in range(tiles):
-            for t, tile in enumerate(cuts(outer, r)):
-                so[r, 4 * g + t] = tile
-    put_o = pltpu.make_async_copy(so, to_ref, stores.at[1])
+
+    def keep_out(r, j, wire):
+        sd[0, r * tiles + j] = wire
+
+    put_d(chunks - 2).wait()
+    cut_up(nn(o_t[...], g_low[...]), keep_out)
+    put_o = pltpu.make_async_copy(sd.at[0], to_ref, stores.at[1])
     put_o.start()
     dk[...] = jnp.zeros_like(dk)
     dv[...] = jnp.zeros_like(dv)
@@ -653,7 +680,7 @@
         dq[:, cols] = (jnp.where(pick_t, outs[0], outs[1]) * 0.125).T.astype(bf16)
         return 0
 
-    lax.fori_loop(0, pairs, backward, 0)
+    lax.fori_loop(0, pairs, backward, 0, unroll=2)
 
     other[...] = (
         nt(dk[there, :], wqkv[:, width : 2 * width]) + nt(dv[there, :], wqkv[:, 2 * width :])
@@ -674,25 +701,24 @@
         dl_ref[p, :, :third] = sum_q[:, third * p : third * p + third]
         dl_ref[p, :, third : 2 * third] = sum_v[:, third * p : third * p + third]
 
-    everyone = pl.ds(0, seq_len)
+    x_t[...] = x[...].T
     puts = []
-    for index, (grad, source) in enumerate(((dq, here), (dk, everyone), (dv, everyone))):
-        for g in range(width // 384):
-            outer = tn(x[source, :], grad[:, 384 * g : 384 * g + 384])
-            count = index * (width // 384) + g
-            if count >= 2:
-                puts[count - 2].wait()
-            for r in range(tiles):
-                for t, tile in enumerate(cuts(outer, r)):
-                    sq[count % 2, t // 2, r, t % 2] = tile
-            put = pltpu.make_async_copy(
-                sq.at[count % 2], tq_ref.at[pl.ds(2 * g, 2), :, index], sq_sem.at[count % 2]
-            )
-            put.start()
-            puts.append(put)
+    for index, grad in enumerate((dk, dv, dq)):
+        part_no = (1, 2, 0)[index]
+        outer = nn(x_t[:, here] if part_no == 0 else x_t[...], grad[...])
+        if index >= 2:
+            puts[index - 2].wait()
+
+        def keep(r, j, wire):
+            sq[index % 2, j // 2, r, j % 2] = wire
+
+        cut_up(outer, keep)
+        put = pltpu.make_async_copy(sq.at[index % 2], tq_ref.at[:, :, part_no], sq_sem.at[index % 2])
+        put.start()
+        puts.append(put)
     for i in (chunks - 2, chunks - 1):
         put_u(i).wait()
-        put_d(i).wait()
+    put_d(chunks - 1).wait()
     for put in (put_out, put_o, put_x, put_own, puts[-2], puts[-1]):
         put.wait()
 
@@ -701,10 +727,9 @@
     width = w_out.shape[0]
     hidden = w_up.shape[1]
     seq_len = tokens.shape[0] // lengths.shape[0]
-    cut = 384
-    chunks = hidden // cut
     groups = vectors.shape[0]
-    half = chunks // groups
+    cut = hidden // groups
+    chunks = groups
     tiles = width // 96
     anywhere = pl.BlockSpec(memory_space=pl.ANY)
     vm = pl.BlockSpec(memory_space=pltpu.VMEM)
@@ -720,9 +745,9 @@
         out_shape=[
             out(tall, bf16),
             out((groups, tiles, 3, 2, 72, 128), bf16),
-            out((tiles, tiles, 72, 128), bf16),
-            out((groups, tiles, half, 4, 72, 128), bf16),
-            out((groups, half, 4 * tiles, 72, 128), bf16),
+            out((tiles * tiles, 72, 128), bf16),
+            out((groups, cut // 96 * tiles, 72, 128), bf16),
+            out((groups, cut // 96 * tiles, 72, 128), bf16),
             out(tall, f32),
             out(tall, bf16),
             out(vectors.shape, f32),
@@ -734,29 +759,198 @@
             V((width // 64, rows, rows), bf16), V(wide, bf16), V(tall, f32), V(tall, bf16), V(wide, bf16),
             V(tall, f32), V((rows, 128), f32), V(tall, f32), V((chunks, rows, cut), bf16),
             V((chunks, rows, cut), bf16), V(tall, bf16), V(tall, bf16), V(tall, bf16), V(long, bf16),
-            V(long, bf16), V(tall, bf16), V(tall, bf16), V((2, tiles, 4, 72, 128), bf16),
-            V((2, 4 * tiles, 72, 128), bf16), V((tiles, tiles, 72, 128), bf16),
-            V((2, 2, tiles, 2, 72, 128), bf16), dma((6,)), dma((4,)), dma((2,)), dma((2,)), dma((2,)),
+            V(long, bf16), V((width, seq_len), bf16), V(tall, bf16), V(tall, bf16),
+            V((2, cut // 96 * tiles, 72, 128), bf16), V((2, cut // 96 * tiles, 72, 128), bf16),
+            V((2, groups, tiles, 2, 72, 128), bf16), dma((6,)), dma((4,)), dma((2,)), dma((2,)), dma((2,)),
         ],
         compiler_params=pltpu.CompilerParams(vmem_limit_bytes=60 << 20),
         name="layer",
     )(tokens, cotangent, lengths, vectors, shared, w_qkv, w_out, w_up, w_down)
 
 
+class ScatterPart(Part):
+    def __init__(self, net, kinds, index, order_ref, held, held_other, bufs, sems):
+        super().__init__(net, kinds, index, sems)
+        self.order_ref, self.held, self.held_other = order_ref, held, held_other
+        self.S, self.A, self.R, self.XD, self.YD, self.X, self.Y, self.Z, self.ZX = bufs
+
+    def at(self, ref, zo, kind, lo=0, n=None):
+        return ref.at[zo, kind, pl.ds(self.base + lo, self.size if n is None else n)]
+
+    def line(self, ref, zo, n):
+        return ref.at[zo, pl.ds(self.base, n)]
+
+    def toward(self, direction):
+        return self.net.up if direction == 0 else self.net.dn
+
+    def c_copy(self, zo, kind):
+        return send(
+            self.at(self.S, zo, kind), self.at(self.R, zo, kind),
+            self.sem(0, zo, kind), self.sem(1, zo, kind), self.net.cn,
+        )
+
+    def xd_copy(self, zo, side):
+        n = self.split(side)[1]
+        return send(
+            self.at(self.A, zo, 3, 0, n), self.line(self.XD, zo, n), self.sem(2, zo), self.sem(3, zo), self.net.xn
+        )
+
+    def yd_copy(self, zo, side):
+        count, lo = self.split(side)
+        n = count - lo
+        return send(
+            self.at(self.A, zo, 3, lo, n), self.line(self.YD, zo, n), self.sem(4, zo), self.sem(5, zo), self.net.yn
+        )
+
+    def x_copy(self, zo, side):
+        n = self.split(side)[0]
+        return send(
+            self.at(self.A, zo, 1, 0, n), self.line(self.X, zo, n), self.sem(6, zo), self.sem(7, zo), self.net.xn
+        )
+
+    def y_copy(self, zo, side):
+        n = self.split(side)[0]
+        return send(
+            self.at(self.A, zo, 2, 0, n), self.line(self.Y, zo, n), self.sem(8, zo), self.sem(9, zo), self.net.yn
+        )
+
+    def z_copy(self, zo, direction):
+        return send(
+            self.at(self.A, zo, 0), self.at(self.Z, zo, direction),
+            self.sem(10, zo), self.sem(11, zo, direction), self.toward(direction),
+        )
+
+    def late_copies(self, zo, direction):
+        first = sum(n for _, n in CHUNKS[: self.index])
+        for k in range(3):
+            yield send(
+                self.at(self.A, zo, k + 1, self.early, self.late),
+                self.ZX.at[zo, direction, k, pl.ds(first, self.late)],
+                self.sem(12, zo, k), self.sem(13, zo, direction, k), self.toward(direction),
+            )
+
+    def place(self, zo, kind):
+        mo, xo = self.kinds[kind]
+        return mo // 2, (zo * 2 + xo) * 24
+
+    def begin(self, zo, side):
+        for kind in (3, 1, 2, 0):
+            row, first = self.place(zo, kind)
+
+            def one(i):
+                self.S[zo, kind, i] = self.held_other[row, self.order_ref[first + i]]
+
+            rounds(self.base, self.size, one)
+            self.c_copy(zo, kind).start()
+
+    def add(self, zo, kind, other, lo, n):
+        def one(i):
+            self.A[zo, kind, i] = self.A[zo, kind, i] + other(i)
+
+        rounds(self.base + lo, n, one)
+
+    def late_add(self, zo, direction):
+        first = sum(n for _, n in CHUNKS[: self.index]) - self.base - self.early
+        for k, copy in enumerate(self.late_copies(zo, direction)):
+            copy.wait_recv()
+            self.add(
+                zo, k + 1, lambda i: self.ZX[zo, direction, k, i + first], self.early, self.late
+            )
+
+    def diagonal(self, zo, side):
+        self.xd_copy(zo, side).start()
+        self.yd_copy(zo, side).start()
+
+    def one(self, zo, side):
+        for kind in (3, 1, 2, 0):
+            self.c_copy(zo, kind).wait_recv()
+            row, first = self.place(zo, kind)
+
+            def both(i):
+                self.A[zo, kind, i] = self.held[row, self.order_ref[first + i]] + self.R[zo, kind, i]
+
+            rounds(self.base, self.size, both)
+            if kind == 3 and not is_own(side):
+                self.diagonal(zo, side)
+        if is_own(side) or side == -1:
+            pl.when(self.net.has_dn)(lambda: self.late_add(zo, 0))
+        if is_own(side) or side == 1:
+            pl.when(self.net.has_up)(lambda: self.late_add(zo, 1))
+        if is_own(side):
+            self.diagonal(zo, side)
+        else:
+            for copy in self.late_copies(zo, 0 if side == -1 else 1):
+                copy.start()
+
+    def two(self, zo, side):
+        count, lo = self.split(side)
+        self.yd_copy(zo, side).wait_recv()
+        self.add(zo, 1, lambda i: self.YD[zo, i - lo], lo, count - lo)
+        self.x_copy(zo, side).start()
+        self.xd_copy(zo, side).wait_recv()
+        self.add(zo, 2, lambda i: self.XD[zo, i], 0, lo)
+        self.y_copy(zo, side).start()
+
+    def three(self, zo, side):
+        self.x_copy(zo, side).wait_recv()
+        self.y_copy(zo, side).wait_recv()
+        self.add(
+            zo, 0, lambda i: (self.X[zo, i].astype(f32) + self.Y[zo, i].astype(f32)).astype(bf16), 0, self.split(side)[0]
+        )
+        if is_own(side):
+            return
+
+        def more(direction):
+            self.z_copy(zo, direction).wait_recv()
+            self.add(zo, 0, lambda i: self.Z[zo, direction, i], 0, self.size)
+
+        if side == -1:
+            pl.when(self.net.has_dn)(lambda: more(0))
+            self.z_copy(zo, 0).start()
+        else:
+            pl.when(self.net.has_up)(lambda: more(1))
+            self.z_copy(zo, 1).start()
+
+    def total(self, zo):
+        pl.when(self.net.has_dn)(lambda: self.z_copy(zo, 0).wait_recv())
+        pl.when(self.net.has_up)(lambda: self.z_copy(zo, 1).wait_recv())
+
+    def sent(self, zo, side):
+        for kind in range(4):
+            self.c_copy(zo, kind).wait_send()
+        self.xd_copy(zo, side).wait_send()
+        self.yd_copy(zo, side).wait_send()
+        self.x_copy(zo, side).wait_send()
+        self.y_copy(zo, side).wait_send()
+        if is_own(side):
+            return
+        self.z_copy(zo, 0).wait_send()
+        for copy in self.late_copies(zo, 0):
+            copy.wait_send()
+
+
+def rounds(first, count, fn):
+    wide = next(n for n in (6, 5, 4, 3, 2, 1) if count % n == 0)
+
+    def body(i, _):
+        for j in range(wide):
+            fn(first + wide * i + j)
+        return 0
+
+    lax.fori_loop(0, count // wide, body, 0)
+
+
 def scatter_kernel(
     nz, order_ref, tq_ref, to_ref, tu_ref, td_ref, own_ref, other_ref, local_ref, shared_ref,
     tile_o, dx_o, local_o, shared_o,
     TA, TB, S, A, R, XD, YD, X, Y, Z, ZX, dx_in, la, lb, sa, sb,
-    tsem, cs, cr, xds, xdr, yds, ydr, xs, xr, ys, yr, zs, zr, zxs, zxr, dxs, vs, vr,
+    tsem, dxs, vs, vr, *sems,
 ):
     net = Net(nz)
     z, x, y, c, m, d = net.z, net.x, net.y, net.c, net.m, net.d
     my = (1 - y) * 2 + c
     far = (lax.rem(z + 2, nz) * 2 + x, m)
     near = ((z + 1 - 2 * (z % 2)) * 2 + x, m)
-    full, late = 24, 5
-    early = full - late
-    flip = 1 - 2 * c
 
     def loads(held, core):
         for group in range(2):
@@ -772,61 +966,16 @@
     for copy in (*loads(TB, 1 - c), *loads(TA, c)):
         copy.start()
     net.greet()
-    net.await_all()
     kinds = ((m, x), (m, 1 - x), (my, x), (my, 1 - x))
-
-    def c_copy(zo, kind):
-        return send(S.at[zo, kind], R.at[zo, kind], cs.at[zo, kind], cr.at[zo, kind], net.cn)
-
-    def fill(ref, zo, kind, held):
-        mo, xo = kinds[kind]
-        base = (zo * 2 + xo) * full
-
-        def body(i, _):
-            for j in range(4):
-                ref[zo, kind, 4 * i + j] = held[mo // 2, order_ref[base + 4 * i + j]]
-            return 0
-
-        lax.fori_loop(0, full // 4, body, 0)
-
-    def is_own(side):
-        return isinstance(side, int) and side == 0
-
-    def split(side):
-        return (full, full // 2) if is_own(side) else (early, early // 2 + 1)
-
-    def xd_copy(zo, side):
-        n = split(side)[1]
-        return send(
-            A.at[zo, 3, pl.ds(0, n)], XD.at[zo, pl.ds(0, n)], xds.at[zo], xdr.at[zo], net.xn
-        )
-
-    def yd_copy(zo, side):
-        count, lo = split(side)
-        n = count - lo
-        return send(
-            A.at[zo, 3, pl.ds(lo, n)], YD.at[zo, pl.ds(0, n)], yds.at[zo], ydr.at[zo], net.yn
-        )
-
-    def x_copy(zo, side):
-        n = split(side)[0]
-        return send(A.at[zo, 1, pl.ds(0, n)], X.at[zo, pl.ds(0, n)], xs.at[zo], xr.at[zo], net.xn)
-
-    def y_copy(zo, side):
-        n = split(side)[0]
-        return send(A.at[zo, 2, pl.ds(0, n)], Y.at[zo, pl.ds(0, n)], ys.at[zo], yr.at[zo], net.yn)
-
-    def z_copy(zo, direction):
-        peer = net.up if direction == 0 else net.dn
-        return send(A.at[zo, 0], Z.at[zo, direction], zs.at[zo], zr.at[zo, direction], peer)
-
-    def late_copies(zo, direction):
-        peer = net.up if direction == 0 else net.dn
-        for k in range(3):
-            yield send(
-                A.at[zo, k + 1, pl.ds(early, late)], ZX.at[zo, direction, k],
-                zxs.at[zo, k], zxr.at[zo, direction, k], peer,
-            )
+    bufs = (S, A, R, XD, YD, X, Y, Z, ZX)
+    parts = [ScatterPart(net, kinds, i, order_ref, TA, TB, bufs, sems) for i in range(len(CHUNKS))]
+
+    def step_of(distance, name):
+        def run(zo, side):
+            for part in parts:
+                getattr(part, name)(zo, side)
+
+        each(net, distance, run)
 
     dx_copy = send(other_ref, dx_in, dxs.at[0], dxs.at[1], net.cn)
     peers = (net.cn, net.xn, net.yn, near, far)
@@ -847,118 +996,26 @@
         la[k + 1] = la[k] + lb[k]
         sa[k + 1] = sa[k] + sb[k]
 
-    def add(zo, kind, other, lo=0, n=full):
-        def body(i, _):
-            A[zo, kind, lo + i] = (A[zo, kind, lo + i].astype(f32) + other(i)).astype(bf16)
-            return 0
-
-        lax.fori_loop(0, n, body, 0)
-
-    def each(step, fn):
-        if step == 0:
-            fn(z, 0)
-            return
-
-        @pl.when(z >= step)
-        def _():
-            fn(z - step, 1)
-
-        @pl.when(z + step < nz)
-        def _():
-            fn(z + step, -1)
-
-    def begin(zo, side):
-        for kind in (3, 1, 2, 0):
-            fill(S, zo, kind, TB)
-            c_copy(zo, kind).start()
-
-    def begin_own(zo, side):
-        for kind in (3, 1, 2, 0):
-            fill(A, zo, kind, TA)
-
-    def late_add(zo, direction):
-        for k, copy in enumerate(late_copies(zo, direction)):
-            copy.wait_recv()
-            add(zo, k + 1, lambda i: ZX[zo, direction, k, i].astype(f32), early, late)
-
-    def diagonal(zo, side):
-        xd_copy(zo, side).start()
-        yd_copy(zo, side).start()
-
-    def phase_one(zo, side):
-        for kind in (3, 1, 2, 0):
-            c_copy(zo, kind).wait_recv()
-            add(zo, kind, lambda i: R[zo, kind, i].astype(f32))
-            if kind == 3 and not is_own(side):
-                diagonal(zo, side)
-        if is_own(side) or side == -1:
-            @pl.when(net.has_dn)
-            def _():
-                late_add(zo, 0)
-
-        if is_own(side) or side == 1:
-            @pl.when(net.has_up)
-            def _():
-                late_add(zo, 1)
-
-        if is_own(side):
-            diagonal(zo, side)
-        else:
-            for copy in late_copies(zo, 0 if side == -1 else 1):
-                copy.start()
-
-    def phase_two(zo, side):
-        count, lo = split(side)
-        yd_copy(zo, side).wait_recv()
-        add(zo, 1, lambda i: YD[zo, i].astype(f32), lo, count - lo)
-        x_copy(zo, side).start()
-        xd_copy(zo, side).wait_recv()
-        add(zo, 2, lambda i: XD[zo, i].astype(f32), 0, lo)
-        y_copy(zo, side).start()
-
-    def phase_three(zo, side):
-        x_copy(zo, side).wait_recv()
-        y_copy(zo, side).wait_recv()
-        add(zo, 0, lambda i: X[zo, i].astype(f32) + Y[zo, i].astype(f32), 0, split(side)[0])
-        if is_own(side):
-            return
-        if side == -1:
-            @pl.when(net.has_dn)
-            def _():
-                z_copy(zo, 0).wait_recv()
-                add(zo, 0, lambda i: Z[zo, 0, i].astype(f32))
-
-            z_copy(zo, 0).start()
-        else:
-            @pl.when(net.has_up)
-            def _():
-                z_copy(zo, 1).wait_recv()
-                add(zo, 0, lambda i: Z[zo, 1, i].astype(f32))
-
-            z_copy(zo, 1).start()
-
     la[0] = local_ref[...]
     sa[0] = shared_ref[...]
-    v_start(0)
     for copy in loads(TB, 1 - c):
         copy.wait()
-    each(nz - 1, begin)
+    net.await_all()
+    step_of(nz - 1, "begin")
     for copy in loads(TA, c):
         copy.wait()
-    each(nz - 1, begin_own)
+    v_start(0)
     for turn_no in range(nz + 2):
         if turn_no + 1 < nz:
-            each(nz - 2 - turn_no, begin)
+            step_of(nz - 2 - turn_no, "begin")
         if turn_no < nz:
-            each(nz - 1 - turn_no, phase_one)
-        if turn_no + 1 < nz:
-            each(nz - 2 - turn_no, begin_own)
+            step_of(nz - 1 - turn_no, "one")
         if turn_no == 0:
             dx_copy.start()
         if 0 <= turn_no - 1 < nz:
-            each(nz - turn_no, phase_two)
+            step_of(nz - turn_no, "two")
         if 0 <= turn_no - 2:
-            each(nz + 1 - turn_no, phase_three)
+            step_of(nz + 1 - turn_no, "three")
         if turn_no < 5:
             v_finish(turn_no)
             if turn_no < 4:
@@ -973,41 +1030,20 @@
         return 0
 
     lax.fori_loop(0, own_ref.shape[0] // 128, join, 0)
-
-    @pl.when(net.has_dn)
-    def _():
-        z_copy(z, 0).wait_recv()
-
-    @pl.when(net.has_up)
-    def _():
-        z_copy(z, 1).wait_recv()
-
-    def finish(i, _):
+    for part in parts:
+        part.total(z)
+
+    def finish(i):
         total = A[z, 0, i].astype(f32)
         total = total + jnp.where(net.has_dn, Z[z, 0, i].astype(f32), 0.0)
         total = total + jnp.where(net.has_up, Z[z, 1, i].astype(f32), 0.0)
-        j = part_of(m, order_ref[d * full + i])
+        j = part_of(m, order_ref[d * 24 + i])
         tile = jnp.concatenate([total, rest_of(total, free_of(j))], 0)
         tile_o[i] = turned(tile, j, -1)
-        return 0
-
-    lax.fori_loop(0, full, finish, 0)
-
-    def sent(zo, side):
-        for kind in range(4):
-            c_copy(zo, kind).wait_send()
-        xd_copy(zo, side).wait_send()
-        yd_copy(zo, side).wait_send()
-        x_copy(zo, side).wait_send()
-        y_copy(zo, side).wait_send()
-        if is_own(side):
-            return
-        z_copy(zo, 0).wait_send()
-        for copy in late_copies(zo, 0):
-            copy.wait_send()
-
+
+    rounds(0, 24, finish)
     for step in range(nz):
-        each(step, sent)
+        step_of(step, "sent")
     dx_copy.wait_send()
     for k in range(5):
         for copy in v_copies(k):
@@ -1031,14 +1067,16 @@
         out_specs=[vm] * 4,
         scratch_shapes=[
             block(2, 48 * nz), block(2, 48 * nz), block(nz, 4, 24), block(nz, 4, 24), block(nz, 4, 24),
-            block(nz, 12), block(nz, 12), block(nz, 24), block(nz, 24), block(nz, 2, 24),
-            block(nz, 2, 3, 5), pltpu.VMEM(other.shape, bf16),
+            block(nz, 24), block(nz, 24), block(nz, 24), block(nz, 24), block(nz, 2, 24),
+            block(nz, 2, 3, sum(late for _, late in CHUNKS)), pltpu.VMEM(other.shape, bf16),
             pltpu.VMEM((6, *local.shape), f32), pltpu.VMEM((5, *local.shape), f32),
             pltpu.VMEM((6, *shared.shape), f32), pltpu.VMEM((5, *shared.shape), f32),
-            dma((4, 4)), dma((nz, 4)), dma((nz, 4)),
+            dma((4, 4)), dma((2,)), dma((5, 2)), dma((5, 2)),
         ]
-        + [dma((nz,))] * 9
-        + [dma((nz, 2)), dma((nz, 3)), dma((nz, 2, 3)), dma((2,)), dma((5, 2)), dma((5, 2))],
+        + [
+            dma((len(CHUNKS), nz, *tail))
+            for tail in ((4,), (4,), *([()] * 9), (2,), (3,), (2, 3))
+        ],
         compiler_params=pltpu.CompilerParams(
             collective_id=1, has_side_effects=True, vmem_limit_bytes=60 << 20
         ),

time: 229 us -> 210 us (0.917)
  Pallas kernels: 225 us -> 207 us
    pallas_call x1, Pallas kernels: 66.1 us -> 53.6 us  [layer(): pl.pallas_call(layer_kernel, in_specs=[anywhere, anywhere, smem, vm, vm]...]
    pallas_call x1, Pallas kernels: 81.7 us -> 76 us  [scatter_grads(): pl.pallas_call(functools.partial(scatter_kernel, nz), out_shape=[jax.Shap...]
where the time goes in v4:
time: 210 us
  Pallas kernels  207 us (99%)
    pallas_call x1, Pallas kernels, scatter_grads(): pl.pallas_call(functools.partial(scatter_kernel, nz), out_shape=[jax.Shap...  76 us
    pallas_call x1, Pallas kernels, gather_weights(): pl.pallas_call(functools.partial(gather_kernel, nz), out_shape=[jax.Shape...  70.4 us
    pallas_call x1, Pallas kernels, layer(): pl.pallas_call(layer_kernel, in_specs=[anywhere, anywhere, smem, vm, vm]...  53.6 us
    pallas_call x1, Pallas kernels, update(): pl.pallas_call(update_kernel, grid=(count // part,), in_specs=[tile(wide)...  6.85 us

profile of v4, /device:TPU:16, one launch (start us, length us, event | category | flops | bytes accessed | tf_op | source)
XLA Modules:
  0.0 210.0 jit_solution(12358951529971072327)
XLA Ops:
  0.6 1.4 select_reduce_fusion.src_ref
  2.0 70.4 %gather_weights.1 = (bf16[768,2304]{1,0:T(8,128)(2,1)}, bf16[768,768]{1,0:T(8,128)(2,1)}, bf16[768,3072]{1,0:T(8,128)(2,1)}, bf16[3072,768]{1,0:T(8,128)(2,1)}, f32[4,1,1152]{2,1,0:T(1,128)}) custom-call(s32[192]{0:T(256)} %order_ref.3, s32[192]{0:T(256)} %select_reduce_fusion.src_ref, f32[24,96,96]{2,1,0:T(8,128)} %bitcast.11, f32[1,1152]{1,0:T(1,128)} %lv_ref.1), custom_call_target="tpu_custom_call" | custom-call | tf_op jit(solution)/shard_map/gather_weights/pallas_call | solution.py:398
  72.4 53.6 %layer.1 = (bf16[512,768]{1,0:T(8,128)(2,1)}, bf16[4,8,3,2,72,128]{5,4,3,2,1,0:T(8,128)(2,1)}, bf16[64,72,128]{2,1,0:T(8,128)(2,1)}, bf16[4,64,72,128]{3,2,1,0:T...) custom-call(bf16[2048,768]{1,0:T(8,128)(2,1)} %tokens_ref.1, ...), custom_call_target="tpu_custom_call" | custom-call | tf_op jit(solution)/shard_map/layer/pallas_call | solution.py:741
  126.0 76.0 %scatter_grads.1 = (f32[24,96,128]{2,1,0:T(8,128)}, f32[512,768]{1,0:T(8,128)}, f32[4,1,1152]{2,1,0:T(1,128)}, f32[6,768]{1,0:T(8,128)}) custom-call(s32[192]{0:T(256)} %order_ref.3, bf16[4,48,72,128]{3,2,1,0:T(8,128)(2,1)} %bitcast.13, bf16[4,16,72,128]{3,2,1,0:T(8,128)(2,1)} %bitcast.14, bf16[4,64,72,128]{3,2,1,0:T(8,128)(2,1)} %get-tuple-element.52.tu_ref, ...), custom_call_target="tpu_custom_call" | custom-call | tf_op jit(solution)/shard_map/scatter_grads/pallas_call | solution.py:1058
  202.0 0.0 copy-start
  202.0 6.8 %update.1 = (f32[24,96,96]{2,1,0:T(8,128)}, f32[24,96,96]{2,1,0:T(8,128)}, f32[24,96,96]{2,1,0:T(8,128)}, f32[24,96,96]{2,1,0:T(8,128)}, f32[1,1152]{1,0:T(1,128...) custom-call(f32[24,96,128]{2,1,0:T(8,128)} %get-tuple-element.59.gra, ...), custom_call_target="tpu_custom_call" | custom-call | tf_op jit(solution)/shard_map/update/pallas_call | solution.py:1152
  208.9 0.0 copy-done
  208.9 1.1 copy.30
Async XLA Ops:
  202.0 6.9 %copy-start = (f32[512,768]{1,0:T(8,128)S(1)}, f32[512,768]{1,0:T(8,128)}, u32[]{:S(2)}) copy-start(f32[512,768]{1,0:T(8,128)} %get-tuple-element.89) | copy-start | bytes 4718596

commit v5 on v4

--- a/solution.py
+++ b/solution.py
@@ -46,10 +46,9 @@
 
 
 def turned(tile, j, sign):
-    out = tile
-    for k in range(1, 4):
-        out = jnp.where(j == k, turn(tile, sign * 96 * k % 128), out)
-    return out
+    half = (j == 1) | (j == 2) if sign > 0 else j >= 2
+    out = jnp.where(half, turn(tile, 64), tile)
+    return jnp.where(j % 2 == 1, turn(out, 32), out)
 
 
 def join_four(wires):
@@ -295,9 +294,9 @@
 
 
 def gather_kernel(
-    nz, order_ref, src_ref, master_ref, local_ref, o_qkv, o_out, o_up, o_down, o_local,
-    G, LV, d_qkv, d_out, d_up, d_down,
-    outs, lvs, lvr, *sems,
+    nz, order_ref, row_ref, master_ref, local_ref, o_qkv, o_out, o_up, o_down, o_local,
+    G, src_ref, inverse, LV, d_qkv, d_out, d_up, d_down,
+    outs, lvs, lvr, inv_sem, *sems,
 ):
     net = Net(nz)
     z, x, y, c, m = net.z, net.x, net.y, net.c, net.m
@@ -356,11 +355,19 @@
     step_of(3, "fin")
     for step in range(nz):
         step_of(step, "other_core")
+    count = row_ref.shape[1]
+    down = lax.broadcasted_iota(jnp.int32, (count, count), 0)
+    along = lax.broadcasted_iota(jnp.int32, (count, count), 1)
+    column = jnp.sum(jnp.where(down == along, row_ref[...], 0), 1, keepdims=True)
+    inverse[...] = jnp.max(jnp.where(column == along, down, 0), 0, keepdims=True)
+    to_scalars = pltpu.make_async_copy(inverse, src_ref, inv_sem.at[0])
+    to_scalars.start()
     mc = m + flip
     send(LV.at[mc], LV.at[mc], lvs.at[1], lvr.at[1], net.cn).wait_recv()
     mc = my + flip
     send(LV.at[mc], LV.at[mc], lvs.at[2], lvr.at[2], net.cn).wait_recv()
     o_local[...] = LV[...]
+    to_scalars.wait()
 
     copies = []
     for i, ((rows, cols, where), dense, out) in enumerate(
@@ -371,17 +378,17 @@
                 tiles = []
                 for t in range(4):
                     p, n = where(r, 4 * g + t)
-                    tiles.append(G[p, src_ref[n]].astype(f32))
+                    tiles.append(G[p, src_ref[0, n]].astype(f32))
                 for k, piece in enumerate(join_four(tiles)):
                     dense[pl.ds(pl.multiple_of(r * 96, 96), 96), pl.ds(384 * g + 128 * k, 128)] = (
                         piece.astype(bf16)
                     )
+            band = pl.ds(pl.multiple_of(r * 96, 96), 96)
+            pltpu.make_async_copy(dense.at[band], out.at[band], outs.at[i]).start()
             return 0
 
         lax.fori_loop(0, rows, fill, 0)
-        copy = pltpu.make_async_copy(dense, out, outs.at[i])
-        copy.start()
-        copies.append(copy)
+        copies.append(pltpu.make_async_copy(dense, out, outs.at[i]))
 
     for step in range(nz):
         step_of(step, "sent")
@@ -392,31 +399,25 @@
         copy.wait()
 
 
-def gather_weights(nz, order, src, master, local):
+def gather_weights(nz, order, master, local):
     dma = pltpu.SemaphoreType.DMA
     shapes = [(r * 96, c * 96) for r, c, _ in GRIDS]
     return pl.pallas_call(
         functools.partial(gather_kernel, nz),
         out_shape=[jax.ShapeDtypeStruct(s, bf16) for s in shapes]
         + [jax.ShapeDtypeStruct((4, *local.shape), f32)],
-        in_specs=[pl.BlockSpec(memory_space=pltpu.SMEM)] * 2
-        + [pl.BlockSpec(memory_space=pltpu.VMEM)] * 2,
+        in_specs=[pl.BlockSpec(memory_space=pltpu.SMEM)] + [pl.BlockSpec(memory_space=pltpu.VMEM)] * 3,
         out_specs=[pl.BlockSpec(memory_space=pl.ANY)] * 4 + [pl.BlockSpec(memory_space=pltpu.VMEM)],
-        scratch_shapes=[pltpu.VMEM((4, 2 * nz * 24, 72, 128), bf16), pltpu.VMEM((4, *local.shape), f32)]
+        scratch_shapes=[pltpu.VMEM((4, 2 * nz * 24, 72, 128), bf16), pltpu.SMEM((1, 2 * nz * 24), jnp.int32),
+            pltpu.VMEM((1, 2 * nz * 24), jnp.int32), pltpu.VMEM((4, *local.shape), f32)]
         + [pltpu.VMEM(s, bf16) for s in shapes]
-        + [dma((4,)), dma((3,)), dma((3,))]
+        + [dma((4,)), dma((3,)), dma((3,)), dma((1,))]
         + [dma((len(CHUNKS), nz, *tail)) for tail in ((2,), (), *([()] * 8), (4,), (4,), (3, 2), (3,), (3,), (3,))],
         compiler_params=pltpu.CompilerParams(
             collective_id=0, has_side_effects=True, vmem_limit_bytes=56 << 20
         ),
         name="gather_weights",
-    )(order, src, master, local)
-
-
-def slot_of_tile(tile_order):
-    count = tile_order.shape[0]
-    slots = jnp.arange(count, dtype=jnp.int32)
-    return jnp.sum(jnp.where(tile_order[None, :] == slots[:, None], slots[None, :], 0), 1)
+    )(order, order.reshape(1, -1), master, local)
 
 
 NEG_BIG = -1e30
@@ -482,7 +483,10 @@
         return copy
 
     get_x = load(tokens_ref.at[pl.ds(pl.multiple_of(seq * seq_len, seq_len), seq_len)], x, 0)
-    get_q = load(wq_ref, wqkv, 1)
+    get_qkv = [
+        load(wq_ref.at[:, pl.ds(i * width, width)], wqkv.at[:, pl.ds(i * width, width)], 6 + i)
+        for i in range(3)
+    ]
     get_o = load(wo_ref, wout, 2)
     get_u = load(wu_ref, wup, 3)
     get_d = load(wd_ref, wdown, 4)
@@ -494,10 +498,13 @@
     bias[:, width:] = jnp.concatenate([vec_ref[p][:, third : 2 * third] for p in range(groups)], 1)
 
     get_x.wait()
-    get_q.wait()
+    get_qkv[0].wait()
     for lo in range(0, width, 256):
         got = nn(x[here, :], wqkv[:, lo : lo + 256]) + bias[:, lo : lo + 256]
         q[:, lo : lo + 256] = got.astype(bf16) * jnp.asarray(0.125, bf16)
+
+    get_qkv[1].wait()
+    get_qkv[2].wait()
 
     def project(r, _):
         at = pl.ds(pl.multiple_of(r * rows, rows), rows)
@@ -533,7 +540,7 @@
         o_t[cols, :] = jnp.where(picks((128, rows), 1), outs[0], outs[1]).astype(bf16)
         return 0
 
-    lax.fori_loop(0, pairs, forward, 0, unroll=2)
+    lax.fori_loop(0, pairs, forward, 0, unroll=3)
 
     def by_rows(fn):
         def body(r, _):
@@ -663,24 +670,24 @@
         cols = pl.ds(pl.multiple_of(pair * 128, 128), 128)
         pick, pick_t = picks((rows, 128), 0), picks((128, rows), 1)
         queries, grads = q[:, cols], g_o[:, cols]
-        grads_t = grads.astype(f32).T
-        inner = grads_t * o_t[cols, :].astype(f32)
+        grads_t = grads.T
+        inner = grads_t.astype(f32) * o_t[cols, :].astype(f32)
         outs = []
         for w, (start, _) in enumerate(windows):
             at = pl.ds(start, rows)
             mine = (lambda a: jnp.where(pick, a, zero)) if w == 0 else (lambda a: jnp.where(pick, zero, a))
-            mine_t = (lambda a: jnp.where(pick_t, a, 0.0)) if w == 0 else (lambda a: jnp.where(pick_t, 0.0, a))
+            mine_t = (lambda a: jnp.where(pick_t, a, jnp.zeros((), a.dtype))) if w == 0 else (lambda a: jnp.where(pick_t, jnp.zeros((), a.dtype), a))
             dot_sum = jnp.sum(mine_t(inner), 0, keepdims=True)
-            grad_probs = nn(v[at, cols], mine_t(grads_t).astype(bf16))
+            grad_probs = nn(v[at, cols], mine_t(grads_t))
             these = probs[2 * pair + w]
             grad_scores = (these.astype(f32) * (grad_probs - dot_sum)).astype(bf16)
             dv[at, cols] = nn(these, mine(grads)).astype(bf16)
             dk[at, cols] = nn(grad_scores, mine(queries)).astype(bf16)
             outs.append(tn(k[at, cols], grad_scores))
-        dq[:, cols] = (jnp.where(pick_t, outs[0], outs[1]) * 0.125).T.astype(bf16)
+        dq[:, cols] = (jnp.where(pick_t, outs[0], outs[1]) * 0.125).astype(bf16).T
         return 0
 
-    lax.fori_loop(0, pairs, backward, 0, unroll=2)
+    lax.fori_loop(0, pairs, backward, 0, unroll=3)
 
     other[...] = (
         nt(dk[there, :], wqkv[:, width : 2 * width]) + nt(dv[there, :], wqkv[:, 2 * width :])
@@ -761,7 +768,7 @@
             V((chunks, rows, cut), bf16), V(tall, bf16), V(tall, bf16), V(tall, bf16), V(long, bf16),
             V(long, bf16), V((width, seq_len), bf16), V(tall, bf16), V(tall, bf16),
             V((2, cut // 96 * tiles, 72, 128), bf16), V((2, cut // 96 * tiles, 72, 128), bf16),
-            V((2, groups, tiles, 2, 72, 128), bf16), dma((6,)), dma((4,)), dma((2,)), dma((2,)), dma((2,)),
+            V((2, groups, tiles, 2, 72, 128), bf16), dma((9,)), dma((4,)), dma((2,)), dma((2,)), dma((2,)),
         ],
         compiler_params=pltpu.CompilerParams(vmem_limit_bytes=60 << 20),
         name="layer",
@@ -830,18 +837,23 @@
             )
 
     def place(self, zo, kind):
-        mo, xo = self.kinds[kind]
-        return mo // 2, (zo * 2 + xo) * 24
-
-    def begin(self, zo, side):
-        for kind in (3, 1, 2, 0):
+        return kind // 2, (zo * 2 + self.kinds[kind][1]) * 24
+
+    def begin(self, zo, side, these=(3, 1, 2, 0)):
+        for kind in these:
             row, first = self.place(zo, kind)
 
             def one(i):
-                self.S[zo, kind, i] = self.held_other[row, self.order_ref[first + i]]
+                self.S[zo, kind, i] = self.held_other[row][self.order_ref[first + i]]
 
             rounds(self.base, self.size, one)
             self.c_copy(zo, kind).start()
+
+    def begin_far(self, zo, side):
+        self.begin(zo, side, (3, 2))
+
+    def begin_near(self, zo, side):
+        self.begin(zo, side, (1, 0))
 
     def add(self, zo, kind, other, lo, n):
         def one(i):
@@ -867,7 +879,7 @@
             row, first = self.place(zo, kind)
 
             def both(i):
-                self.A[zo, kind, i] = self.held[row, self.order_ref[first + i]] + self.R[zo, kind, i]
+                self.A[zo, kind, i] = self.held[row][self.order_ref[first + i]] + self.R[zo, kind, i]
 
             rounds(self.base, self.size, both)
             if kind == 3 and not is_own(side):
@@ -941,9 +953,9 @@
 
 
 def scatter_kernel(
-    nz, order_ref, tq_ref, to_ref, tu_ref, td_ref, own_ref, other_ref, local_ref, shared_ref,
+    nz, order_ref, tq_ref, to_ref, tu_ref, td_ref, other_ref, local_ref, shared_ref,
     tile_o, dx_o, local_o, shared_o,
-    TA, TB, S, A, R, XD, YD, X, Y, Z, ZX, dx_in, la, lb, sa, sb,
+    TAN, TAF, TBN, TBF, S, A, R, XD, YD, X, Y, Z, ZX, la, lb, sa, sb,
     tsem, dxs, vs, vr, *sems,
 ):
     net = Net(nz)
@@ -952,23 +964,30 @@
     far = (lax.rem(z + 2, nz) * 2 + x, m)
     near = ((z + 1 - 2 * (z % 2)) * 2 + x, m)
 
-    def loads(held, core):
-        for group in range(2):
-            first = 0
-            for i, src in enumerate((tq_ref, to_ref, tu_ref, td_ref)):
-                count = src.shape[1]
-                yield pltpu.make_async_copy(
-                    src.at[2 * group + core], held.at[group, pl.ds(first, count)],
-                    tsem.at[2 * group + core, i],
-                )
-                first += count
-
-    for copy in (*loads(TB, 1 - c), *loads(TA, c)):
-        copy.start()
+    def loads(held, group):
+        first = 0
+        for i, src in enumerate((tq_ref, to_ref, tu_ref, td_ref)):
+            count = src.shape[1]
+            yield pltpu.make_async_copy(
+                src.at[group], held.at[pl.ds(first, count)], tsem.at[group, i]
+            )
+            first += count
+
+    groups = (
+        (TBF, (1 - y) * 2 + 1 - c), (TBN, y * 2 + 1 - c), (TAF, my), (TAN, m),
+    )
+    for held, group in groups:
+        for copy in loads(held, group):
+            copy.start()
+
+    def loaded(i):
+        for copy in loads(*groups[i]):
+            copy.wait()
+
     net.greet()
     kinds = ((m, x), (m, 1 - x), (my, x), (my, 1 - x))
     bufs = (S, A, R, XD, YD, X, Y, Z, ZX)
-    parts = [ScatterPart(net, kinds, i, order_ref, TA, TB, bufs, sems) for i in range(len(CHUNKS))]
+    parts = [ScatterPart(net, kinds, i, order_ref, (TAN, TAF), (TBN, TBF), bufs, sems) for i in range(len(CHUNKS))]
 
     def step_of(distance, name):
         def run(zo, side):
@@ -977,7 +996,7 @@
 
         each(net, distance, run)
 
-    dx_copy = send(other_ref, dx_in, dxs.at[0], dxs.at[1], net.cn)
+    dx_copy = send(other_ref, dx_o, dxs.at[0], dxs.at[1], net.cn)
     peers = (net.cn, net.xn, net.yn, near, far)
 
     def v_copies(k):
@@ -998,12 +1017,13 @@
 
     la[0] = local_ref[...]
     sa[0] = shared_ref[...]
-    for copy in loads(TB, 1 - c):
-        copy.wait()
     net.await_all()
-    step_of(nz - 1, "begin")
-    for copy in loads(TA, c):
-        copy.wait()
+    loaded(0)
+    step_of(nz - 1, "begin_far")
+    loaded(1)
+    step_of(nz - 1, "begin_near")
+    loaded(2)
+    loaded(3)
     v_start(0)
     for turn_no in range(nz + 2):
         if turn_no + 1 < nz:
@@ -1024,22 +1044,13 @@
     shared_o[...] = sa[5]
     dx_copy.wait_recv()
 
-    def join(r, _):
-        at = pl.ds(pl.multiple_of(r * 128, 128), 128)
-        dx_o[at, :] = own_ref[at, :] + dx_in[at, :].astype(f32)
-        return 0
-
-    lax.fori_loop(0, own_ref.shape[0] // 128, join, 0)
     for part in parts:
         part.total(z)
 
     def finish(i):
         total = A[z, 0, i].astype(f32)
         total = total + jnp.where(net.has_dn, Z[z, 0, i].astype(f32), 0.0)
-        total = total + jnp.where(net.has_up, Z[z, 1, i].astype(f32), 0.0)
-        j = part_of(m, order_ref[d * 24 + i])
-        tile = jnp.concatenate([total, rest_of(total, free_of(j))], 0)
-        tile_o[i] = turned(tile, j, -1)
+        tile_o[i] = total + jnp.where(net.has_up, Z[z, 1, i].astype(f32), 0.0)
 
     rounds(0, 24, finish)
     for step in range(nz):
@@ -1050,7 +1061,7 @@
             copy.wait_send()
 
 
-def scatter_grads(nz, order, parts, own, other, local, shared):
+def scatter_grads(nz, order, parts, other, local, shared):
     dma = pltpu.SemaphoreType.DMA
     vm = pl.BlockSpec(memory_space=pltpu.VMEM)
     block = lambda *lead: pltpu.VMEM((*lead, 72, 128), bf16)
@@ -1058,17 +1069,17 @@
     return pl.pallas_call(
         functools.partial(scatter_kernel, nz),
         out_shape=[
-            jax.ShapeDtypeStruct((24, 96, 128), f32),
-            jax.ShapeDtypeStruct(own.shape, f32),
+            jax.ShapeDtypeStruct((24, 72, 128), f32),
+            jax.ShapeDtypeStruct(other.shape, bf16),
             jax.ShapeDtypeStruct(local.shape, f32),
             jax.ShapeDtypeStruct(shared.shape, f32),
         ],
-        in_specs=[pl.BlockSpec(memory_space=pltpu.SMEM)] + [anywhere] * 4 + [vm] * 4,
-        out_specs=[vm] * 4,
+        in_specs=[pl.BlockSpec(memory_space=pltpu.SMEM)] + [anywhere] * 5 + [vm] * 2,
+        out_specs=[vm, anywhere, vm, vm],
         scratch_shapes=[
-            block(2, 48 * nz), block(2, 48 * nz), block(nz, 4, 24), block(nz, 4, 24), block(nz, 4, 24),
+            block(48 * nz), block(48 * nz), block(48 * nz), block(48 * nz), block(nz, 4, 24), block(nz, 4, 24), block(nz, 4, 24),
             block(nz, 24), block(nz, 24), block(nz, 24), block(nz, 24), block(nz, 2, 24),
-            block(nz, 2, 3, sum(late for _, late in CHUNKS)), pltpu.VMEM(other.shape, bf16),
+            block(nz, 2, 3, sum(late for _, late in CHUNKS)),
             pltpu.VMEM((6, *local.shape), f32), pltpu.VMEM((5, *local.shape), f32),
             pltpu.VMEM((6, *shared.shape), f32), pltpu.VMEM((5, *shared.shape), f32),
             dma((4, 4)), dma((2,)), dma((5, 2)), dma((5, 2)),
@@ -1081,7 +1092,7 @@
             collective_id=1, has_side_effects=True, vmem_limit_bytes=60 << 20
         ),
         name="scatter_grads",
-    )(order, *parts, own, other, local, shared)
+    )(order, *parts, other, local, shared)
 
 
 STEP = 5
@@ -1105,9 +1116,9 @@
 
 
 def update_kernel(
-    grad_ref, first_ref, second_ref, left_ref, right_ref, master_ref,
+    order_ref, own_ref, came_ref, grad_ref, first_ref, second_ref, left_ref, right_ref, master_ref,
     lg_ref, lv_ref, lf_ref, ls_ref, sg_ref, sv_ref, sf_ref, ss_ref,
-    o_grad, o_first, o_second, o_weight, o_lg, o_lf, o_ls, o_lv, o_sg, o_sf, o_ss, o_sv,
+    o_own, o_grad, o_first, o_second, o_weight, o_lg, o_lf, o_ls, o_lv, o_sg, o_sf, o_ss, o_sv,
 ):
     @pl.when(pl.program_id(0) == 0)
     def _():
@@ -1124,13 +1135,21 @@
         o_ss[...] = second
         o_sv[...] = sv_ref[...] - RATE_VECTORS * step_dir
 
+    o_own[...] = own_ref[...] + came_ref[...].astype(f32)
     every = range(grad_ref.shape[0])
     edge = left_ref.shape[-1]
+    place_at = (lax.axis_index("dp") * pl.num_programs(0) + pl.program_id(0)) * grad_ref.shape[0]
+    grads = []
+    for i in every:
+        j = part_of(lax.axis_index("mp"), order_ref[place_at + i])
+        wire = grad_ref[i]
+        tile = jnp.concatenate([wire, rest_of(wire, free_of(j))], 0)
+        grads.append(turned(tile, j, -1)[:, :edge])
     left = [left_ref[i].astype(bf16) for i in every]
     right = [right_ref[i].astype(bf16) for i in every]
     for i in every:
-        o_grad[i] = grad_ref[i][:, :edge]
-    half = [nn(grad_ref[i][:, :edge].astype(bf16), right[i]).astype(bf16) for i in every]
+        o_grad[i] = grads[i]
+    half = [nn(grads[i].astype(bf16), right[i]).astype(bf16) for i in every]
     rotated = [tn(left[i], half[i]) for i in every]
     moved = [adam(rotated[i], first_ref[i], second_ref[i]) for i in every]
     for i in every:
@@ -1143,21 +1162,23 @@
         o_weight[i] = master - RATE_TILES * (turn_back + DECAY * master)
 
 
-def update(grad, first, second, left, right, master, local, shared):
-    count, edge, wide = grad.shape
-    part = 6 if count % 6 == 0 else count
-    tile = lambda w: pl.BlockSpec((part, edge, w), lambda i: (i, 0, 0))
+def update(order, own, came, grad, first, second, left, right, master, local, shared):
+    count, edge = first.shape[:2]
+    part = 12 if count % 12 == 0 else count
+    tile = lambda rows, lanes: pl.BlockSpec((part, rows, lanes), lambda i: (i, 0, 0))
     whole = lambda v: pl.BlockSpec(v.shape, lambda i: (0,) * v.ndim)
+    band = pl.BlockSpec((own.shape[0] * part // count, own.shape[1]), lambda i: (i, 0))
     out = lambda v: jax.ShapeDtypeStruct(v.shape, f32)
     return pl.pallas_call(
         update_kernel,
         grid=(count // part,),
-        in_specs=[tile(wide)] + [tile(edge)] * 5 + [whole(v) for v in (*local, *shared)],
-        out_specs=[tile(edge)] * 4 + [whole(local[1])] * 4 + [whole(shared[1])] * 4,
-        out_shape=[out(first)] * 4 + [out(local[1])] * 4 + [out(shared[1])] * 4,
+        in_specs=[pl.BlockSpec(memory_space=pltpu.SMEM), band, band, tile(*grad.shape[1:])]
+        + [tile(edge, edge)] * 5 + [whole(v) for v in (*local, *shared)],
+        out_specs=[band] + [tile(edge, edge)] * 4 + [whole(local[1])] * 4 + [whole(shared[1])] * 4,
+        out_shape=[out(own)] + [out(first)] * 4 + [out(local[1])] * 4 + [out(shared[1])] * 4,
         compiler_params=pltpu.CompilerParams(vmem_limit_bytes=58 << 20),
         name="update",
-    )(grad, first, second, left, right, master, *local, *shared)
+    )(order, own, came, grad, first, second, left, right, master, *local, *shared)
 
 
 def from_tiles(tile_set, row_count, col_count):
@@ -1187,20 +1208,14 @@
     return (*dense, lax.all_gather(local, "mp", axis=0))
 
 
-def plain_scatter(order, parts, own, other, local, shared):
+def plain_scatter(order, parts, other, local, shared):
     tiles = jnp.concatenate(parts, 1)[:, order]
     mine = lax.psum_scatter(tiles, "mp", scatter_dimension=0, tiled=False).astype(f32)
-    turns = part_of(lax.axis_index("mp"), order)[:, None, None]
-    back = mine
-    for k in range(1, 4):
-        back = jnp.where(turns == k, jnp.roll(mine, -96 * k, -1), back)
-    rest = back[..., 96:].reshape(-1, 3, 24, 32).transpose(0, 2, 1, 3).reshape(-1, 24, 96)
-    tiles = jnp.concatenate([back[..., :96], rest], 1)
-    owned = lax.psum_scatter(tiles, "dp", scatter_dimension=0, tiled=True)
+    owned = lax.psum_scatter(mine, "dp", scatter_dimension=0, tiled=True)
     count = lax.axis_size("mp")
     swapped = lax.ppermute(other, "mp", [(i, i ^ 1) for i in range(count)])
     local_sum, shared_sum = lax.psum((local, shared), ("dp", "mp"))
-    return owned, own + swapped.astype(f32), local_sum, shared_sum
+    return owned, swapped, local_sum, shared_sum
 
 
 def shards(
@@ -1231,7 +1246,7 @@
 
     if routed:
         w_qkv, w_out, w_up, w_down, vectors = gather_weights(
-            nz, tile_order, slot_of_tile(tile_order), master[0], local_vec
+            nz, tile_order, master[0], local_vec
         )
     else:
         w_qkv, w_out, w_up, w_down, vectors = plain_weights(tile_order, master[0], local_vec)
@@ -1240,15 +1255,15 @@
     )
     parts = [t.reshape(group_count, -1, 72, 128) for t in (tq, to, tu, td)]
     if routed:
-        owned, input_grad, local_sum, shared_grad = scatter_grads(
-            nz, tile_order, parts, own, other, local_terms, shared_terms
+        owned, came, local_sum, shared_grad = scatter_grads(
+            nz, tile_order, parts, other, local_terms, shared_terms
         )
     else:
-        owned, input_grad, local_sum, shared_grad = plain_scatter(
-            tile_order, parts, own, other, local_terms, shared_terms
+        owned, came, local_sum, shared_grad = plain_scatter(
+            tile_order, parts, other, local_terms, shared_terms
         )
-    tiles = update(
-        owned, first_moment[0], second_moment[0], basis_left[0], basis_right[0], master[0],
+    input_grad, *tiles = update(
+        tile_order, own, came, owned, first_moment[0], second_moment[0], basis_left[0], basis_right[0], master[0],
         (local_sum, local_vec, local_first, local_second),
         (shared_grad, shared_vec, shared_first, shared_second),
     )

time: 210 us -> 206 us (0.981)
    pallas_call x1, Pallas kernels: 76 us -> 73.8 us  [scatter_grads(): pl.pallas_call(functools.partial(scatter_kernel, nz), out_shape=[jax.Shap...]
where the time goes in v5:
time: 206 us
  Pallas kernels  205 us (100%)
    pallas_call x1, Pallas kernels, scatter_grads(): pl.pallas_call(functools.partial(scatter_kernel, nz), out_shape=[jax.Shap...  73.8 us
    pallas_call x1, Pallas kernels, gather_weights(): pl.pallas_call(functools.partial(gather_kernel, nz), out_shape=[jax.Shape...  71.2 us
    pallas_call x1, Pallas kernels, layer(): pl.pallas_call(layer_kernel, in_specs=[anywhere, anywhere, smem, vm, vm]...  52.6 us
    pallas_call x1, Pallas kernels, update(): pl.pallas_call(update_kernel, grid=(count // part,), in_specs=[pl.BlockSp...  7 us

profile of v5, /device:TPU:16, one launch (start us, length us, event | category | flops | bytes accessed | tf_op | source)
XLA Modules:
  0.0 205.5 jit_solution(5864991870169781804)
XLA Ops:
  0.6 71.2 %gather_weights.1 = (bf16[768,2304]{1,0:T(8,128)(2,1)}, bf16[768,768]{1,0:T(8,128)(2,1)}, bf16[768,3072]{1,0:T(8,128)(2,1)}, bf16[3072,768]{1,0:T(8,128)(2,1)}, f32[4,1,1152]{2,1,0:T(1,128)}) custom-call(s32[192]{0:T(256)} %order_ref.5, s32[1,192]{1,0:T(1,128)} %bitcast.20, f32[24,96,96]{2,1,0:T(8,128)} %bitcast.12, f32[1,1152]{1,0:T(1,128)} %lv_ref.1), custom_call_target="tpu_custom_call" | custom-call | tf_op jit(solution)/shard_map/gather_weights/pallas_call | solution.py:405
  71.9 52.6 %layer.1 = (bf16[512,768]{1,0:T(8,128)(2,1)}, bf16[4,8,3,2,72,128]{5,4,3,2,1,0:T(8,128)(2,1)}, bf16[64,72,128]{2,1,0:T(8,128)(2,1)}, bf16[4,64,72,128]{3,2,1,0:T...) custom-call(bf16[2048,768]{1,0:T(8,128)(2,1)} %tokens_ref.1, ...), custom_call_target="tpu_custom_call" | custom-call | tf_op jit(solution)/shard_map/layer/pallas_call | solution.py:748
  124.5 73.8 %scatter_grads.1 = (f32[24,72,128]{2,1,0:T(8,128)}, bf16[512,768]{1,0:T(8,128)(2,1)}, f32[4,1,1152]{2,1,0:T(1,128)}, f32[6,768]{1,0:T(8,128)}) custom-call(s32[192]{0:T(256)} %order_ref.5, bf16[4,48,72,128]{3,2,1,0:T(8,128)(2,1)} %bitcast.14, bf16[4,16,72,128]{3,2,1,0:T(8,128)(2,1)} %bitcast.19, bf16[4,64,72,128]{3,2,1,0:T(8,128)(2,1)} %get-tuple-element.54.tu_ref, ...), custom_call_target="tpu_custom_call" | custom-call | tf_op jit(solution)/shard_map/scatter_grads/pallas_call | solution.py:1069
  198.3 7.0 %update.1 = (f32[512,768]{1,0:T(8,128)}, f32[24,96,96]{2,1,0:T(8,128)}, f32[24,96,96]{2,1,0:T(8,128)}, f32[24,96,96]{2,1,0:T(8,128)}, f32[24,96,96]{2,1,0:T(8,12...) custom-call(s32[192]{0:T(256)} %order_ref.5, ...), custom_call_target="tpu_custom_call" | custom-call | tf_op jit(solution)/shard_map/update/pallas_call | solution.py:1172

commit v6 on v5

--- a/solution.py
+++ b/solution.py
@@ -378,7 +378,7 @@
                 tiles = []
                 for t in range(4):
                     p, n = where(r, 4 * g + t)
-                    tiles.append(G[p, src_ref[0, n]].astype(f32))
+                    tiles.append(G[p, src_ref[0, n]])
                 for k, piece in enumerate(join_four(tiles)):
                     dense[pl.ds(pl.multiple_of(r * 96, 96), 96), pl.ds(384 * g + 128 * k, 128)] = (
                         piece.astype(bf16)
@@ -499,19 +499,15 @@
 
     get_x.wait()
     get_qkv[0].wait()
-    for lo in range(0, width, 256):
-        got = nn(x[here, :], wqkv[:, lo : lo + 256]) + bias[:, lo : lo + 256]
-        q[:, lo : lo + 256] = got.astype(bf16) * jnp.asarray(0.125, bf16)
+    q[...] = (nn(x[here, :], wqkv[:, :width]) + bias[:, :width]).astype(bf16) * jnp.asarray(0.125, bf16)
 
     get_qkv[1].wait()
     get_qkv[2].wait()
 
     def project(r, _):
         at = pl.ds(pl.multiple_of(r * rows, rows), rows)
-        for lo in range(0, width, 256):
-            k[at, lo : lo + 256] = nn(x[at, :], wqkv[:, width + lo : width + lo + 256]).astype(bf16)
-            got = nn(x[at, :], wqkv[:, 2 * width + lo : 2 * width + lo + 256])
-            v[at, lo : lo + 256] = (got + bias[:, width + lo : width + lo + 256]).astype(bf16)
+        k[at, :] = nn(x[at, :], wqkv[:, width : 2 * width]).astype(bf16)
+        v[at, :] = (nn(x[at, :], wqkv[:, 2 * width :]) + bias[:, width:]).astype(bf16)
         return 0
 
     lax.fori_loop(0, share, project, 0, unroll=True)
@@ -627,8 +623,6 @@
 
         grad_low = (nt(g_low[...], wdown[at, :]) * slope[i].astype(f32)).astype(bf16)
         dl_ref[i, :, 2 * third :] = col_sum(grad_low.astype(f32))
-        acc[...] += nt(grad_low, wup[:, at])
-
         def keep_down(r, j, wire):
             sd[i % 2, r * tiles + j] = wire
 
@@ -637,6 +631,7 @@
 
         cut_up(tn(act[i], g_low[...]), keep_down)
         cut_up(nn(low_t[...], grad_low), keep_up)
+        acc[...] += nt(grad_low, wup[:, at])
         put_u(i).start()
         put_d(i).start()
         return 0
@@ -663,8 +658,8 @@
     cut_up(nn(o_t[...], g_low[...]), keep_out)
     put_o = pltpu.make_async_copy(sd.at[0], to_ref, stores.at[1])
     put_o.start()
-    dk[...] = jnp.zeros_like(dk)
-    dv[...] = jnp.zeros_like(dv)
+    dk[rows:, :] = jnp.zeros((seq_len - rows, width), bf16)
+    dv[rows:, :] = jnp.zeros((seq_len - rows, width), bf16)
 
     def backward(pair, _):
         cols = pl.ds(pl.multiple_of(pair * 128, 128), 128)

time: 206 us -> 205 us (level)
  no operation moved by 1% of the time
where the time goes in v6:
time: 205 us; the launch traced here: 204 us
  Pallas kernels  204 us (100%)
    pallas_call x1, Pallas kernels, scatter_grads(): pl.pallas_call(functools.partial(scatter_kernel, nz), out_shape=[jax.Shap...  73.8 us
    pallas_call x1, Pallas kernels, gather_weights(): pl.pallas_call(functools.partial(gather_kernel, nz), out_shape=[jax.Shape...  70.9 us
    pallas_call x1, Pallas kernels, layer(): pl.pallas_call(layer_kernel, in_specs=[anywhere, anywhere, smem, vm, vm]...  51.8 us
    pallas_call x1, Pallas kernels, update(): pl.pallas_call(update_kernel, grid=(count // part,), in_specs=[pl.BlockSp...  6.99 us

profile of v6, /device:TPU:16, one launch (start us, length us, event | category | flops | bytes accessed | tf_op | source)
XLA Modules:
  0.0 204.4 jit_solution(16676057036464064713)
XLA Ops:
  0.6 70.9 %gather_weights.1 = (bf16[768,2304]{1,0:T(8,128)(2,1)}, bf16[768,768]{1,0:T(8,128)(2,1)}, bf16[768,3072]{1,0:T(8,128)(2,1)}, bf16[3072,768]{1,0:T(8,128)(2,1)}, f32[4,1,1152]{2,1,0:T(1,128)}) custom-call(s32[192]{0:T(256)} %order_ref.5, s32[1,192]{1,0:T(1,128)} %bitcast.20, f32[24,96,96]{2,1,0:T(8,128)} %bitcast.12, f32[1,1152]{1,0:T(1,128)} %lv_ref.1), custom_call_target="tpu_custom_call" | custom-call | tf_op jit(solution)/shard_map/gather_weights/pallas_call | solution.py:405
  71.5 51.8 %layer.1 = (bf16[512,768]{1,0:T(8,128)(2,1)}, bf16[4,8,3,2,72,128]{5,4,3,2,1,0:T(8,128)(2,1)}, bf16[64,72,128]{2,1,0:T(8,128)(2,1)}, bf16[4,64,72,128]{3,2,1,0:T...) custom-call(bf16[2048,768]{1,0:T(8,128)(2,1)} %tokens_ref.1, ...), custom_call_target="tpu_custom_call" | custom-call | tf_op jit(solution)/shard_map/layer/pallas_call | solution.py:743
  123.4 73.8 %scatter_grads.1 = (f32[24,72,128]{2,1,0:T(8,128)}, bf16[512,768]{1,0:T(8,128)(2,1)}, f32[4,1,1152]{2,1,0:T(1,128)}, f32[6,768]{1,0:T(8,128)}) custom-call(s32[192]{0:T(256)} %order_ref.5, bf16[4,48,72,128]{3,2,1,0:T(8,128)(2,1)} %bitcast.14, bf16[4,16,72,128]{3,2,1,0:T(8,128)(2,1)} %bitcast.19, bf16[4,64,72,128]{3,2,1,0:T(8,128)(2,1)} %get-tuple-element.54.tu_ref, ...), custom_call_target="tpu_custom_call" | custom-call | tf_op jit(solution)/shard_map/scatter_grads/pallas_call | solution.py:1064
  197.2 7.0 %update.1 = (f32[512,768]{1,0:T(8,128)}, f32[24,96,96]{2,1,0:T(8,128)}, f32[24,96,96]{2,1,0:T(8,128)}, f32[24,96,96]{2,1,0:T(8,128)}, f32[24,96,96]{2,1,0:T(8,12...) custom-call(s32[192]{0:T(256)} %order_ref.5, ...), custom_call_target="tpu_custom_call" | custom-call | tf_op jit(solution)/shard_map/update/pallas_call | solution.py:1167
